TPU v7x, 32 devices: a whole 2x2x4 slice. The times are simulated.
32 devices in a mesh: dp: 2 (over x), expert: 16 (over z, y, core).
Axes of the slice: x: 2, y: 2, z: 4, core: 2. Of those that a mesh axis runs over, the one named last changes fastest.
Arguments:
- tokens: bfloat16 [1024, 3584], P(('dp', 'expert')), may hold values from -6 to 6
- expert_ids: int32 [1024, 8], P(('dp', 'expert')), may hold values from 0 to 15, all different within a row; in each aligned block of 32 rows (0 to 31, 32 to 63, ...) at most 24 rows name the same one
- route_weights: float32 [1024, 8], P(('dp', 'expert')), may hold values from 0.1 to 1
- out_grad: bfloat16 [1024, 3584], P(('dp', 'expert')), may hold values from -6 to 6
- gate_weight: bfloat16 [16, 3584, 1024], P('expert', 'dp'), may hold values from -0.09375 to 0.09375
- up_weight: bfloat16 [16, 3584, 1024], P('expert', 'dp'), may hold values from -0.09375 to 0.09375
- down_weight: bfloat16 [16, 1024, 3584], P('expert', None, 'dp'), may hold values from -0.1875 to 0.1875
Outputs:
- mixed: bfloat16 [1024, 3584], P(('dp', 'expert'))
- tokens_grad: bfloat16 [1024, 3584], P(('dp', 'expert'))
- route_grad: float32 [1024, 8], P(('dp', 'expert'))
- gate_grad: bfloat16 [16, 3584, 1024], P('expert', 'dp')
- up_grad: bfloat16 [16, 3584, 1024], P('expert', 'dp')
- down_grad: bfloat16 [16, 1024, 3584], P('expert', None, 'dp')
Inputs may be any that keep to these rules, and one draw needn't show every extreme that they name: `expert_ids`: each row names 8 different experts; in each aligned block of 32 rows (the rows of one device) no expert is named by more than 24 rows, a bound that some block reaches.
All inputs are finite; a program needn't handle non-finite values.
Results may differ from a plain program's by a relative error of at most 0.0065.
Values may be sent and summed in bfloat16 or wider, within the bound.
No kernel may reach another device: no remote copies, remote signals or barrier semaphores. Data moves between devices by JAX's collectives and lax.ppermute only.
A program may use at most 192 MiB of HBM per device.

v0:
```python
import jax
import jax.numpy as jnp
from jax import lax
from jax.experimental import pallas as pl
from jax.experimental.pallas import tpu as pltpu
from jax.sharding import PartitionSpec as P

BF = jnp.bfloat16
F32 = jnp.float32


def silu_parts(pre_act):
    sigmoid_val = jax.nn.sigmoid(pre_act)
    return (pre_act * sigmoid_val, sigmoid_val * (1.0 + pre_act * (1.0 - sigmoid_val)))


def dot_nn(first, second):
    return lax.dot_general(first, second, (((1,), (0,)), ((), ())), preferred_element_type=F32)


def dot_nt(first, second):
    return lax.dot_general(first, second, (((1,), (1,)), ((), ())), preferred_element_type=F32)


def dot_tn(first, second):
    return lax.dot_general(first, second, (((0,), (0,)), ((), ())), preferred_element_type=F32)


def shift_dp(value, step):
    groups = lax.axis_size("dp")
    return lax.ppermute(value, "dp", [(i, (i + step) % groups) for i in range(groups)])


def choose(parts, index):
    picked = parts[0]
    for number in range(1, len(parts)):
        picked = jnp.where(index == number, parts[number], picked)
    return picked


def swap_groups(parts):
    groups = len(parts)
    mine = lax.axis_index("dp")
    by_step = [choose(parts, mine)]
    for step in range(1, groups):
        by_step.append(shift_dp(choose(parts, (mine + step) % groups), step))
    return [choose(by_step, (mine - group) % groups) for group in range(groups)]


def exchange(sent):
    return [shift_dp(sent, step) for step in range(1, lax.axis_size("dp"))]


def add_all(total, arrived):
    for value in arrived:
        total = total + value.astype(F32)
    return total


class Order:
    def __init__(self):
        self.last = []

    def enter(self, *values):
        flat, tree = jax.tree.flatten(values)
        tied = lax.optimization_barrier(tuple(flat) + tuple(self.last))[: len(flat)]
        return jax.tree.unflatten(tree, tied)

    def leave(self, *values):
        self.last = list(values)


def factors(experts):
    core = 2 if experts % 2 == 0 else 1
    rest = experts // core
    inner = 1
    while rest % (inner * 2) == 0 and (inner * 2) ** 2 <= rest:
        inner = inner * 2
    return (rest // inner, inner, core)


def shift_expert(value, level, step):
    dims = factors(lax.axis_size("expert"))
    stride = 1
    for dim in dims[level + 1 :]:
        stride = stride * dim
    size = dims[level]
    pairs = []
    for source in range(lax.axis_size("expert")):
        place = source // stride % size
        pairs.append((source, source + ((place + step) % size - place) * stride))
    return lax.ppermute(value, "expert", pairs)


def level_size(level):
    return factors(lax.axis_size("expert"))[level]


def gather_start(piece, level):
    return [piece] + [shift_expert(piece, level, step) for step in range(1, level_size(level))]


def three_pieces(value):
    high = lax.reduce_precision(value, 8, 7)
    rest = value - high
    mid = lax.reduce_precision(rest, 8, 7)
    return [high.astype(BF), mid.astype(BF), (rest - mid).astype(BF)]


def stacked_rows(values):
    return jnp.concatenate(values, axis=0) if len(values) > 1 else values[0]


def project_body(number_parts, part, *refs):
    mask_ref, order_ref, base_ref = refs[:3]
    part_refs = refs[3 : 3 + number_parts]
    gate_ref, up_ref, down_ref = refs[3 + number_parts : 6 + number_parts]
    x_ref, grad_ref, term_ref, weight_ref, pick_ref, own_ref, sent_ref = refs[6 + number_parts :]

    @pl.when(pl.program_id(0) == 0)
    def _():
        slots = x_ref.shape[0]
        arrived = stacked_rows([ref[...] for ref in part_refs])
        count = arrived.shape[0]
        mask = mask_ref[...]
        weight = dot_nt(mask, arrived[:, 2 * part :])
        live = weight > 0.0
        place = dot_nn(jnp.where(live, 1.0, 0.0).astype(BF), order_ref[...])
        slot = jnp.where(live, place - 1.0 + base_ref[...], -1.0)[:1]
        index = lax.broadcasted_iota(jnp.int32, (slots, count), 0).astype(F32)
        pick = jnp.where(index == slot, 1.0, 0.0).astype(BF)
        pick_ref[...] = pick
        x_ref[...] = dot_nn(pick, arrived[:, :part]).astype(BF)
        grad = dot_nn(pick, arrived[:, part : 2 * part])
        grad_ref[...] = grad.astype(BF)
        chosen = dot_nn(pick, arrived[:, 2 * part :]) * mask[:1].astype(F32)
        weight_rows = jnp.sum(chosen, axis=1, keepdims=True)
        weight_ref[...] = jnp.broadcast_to(weight_rows, weight_ref.shape)
        term_ref[...] = (weight_rows * grad).astype(BF)

    x_rows = x_ref[...]
    values = (
        dot_nn(x_rows, gate_ref[...]),
        dot_nn(x_rows, up_ref[...]),
        dot_nt(term_ref[...], down_ref[...]),
    )
    for number, value in enumerate(values):
        own_ref[number] = value
        sent_ref[number] = value.astype(BF)


def project(parts, mask, order, base, slots, gate_w, up_w, down_w):
    part, hidden = gate_w.shape
    tile = min(256, hidden)
    count = sum(value.shape[0] for value in parts)
    whole = lambda shape: pl.BlockSpec(shape, lambda j: (0,) * len(shape))
    columns = lambda rows: pl.BlockSpec((rows, tile), lambda j: (0, j))
    stacked = pl.BlockSpec((3, slots, tile), lambda j: (0, 0, j))
    row_out = jax.ShapeDtypeStruct((slots, part), BF)
    return pl.pallas_call(
        lambda *refs: project_body(len(parts), part, *refs),
        grid=(hidden // tile,),
        in_specs=[whole(mask.shape), whole(order.shape), whole(base.shape)]
        + [whole(value.shape) for value in parts]
        + [columns(part), columns(part), pl.BlockSpec((tile, part), lambda j: (j, 0))],
        out_specs=[whole((slots, part))] * 3
        + [whole((slots, 128)), whole((slots, count)), stacked, stacked],
        out_shape=[row_out] * 3
        + [
            jax.ShapeDtypeStruct((slots, 128), F32),
            jax.ShapeDtypeStruct((slots, count), BF),
            jax.ShapeDtypeStruct((3, slots, hidden), F32),
            jax.ShapeDtypeStruct((3, slots, hidden), BF),
        ],
        compiler_params=pltpu.CompilerParams(vmem_limit_bytes=56 * 2**20),
        name="project",
    )(mask, order, base, *parts, gate_w, up_w, down_w)


def merge(values, pieces):
    total = add_all(values[0].astype(F32), values[1:])
    rows = total.shape[0] // pieces
    parts = [total[number * rows : (number + 1) * rows] for number in range(pieces)]
    return parts[:1] + [part.astype(BF) for part in parts[1:]]


def merge_between(values, pieces):
    rows, wide = values[0].shape
    rows = rows // pieces
    kinds = [F32] + [BF] * (pieces - 1)

    def body(*refs):
        for number in range(pieces):
            here = slice(number * rows, (number + 1) * rows)
            total = add_all(refs[0][here].astype(F32), [ref[here] for ref in refs[1 : len(values)]])
            refs[len(values) + number][...] = total.astype(kinds[number])

    return pl.pallas_call(
        body,
        out_shape=[jax.ShapeDtypeStruct((rows, wide), kind) for kind in kinds],
        compiler_params=pltpu.CompilerParams(vmem_limit_bytes=56 * 2**20),
        name="merge",
    )(*values)


def finish_body(number_sent, number_parts, *refs):
    own_ref = refs[0]
    sent_refs = refs[1 : 1 + number_sent]
    grad_ref, weight_ref, pick_ref, route_ref, gate_ref, up_ref, down_ref = refs[
        1 + number_sent : 8 + number_sent
    ]
    hidden_ref, gate_term_ref, up_term_ref = refs[8 + number_sent : 11 + number_sent]
    back_refs = refs[11 + number_sent : 11 + number_sent + number_parts]
    out_acc, in_acc = refs[11 + number_sent + number_parts :]
    step = pl.program_id(0)
    gate_pre, up_pre, hidden_grad = (
        add_all(own_ref[number], [ref[number] for ref in sent_refs]) for number in range(3)
    )
    act_val, act_slope = silu_parts(gate_pre)
    hidden = (act_val * up_pre).astype(BF)
    gate_term = (hidden_grad * up_pre * act_slope).astype(BF)
    up_term = (hidden_grad * act_val).astype(BF)
    hidden_ref[...] = hidden
    gate_term_ref[...] = gate_term
    up_term_ref[...] = up_term
    out_part = dot_nn(hidden, down_ref[...])
    in_part = dot_nt(gate_term, gate_ref[...]) + dot_nt(up_term, up_ref[...])

    @pl.when(step == 0)
    def _():
        out_acc[...] = out_part
        in_acc[...] = in_part

    @pl.when(step > 0)
    def _():
        out_acc[...] += out_part
        in_acc[...] += in_part

    @pl.when(step == pl.num_programs(0) - 1)
    def _():
        part = out_acc.shape[1]
        extra = route_ref.shape[1]
        expert_out = out_acc[...].astype(BF).astype(F32)
        rest = jnp.sum(grad_ref[...].astype(F32) * expert_out, axis=1, keepdims=True)
        route = jnp.zeros((rest.shape[0], extra), F32)
        for number in range(3):
            piece = rest.astype(BF).astype(F32)
            route = route + piece * route_ref[number : number + 1]
            rest = rest - piece
        pick = pick_ref[...]
        weighted = (weight_ref[:, :1] * expert_out).astype(BF)
        backs = (
            dot_tn(pick, weighted).astype(BF),
            dot_tn(pick, route.astype(BF)).astype(BF),
            dot_tn(pick, in_acc[...].astype(BF)).astype(BF),
        )
        rows = back_refs[0].shape[0]
        for number, ref in enumerate(back_refs):
            here = slice(number * rows, (number + 1) * rows)
            ref[:, :part] = backs[0][here]
            ref[:, part : part + extra] = backs[1][here]
            ref[:, part + extra :] = backs[2][here]


def finish(own, sent, grad, weight, pick, route, gate_w, up_w, down_w, number_parts):
    part, hidden = gate_w.shape
    tile = min(256, hidden)
    slots, count = pick.shape
    rows = count // number_parts
    wide = 2 * part + route.shape[1]
    whole = lambda shape: pl.BlockSpec(shape, lambda j: (0,) * len(shape))
    columns = lambda size: pl.BlockSpec((size, tile), lambda j: (0, j))
    stacked = pl.BlockSpec((3, slots, tile), lambda j: (0, 0, j))
    return pl.pallas_call(
        lambda *refs: finish_body(len(sent), number_parts, *refs),
        grid=(hidden // tile,),
        in_specs=[stacked] * (1 + len(sent))
        + [whole(value.shape) for value in (grad, weight, pick, route)]
        + [columns(part), columns(part), pl.BlockSpec((tile, part), lambda j: (j, 0))],
        out_specs=[columns(slots)] * 3 + [whole((rows, wide))] * number_parts,
        out_shape=[jax.ShapeDtypeStruct((slots, hidden), BF)] * 3
        + [jax.ShapeDtypeStruct((rows, wide), BF)] * number_parts,
        scratch_shapes=[pltpu.VMEM((slots, part), F32), pltpu.VMEM((slots, part), F32)],
        compiler_params=pltpu.CompilerParams(vmem_limit_bytes=56 * 2**20),
        name="finish",
    )(own, *sent, grad, weight, pick, route, gate_w, up_w, down_w)


def finish_and_project(left, parts, mask, order, base, slots, gate_w, up_w, down_w, number_parts):
    own, sent, grad, weight, pick, route = left
    part, hidden = gate_w.shape
    tile = min(256, hidden)
    count = sum(value.shape[0] for value in parts)
    rows = pick.shape[1] // number_parts
    wide = 2 * part + route.shape[1]
    whole = lambda shape: pl.BlockSpec(shape, lambda j: (0,) * len(shape))
    columns = lambda size: pl.BlockSpec((size, tile), lambda j: (0, j))
    stacked = pl.BlockSpec((3, slots, tile), lambda j: (0, 0, j))
    first = 3 + len(parts)
    second = first + 5 + len(sent)
    weights = second + 3

    def body(*refs):
        outs = refs[weights : weights + 7]
        ends = refs[weights + 7 :]
        finish_body(len(sent), number_parts, *refs[first:weights], *ends)
        project_body(len(parts), part, *refs[:first], *refs[second:weights], *outs)

    results = pl.pallas_call(
        body,
        grid=(hidden // tile,),
        in_specs=[whole(value.shape) for value in (mask, order, base, *parts)]
        + [stacked] * (1 + len(sent))
        + [whole(value.shape) for value in (grad, weight, pick, route)]
        + [columns(part), columns(part), pl.BlockSpec((tile, part), lambda j: (j, 0))],
        out_specs=[whole((slots, part))] * 3
        + [whole((slots, 128)), whole((slots, count)), stacked, stacked]
        + [columns(slots)] * 3
        + [whole((rows, wide))] * number_parts,
        out_shape=[jax.ShapeDtypeStruct((slots, part), BF)] * 3
        + [
            jax.ShapeDtypeStruct((slots, 128), F32),
            jax.ShapeDtypeStruct((slots, count), BF),
            jax.ShapeDtypeStruct((3, slots, hidden), F32),
            jax.ShapeDtypeStruct((3, slots, hidden), BF),
        ]
        + [jax.ShapeDtypeStruct((slots, hidden), BF)] * 3
        + [jax.ShapeDtypeStruct((rows, wide), BF)] * number_parts,
        scratch_shapes=[pltpu.VMEM((slots, part), F32), pltpu.VMEM((slots, part), F32)],
        compiler_params=pltpu.CompilerParams(vmem_limit_bytes=56 * 2**20),
        name="step",
    )(mask, order, base, *parts, own, *sent, grad, weight, pick, route, gate_w, up_w, down_w)
    return results[:7], results[7:]


def per_device(tokens, expert_ids, route_weights, out_grad, gate_weight, up_weight, down_weight):
    experts = lax.axis_size("expert")
    groups = lax.axis_size("dp")
    my_expert = lax.axis_index("expert")
    outer, inner, core = factors(experts)
    rows, width = tokens.shape
    hidden_width = gate_weight.shape[2]
    choices = expert_ids.shape[1]
    part = width // groups
    most = min(rows, 3 * rows * choices // (2 * experts))
    extra = -(-3 * experts // 128) * 128
    gate_w, up_w, down_w = gate_weight[0], up_weight[0], down_weight[0]

    chosen = expert_ids[:, :, None] == jnp.arange(experts, dtype=jnp.int32)[None, None, :]
    weight_table = jnp.sum(jnp.where(chosen, route_weights[:, :, None], 0.0), axis=1)
    weight_cols = jnp.concatenate(
        three_pieces(weight_table) + [jnp.zeros((rows, extra - 3 * experts), BF)], axis=1
    )
    payload = jnp.concatenate(
        swap_groups(
            [
                jnp.concatenate(
                    [
                        tokens[:, g * part : (g + 1) * part],
                        out_grad[:, g * part : (g + 1) * part],
                        weight_cols,
                    ],
                    axis=1,
                )
                for g in range(groups)
            ]
        ),
        axis=0,
    )

    column = jnp.arange(extra, dtype=jnp.int32)[None, :]
    mask = jnp.broadcast_to(
        (column % experts == my_expert) & (column < 3 * experts), (8, extra)
    ).astype(BF)
    route_cols = (
        column == jnp.arange(8, dtype=jnp.int32)[:, None] * experts + my_expert
    ) & (jnp.arange(8)[:, None] < 3)
    route_cols = route_cols.astype(F32)
    last = outer - 1
    count = inner * core * groups * rows
    slots = inner * core * groups * most
    token = jnp.arange(count, dtype=jnp.int32)
    block = token // rows
    before = (block[:, None] == block[None, :]) & (token[:, None] <= token[None, :])
    tables = (mask, before.astype(BF), jnp.broadcast_to((block * most).astype(F32)[None], (8, count)))
    order = Order()
    pieces, along, around, picked, sums, ends = {0: payload}, {}, {}, {}, {}, {}
    moving, finals, held = {}, {}, {}

    def start_outer(number):
        if number < outer:
            (tied,) = order.enter(payload)
            pieces[number] = shift_expert(tied, 0, number)

    def start_inner(number):
        (mine,) = order.enter(pieces[number])
        along[number] = gather_start(mine, 1)
        around[number] = [] if number else [gather_start(mine, 2)]

    def start_back(number):
        mine, others = held[number]
        (others,) = order.enter(others)
        moving[number] = (
            mine,
            [shift_expert(other, 1, -step) for step, other in enumerate(others, 1)],
        )

    def start_core(number):
        (mine,) = order.enter(along[number])
        order.leave(*mine)
        around[number] = around[number] + [
            gather_start(value, 2) for value in (mine if number else mine[1:])
        ]

    def ready_parts(across):
        return [piece[index] for index in range(core) for piece in across]

    def partial_sums(number):
        across, tied = order.enter(around[number], pieces.get(2) if number == 1 else None)
        if number == 1 and outer > 2:
            pieces[2] = tied
            if outer > 3:
                late, _ = lax.optimization_barrier((payload, tied))
                pieces[3] = shift_expert(late, 0, 3)
        projected(
            number, project(ready_parts(across), *tables, slots, gate_w, up_w, down_w)
        )
        order.leave(picked[number][6])

    def projected(number, results):
        picked[number] = results
        own, sent = results[5:]
        sums[number] = (own, exchange(sent))

    def finished(number, results):
        ends[number] = results[:3]
        back = results[3:]
        moving[number] = (
            back[0],
            [shift_expert(back[step], 2, -step) for step in range(1, core)],
        )

    def finish_chunk(number, later=None):
        own, arrived, across = order.enter(*sums[number], around.get(later))
        x_rows, grad, term, weight, pick = picked[number][:5]
        left = (own, arrived, grad, weight, pick, route_cols)
        if later is None:
            results = finish(*left, gate_w, up_w, down_w, core)
            order.leave(*results[3:])
            finished(number, results)
        else:
            made, results = finish_and_project(
                left, ready_parts(across), *tables, slots, gate_w, up_w, down_w, core
            )
            order.leave(made[6], *results[3:])
            projected(later, made)
            finished(number, results)

    def next_inner(number):
        mine, arrived = order.enter(*moving[number])
        mine, *others = (merge_between if 0 < number < last else merge)([mine] + arrived, inner)
        order.leave(mine, *others)
        held[number] = (mine, others)
        if number or not last:
            start_back(number)

    def next_outer(number):
        mine, arrived = order.enter(*moving[number])
        (total,) = merge([mine] + arrived, 1)
        if number:
            total = total.astype(BF)
        order.leave(total)
        finals[number] = shift_expert(total, 0, -number) if number else total

    pieces[0], tables = order.enter(payload, tables)
    payload = pieces[0]
    start_inner(0)
    start_outer(1)
    along[0], pieces = order.enter(along[0], pieces)
    order.leave(*along[0])
    start_core(0)
    if last:
        start_inner(1)
    start_outer(2)
    partial_sums(0)
    if last:
        start_core(1)
        partial_sums(1)
    if last > 1:
        start_inner(2)
        if last > 2:
            start_inner(3)
        start_core(2)
    for number in range(last + 1):
        later = number + 2
        if later <= last:
            finish_chunk(number, later)
            if later < last:
                if later > 2:
                    start_inner(later + 1)
                start_core(later + 1)
                start_outer(later + 2)
        else:
            finish_chunk(number)
        if 0 < number < last:
            next_inner(number)
    for number in range(1, last):
        next_outer(number)
    next_inner(last)

    def rows_of(table, index):
        return [table[number][index] for number in range(last + 1)]

    def joined(values):
        return jnp.concatenate(values, axis=0)

    hidden_all, out_all = order.enter(rows_of(ends, 0), rows_of(picked, 2))
    down_grad = dot_tn(joined(hidden_all), joined(out_all)).astype(BF)[None]
    order.leave(down_grad)
    next_outer(last)
    if last:
        next_inner(0)
        start_back(0)
    x_all, gate_all, up_all = order.enter(
        rows_of(picked, 0), rows_of(ends, 1), rows_of(ends, 2)
    )
    x_all = joined(x_all)
    gate_grad = dot_tn(x_all, joined(gate_all)).astype(BF)[None]
    up_grad = dot_tn(x_all, joined(up_all)).astype(BF)[None]
    order.leave(gate_grad, up_grad)
    if last:
        next_outer(0)
    (arrived,) = order.enter(list(finals.values()))
    final = add_all(arrived[0].astype(F32), arrived[1:]).astype(BF)
    parts = swap_groups([final[g * rows : (g + 1) * rows] for g in range(groups)])
    mixed = jnp.concatenate([value[:, :part] for value in parts], axis=1)
    tokens_grad = jnp.concatenate([value[:, part + extra :] for value in parts], axis=1)
    route_table = jnp.zeros((), F32)
    for value in parts:
        for number in range(3):
            start = part + number * experts
            route_table = route_table + value[:, start : start + experts].astype(F32)
    route_grad = jnp.sum(jnp.where(chosen, route_table[:, None, :], 0.0), axis=2)
    return (mixed, tokens_grad, route_grad, gate_grad, up_grad, down_grad)


def solution(mesh):
    return jax.shard_map(
        per_device,
        mesh=mesh,
        in_specs=(
            P(("dp", "expert"), None),
            P(("dp", "expert"), None),
            P(("dp", "expert"), None),
            P(("dp", "expert"), None),
            P("expert", "dp", None),
            P("expert", "dp", None),
            P("expert", None, "dp"),
        ),
        out_specs=(
            P(("dp", "expert"), None),
            P(("dp", "expert"), None),
            P(("dp", "expert"), None),
            P("expert", "dp", None),
            P("expert", "dp", None),
            P("expert", None, "dp"),
        ),
        check_vma=False,
    )
```

profile of v0, /device:TPU:0, one launch (start us, length us, event | category | flops | bytes accessed | tf_op | source)
XLA Modules:
  0.0 215.7 jit_solution(17264842326179783934)
XLA Ops:
  0.6 0.7 select_reduce_fusion.1
  1.5 1.1 fusion.41
  2.9 3.0 %collective-permute-start = (bf16[32,3712]{1,0:T(8,128)(2,1)S(1)}, bf16[32,3712]{1,0:T(8,128)(2,1)S(1)}, u32[]{:S(2)}, u32[]{:S(2)}) collective-permute-start(bf16[32,3712]{1,0:T(8,128)(2,1)S(1)} %broadcast_select_fusion.5), channel_id=1, source_target_pairs={{0,16},{16,0},{1,17},{17,1},{2,18},{18,2},{3,19},{19,3},{4,20},{20... | collective-permute-start | bytes 712712 | tf_op jit(solution)/shard_map/ppermute | solution.py:31
  5.9 0.8 fusion.32.refs_1_
  6.7 5.0 %collective-permute-done = bf16[32,3712]{1,0:T(8,128)(2,1)S(1)} collective-permute-done((bf16[32,3712]{1,0:T(8,128)(2,1)S(1)}, bf16[32,3712]{1,0:T(8,128)(2,1)S(1)}, u32[]{:S(2)}, u32[]{:S(2)}) %collective-permute-start) | collective-permute-done | bytes 237600 | tf_op jit(solution)/shard_map/ppermute | solution.py:31
  11.7 0.8 pad_maximum_fusion.refs_3_
  13.7 1.8 collective-permute-start.2
  15.6 1.5 collective-permute-start.1
  17.1 10.7 %collective-permute-done.2.refs_3_ = bf16[64,3712]{1,0:T(8,128)(2,1)S(1)} collective-permute-done((bf16[64,3712]{1,0:T(8,128)(2,1)}, bf16[64,3712]{1,0:T(8,128)(2,1)S(1)}, u32[]{:S(2)}, u32[]{:S(2)}) %collective-permute-start.2) | collective-permute-done | bytes 475168 | tf_op jit(solution)/shard_map/ppermute | solution.py:92
  27.9 1.6 collective-permute-start.3
  29.5 1.9 collective-permute-start.8
  31.4 0.8 copy-done.26
  32.3 9.6 %project.2 = (bf16[192,1792]{1,0:T(8,128)(2,1)}, bf16[192,1792]{1,0:T(8,128)(2,1)}, bf16[192,1792]{1,0:T(8,128)(2,1)}, f32[192,128]{1,0:T(8,128)}, bf16[192,256]...) custom-call(bf16[8,128]{1,0:T(8,128)(2,1)} %broadcast_in_dim.33.refs_0_, ...), custom_call_target="tpu_custom_call" | custom-call | tf_op jit(solution)/shard_map/project/pallas_call | solution.py:160
  42.5 1.5 collective-permute-start.12
  44.0 9.7 %collective-permute-done.8.refs_3_ = bf16[64,3712]{1,0:T(8,128)(2,1)S(1)} collective-permute-done((bf16[64,3712]{1,0:T(8,128)(2,1)}, bf16[64,3712]{1,0:T(8,128)(2,1)S(1)}, u32[]{:S(2)}, u32[]{:S(2)}) %collective-permute-start.8) | collective-permute-done | bytes 475168 | tf_op jit(solution)/shard_map/ppermute | solution.py:92
  53.7 0.8 copy-done.27
  54.5 0.8 copy-done.29
  55.3 9.7 %project.3 = (bf16[192,1792]{1,0:T(8,128)(2,1)}, bf16[192,1792]{1,0:T(8,128)(2,1)}, bf16[192,1792]{1,0:T(8,128)(2,1)}, f32[192,128]{1,0:T(8,128)}, bf16[192,256]...) custom-call(bf16[8,128]{1,0:T(8,128)(2,1)} %broadcast_in_dim.33.refs_0_, ...), custom_call_target="tpu_custom_call" | custom-call | tf_op jit(solution)/shard_map/project/pallas_call | solution.py:160
  65.5 1.7 collective-permute-start.10
  67.2 1.5 collective-permute-start.9
  68.7 8.7 %collective-permute-done.13.refs_4_ = bf16[64,3712]{1,0:T(8,128)(2,1)S(1)} collective-permute-done((bf16[64,3712]{1,0:T(8,128)(2,1)S(1)}, bf16[64,3712]{1,0:T(8,128)(2,1)S(1)}, u32[]{:S(2)}, u32[]{:S(2)}) %collective-permute-start.13) | collective-permute-done | bytes 475168 | tf_op jit(solution)/shard_map/ppermute | solution.py:92
  77.9 1.4 collective-permute-start.11
  80.1 1.0 copy-done.2
  81.4 15.2 %step.2 = (bf16[192,1792]{1,0:T(8,128)(2,1)}, bf16[192,1792]{1,0:T(8,128)(2,1)}, bf16[192,1792]{1,0:T(8,128)(2,1)}, f32[192,128]{1,0:T(8,128)}, bf16[192,256]{1,...) custom-call(bf16[8,128]{1,0:T(8,128)(2,1)} %broadcast_in_dim.33.refs, ...), custom_call_target="tpu_custom_call" | custom-call | tf_op jit(solution)/shard_map/step/pallas_call | solution.py:309
  97.3 1.5 collective-permute-start.21
  100.1 15.0 %step.3 = (bf16[192,1792]{1,0:T(8,128)(2,1)}, bf16[192,1792]{1,0:T(8,128)(2,1)}, bf16[192,1792]{1,0:T(8,128)(2,1)}, f32[192,128]{1,0:T(8,128)}, bf16[192,256]{1,...) custom-call(bf16[8,128]{1,0:T(8,128)(2,1)} %broadcast_in_dim.33.refs, ...), custom_call_target="tpu_custom_call" | custom-call | tf_op jit(solution)/shard_map/step/pallas_call | solution.py:309
  115.3 1.5 collective-permute-start.20
  116.8 1.1 collective-permute-done.18.refs_1_
  117.9 0.9 copy-done.8
  118.8 2.7 %merge.2 = (f32[64,3712]{1,0:T(8,128)}, bf16[64,3712]{1,0:T(8,128)(2,1)}) custom-call(bf16[128,3712]{1,0:T(8,128)(2,1)} %get-tuple-element.204.refs_0_, bf16[128,3712]{1,0:T(8,128)(2,1)} %copy-done.8), custom_call_target="tpu_custom_call" | custom-call | tf_op jit(solution)/shard_map/merge/pallas_call | solution.py:198
  121.5 4.8 %collective-permute-done.21.refs_1_ = bf16[3,192,1024]{2,1,0:T(8,128)(2,1)S(1)} collective-permute-done((bf16[3,192,1024]{2,1,0:T(8,128)(2,1)}, bf16[3,192,1024]{2,1,0:T(8,128)(2,1)S(1)}, u32[]{:S(2)}, u32[]{:S(2)}) %collective-permute-start.21) | collective-permute-done | bytes 1179680 | tf_op jit(solution)/shard_map/ppermute | solution.py:31
  126.3 1.0 copy-done.3
  127.3 10.8 %finish.2 = (bf16[192,1024]{1,0:T(8,128)(2,1)}, bf16[192,1024]{1,0:T(8,128)(2,1)}, bf16[192,1024]{1,0:T(8,128)(2,1)}, bf16[128,3712]{1,0:T(8,128)(2,1)}, bf16[128,3712]{1,0:T(8,128)(2,1)}) custom-call(f32[3,192,1024]{2,1,0:T(8,128)} %get-tuple-element.211.refs_0_, bf16[3,192,1024]{2,1,0:T(8,128)(2,1)} %copy-done.3, ...), custom_call_target="tpu_custom_call" | custom-call | tf_op jit(solution)/shard_map/finish/pallas_call | solution.py:274
  139.0 1.9 collective-permute-done.22.refs_1_
  140.9 0.9 copy-done.7
  141.8 2.7 %merge.3 = (f32[64,3712]{1,0:T(8,128)}, bf16[64,3712]{1,0:T(8,128)(2,1)}) custom-call(bf16[128,3712]{1,0:T(8,128)(2,1)} %get-tuple-element.218.refs_0_, bf16[128,3712]{1,0:T(8,128)(2,1)} %copy-done.7), custom_call_target="tpu_custom_call" | custom-call | tf_op jit(solution)/shard_map/merge/pallas_call | solution.py:198
  145.1 5.6 %collective-permute-done.20.refs_1_ = bf16[3,192,1024]{2,1,0:T(8,128)(2,1)S(1)} collective-permute-done((bf16[3,192,1024]{2,1,0:T(8,128)(2,1)}, bf16[3,192,1024]{2,1,0:T(8,128)(2,1)S(1)}, u32[]{:S(2)}, u32[]{:S(2)}) %collective-permute-start.20) | collective-permute-done | bytes 1179680 | tf_op jit(solution)/shard_map/ppermute | solution.py:31
  150.7 1.0 copy-done.4
  151.7 10.8 %finish.3 = (bf16[192,1024]{1,0:T(8,128)(2,1)}, bf16[192,1024]{1,0:T(8,128)(2,1)}, bf16[192,1024]{1,0:T(8,128)(2,1)}, bf16[128,3712]{1,0:T(8,128)(2,1)}, bf16[128,3712]{1,0:T(8,128)(2,1)}) custom-call(f32[3,192,1024]{2,1,0:T(8,128)} %get-tuple-element.222.refs_0_, bf16[3,192,1024]{2,1,0:T(8,128)(2,1)} %copy-done.4, ...), custom_call_target="tpu_custom_call" | custom-call | tf_op jit(solution)/shard_map/finish/pallas_call | solution.py:274
  162.7 3.3 %collective-permute-start.23 = (bf16[64,3712]{1,0:T(8,128)(2,1)S(1)}, bf16[64,3712]{1,0:T(8,128)(2,1)S(1)}, u32[]{:S(2)}, u32[]{:S(2)}) collective-permute-start(bf16[64,3712]{1,0:T(8,128)(2,1)S(1)} %add_convert_fusion.3), channel_id=1, source_target_pairs={{0,12},{1,13},{2,14},{3,15},{4,0},{5,1},{6,2},{7,3},{8,4},{9,5},{1... | collective-permute-start | bytes 1425416 | tf_op jit(solution)/shard_map/ppermute | solution.py:92
  168.2 4.9 %fusion = bf16[1,1024,1792]{2,1,0:T(8,128)(2,1)} fusion(bf16[192,1792]{1,0:T(8,128)(2,1)S(1)} %copy-done.35, bf16[192,1792]{1,0:T(8,128)(2,1)S(1)} %copy-done.34, bf16[192,1792]{1,0:T(8,128)(2,1)S(1)} %copy-done.33, bf16[192,1792]{1,0:T(8,128)(2,1)S(1)} %copy-done.32, bf16[192,1024]{1,0:T(8,128)(2,1)S(1)} %copy-done.48, ...), kind=kOutput, calls=%fused_computation.3 | convolution fusion | flops 2837708800 | bytes 7995392 | tf_op jit(solution)/shard_map/dot_general | solution.py:26
  173.2 6.4 %collective-permute-done.27 = bf16[64,3712]{1,0:T(8,128)(2,1)S(1)} collective-permute-done((bf16[64,3712]{1,0:T(8,128)(2,1)S(1)}, bf16[64,3712]{1,0:T(8,128)(2,1)S(1)}, u32[]{:S(2)}, u32[]{:S(2)}) %collective-permute-start.27) | collective-permute-done | bytes 475168 | tf_op jit(solution)/shard_map/ppermute | solution.py:92
  182.7 4.5 %fusion.2 = bf16[1,1792,1024]{2,1,0:T(8,128)(2,1)} fusion(bf16[768,1792]{1,0:T(8,128)(2,1)S(1)} %constant_dynamic-update-slice_fusion, bf16[192,1024]{1,0:T(8,128)(2,1)S(1)} %copy-done.46, bf16[192,1024]{1,0:T(8,128)(2,1)S(1)} %copy-done.43, bf16[192,1024]{1,0:T(8,128)(2,1)S(1)} %copy-done.41, bf16[192,1024]{1,0:T(8,128)(2,1)S(1)} %copy-done.38), kind=kOutput, calls=%fused_computation.5 | convolution fusion | flops 2826698752 | bytes 7995392 | tf_op jit(solution)/shard_map/dot_general | solution.py:26
  187.3 4.5 %fusion.1 = bf16[1,1792,1024]{2,1,0:T(8,128)(2,1)} fusion(bf16[768,1792]{1,0:T(8,128)(2,1)S(1)} %constant_dynamic-update-slice_fusion, bf16[192,1024]{1,0:T(8,128)(2,1)S(1)} %copy-done.45, bf16[192,1024]{1,0:T(8,128)(2,1)S(1)} %copy-done.42, bf16[192,1024]{1,0:T(8,128)(2,1)S(1)} %copy-done.39, bf16[192,1024]{1,0:T(8,128)(2,1)S(1)} %copy-done.37), kind=kOutput, calls=%fused_computation.4 | convolution fusion | flops 2826698752 | bytes 7995392 | tf_op jit(solution)/shard_map/dot_general | solution.py:26
  191.8 0.8 collective-permute-done.30
  192.8 12.9 %collective-permute-done.25 = bf16[64,3712]{1,0:T(8,128)(2,1)S(1)} collective-permute-done((bf16[64,3712]{1,0:T(8,128)(2,1)S(1)}, bf16[64,3712]{1,0:T(8,128)(2,1)S(1)}, u32[]{:S(2)}, u32[]{:S(2)}) %collective-permute-start.25) | collective-permute-done | bytes 475168 | tf_op jit(solution)/shard_map/ppermute | solution.py:92
  206.0 1.6 collective-permute-start.31
  207.5 5.9 %collective-permute-done.31 = bf16[32,3712]{1,0:T(8,128)(2,1)S(1)} collective-permute-done((bf16[32,3712]{1,0:T(8,128)(2,1)S(1)}, bf16[32,3712]{1,0:T(8,128)(2,1)S(1)}, u32[]{:S(2)}, u32[]{:S(2)}) %collective-permute-start.31) | collective-permute-done | bytes 237600 | tf_op jit(solution)/shard_map/ppermute | solution.py:31
  (171 shorter events, 16.1 us)
Async XLA Ops:
  2.9 8.8 %collective-permute-start = (bf16[32,3712]{1,0:T(8,128)(2,1)S(1)}, bf16[32,3712]{1,0:T(8,128)(2,1)S(1)}, u32[]{:S(2)}, u32[]{:S(2)}) collective-permute-start(bf16[32,3712]{1,0:T(8,128)(2,1)S(1)} %broadcast_select_fusion.5), channel_id=1, source_target_pairs={{0,16},{16,0},{1,17},{17,1},{2,18},{18,2},{3,19},{19,3},{4,20},{20... | collective-permute-start | bytes 712712 | tf_op jit(solution)/shard_map/ppermute | solution.py:31
  13.7 14.1 %collective-permute-start.2 = (bf16[64,3712]{1,0:T(8,128)(2,1)}, bf16[64,3712]{1,0:T(8,128)(2,1)S(1)}, u32[]{:S(2)}, u32[]{:S(2)}) collective-permute-start(bf16[64,3712]{1,0:T(8,128)(2,1)} %pad_maximum_fusion.refs_3_), channel_id=1, source_target_pairs={{0,4},{1,5},{2,6},{3,7},{4,8},{5,9},{6,10},{7,11},{8,12},{9,13},{1... | collective-permute-start | bytes 1425416 | tf_op jit(solution)/shard_map/ppermute | solution.py:92
  15.6 12.2 %collective-permute-start.1 = (bf16[64,3712]{1,0:T(8,128)(2,1)}, bf16[64,3712]{1,0:T(8,128)(2,1)S(1)}, u32[]{:S(2)}, u32[]{:S(2)}) collective-permute-start(bf16[64,3712]{1,0:T(8,128)(2,1)} %pad_maximum_fusion.refs_3_), channel_id=1, source_target_pairs={{0,2},{1,3},{2,0},{3,1},{4,6},{5,7},{6,4},{7,5},{8,10},{9,11},{10,... | collective-permute-start | bytes 1425416 | tf_op jit(solution)/shard_map/ppermute | solution.py:92
  17.1 14.3 %collective-permute-start.4 = (bf16[64,3712]{1,0:T(8,128)(2,1)}, bf16[64,3712]{1,0:T(8,128)(2,1)S(1)}, u32[]{:S(2)}, u32[]{:S(2)}) collective-permute-start(bf16[64,3712]{1,0:T(8,128)(2,1)} %pad_maximum_fusion.refs_3_), channel_id=1, source_target_pairs={{0,1},{1,0},{2,3},{3,2},{4,5},{5,4},{6,7},{7,6},{8,9},{9,8},{10,11... | collective-permute-start | bytes 1425416 | tf_op jit(solution)/shard_map/ppermute | solution.py:92
  27.8 14.2 %copy-start.23 = (bf16[64,3712]{1,0:T(8,128)(2,1)}, bf16[64,3712]{1,0:T(8,128)(2,1)S(1)}, u32[]{:S(2)}) copy-start(bf16[64,3712]{1,0:T(8,128)(2,1)S(1)} %collective-permute-done.2.refs_3_) | copy-start | bytes 1425412
  27.8 3.5 %collective-permute-start.5 = (bf16[64,3712]{1,0:T(8,128)(2,1)S(1)}, bf16[64,3712]{1,0:T(8,128)(2,1)S(1)}, u32[]{:S(2)}, u32[]{:S(2)}) collective-permute-start(bf16[64,3712]{1,0:T(8,128)(2,1)S(1)} %collective-permute-done.1.refs_4_), channel_id=1, source_target_pairs={{0,1},{1,0},{2,3},{3,2},{4,5},{5,4},{6,7},{7,6},{8,9},{9,8},{10,11... | collective-permute-start | bytes 1425416 | tf_op jit(solution)/shard_map/ppermute | solution.py:92
  27.9 14.1 %collective-permute-start.3 = (bf16[64,3712]{1,0:T(8,128)(2,1)S(1)}, bf16[64,3712]{1,0:T(8,128)(2,1)S(1)}, u32[]{:S(2)}, u32[]{:S(2)}) collective-permute-start(bf16[64,3712]{1,0:T(8,128)(2,1)S(1)} %collective-permute-done.2.refs_3_), channel_id=1, source_target_pairs={{0,2},{1,3},{2,0},{3,1},{4,6},{5,7},{6,4},{7,5},{8,10},{9,11},{10,... | collective-permute-start | bytes 1425416 | tf_op jit(solution)/shard_map/ppermute | solution.py:92
  29.5 24.2 %collective-permute-start.8 = (bf16[64,3712]{1,0:T(8,128)(2,1)}, bf16[64,3712]{1,0:T(8,128)(2,1)S(1)}, u32[]{:S(2)}, u32[]{:S(2)}) collective-permute-start(bf16[64,3712]{1,0:T(8,128)(2,1)} %pad_maximum_fusion.refs_3_), channel_id=1, source_target_pairs={{0,8},{1,9},{2,10},{3,11},{4,12},{5,13},{6,14},{7,15},{8,0},{9,1},... | collective-permute-start | bytes 1425416 | tf_op jit(solution)/shard_map/ppermute | solution.py:92
  41.9 11.8 %copy-start.24 = (bf16[64,3712]{1,0:T(8,128)(2,1)}, bf16[64,3712]{1,0:T(8,128)(2,1)S(1)}, u32[]{:S(2)}) copy-start(bf16[64,3712]{1,0:T(8,128)(2,1)S(1)} %collective-permute-done.3.refs_4_) | copy-start | bytes 1425412
  42.0 11.7 %collective-permute-start.6 = (bf16[64,3712]{1,0:T(8,128)(2,1)S(1)}, bf16[64,3712]{1,0:T(8,128)(2,1)S(1)}, u32[]{:S(2)}, u32[]{:S(2)}) collective-permute-start(bf16[64,3712]{1,0:T(8,128)(2,1)S(1)} %collective-permute-done.2.refs_3_), channel_id=1, source_target_pairs={{0,1},{1,0},{2,3},{3,2},{4,5},{5,4},{6,7},{7,6},{8,9},{9,8},{10,11... | collective-permute-start | bytes 1425416 | tf_op jit(solution)/shard_map/ppermute | solution.py:92
  42.0 11.7 %collective-permute-start.7 = (bf16[64,3712]{1,0:T(8,128)(2,1)S(1)}, bf16[64,3712]{1,0:T(8,128)(2,1)S(1)}, u32[]{:S(2)}, u32[]{:S(2)}) collective-permute-start(bf16[64,3712]{1,0:T(8,128)(2,1)S(1)} %collective-permute-done.3.refs_4_), channel_id=1, source_target_pairs={{0,1},{1,0},{2,3},{3,2},{4,5},{5,4},{6,7},{7,6},{8,9},{9,8},{10,11... | collective-permute-start | bytes 1425416 | tf_op jit(solution)/shard_map/ppermute | solution.py:92
  42.5 37.5 %collective-permute-start.12 = (bf16[3,192,1024]{2,1,0:T(8,128)(2,1)}, bf16[3,192,1024]{2,1,0:T(8,128)(2,1)S(1)}, u32[]{:S(2)}, u32[]{:S(2)}) collective-permute-start(bf16[3,192,1024]{2,1,0:T(8,128)(2,1)} %get-tuple-element.161), channel_id=1, source_target_pairs={{0,16},{16,0},{1,17},{17,1},{2,18},{18,2},{3,19},{19,3},{4,20},{20... | collective-permute-start | bytes 3538952 | tf_op jit(solution)/shard_map/ppermute | solution.py:31
  53.7 23.7 %copy-start.15 = (bf16[64,3712]{1,0:T(8,128)(2,1)}, bf16[64,3712]{1,0:T(8,128)(2,1)S(1)}, u32[]{:S(2)}) copy-start(bf16[64,3712]{1,0:T(8,128)(2,1)S(1)} %collective-permute-done.8.refs_3_) | copy-start | bytes 1425412
  64.9 12.5 %collective-permute-start.13 = (bf16[64,3712]{1,0:T(8,128)(2,1)S(1)}, bf16[64,3712]{1,0:T(8,128)(2,1)S(1)}, u32[]{:S(2)}, u32[]{:S(2)}) collective-permute-start(bf16[64,3712]{1,0:T(8,128)(2,1)S(1)} %collective-permute-done.8.refs_3_), channel_id=1, source_target_pairs={{0,2},{1,3},{2,0},{3,1},{4,6},{5,7},{6,4},{7,5},{8,10},{9,11},{10,... | collective-permute-start | bytes 1425416 | tf_op jit(solution)/shard_map/ppermute | solution.py:92
  65.5 12.4 %collective-permute-start.10 = (bf16[64,3712]{1,0:T(8,128)(2,1)}, bf16[64,3712]{1,0:T(8,128)(2,1)S(1)}, u32[]{:S(2)}, u32[]{:S(2)}) collective-permute-start(bf16[64,3712]{1,0:T(8,128)(2,1)} %pad_maximum_fusion.refs_3_), channel_id=1, source_target_pairs={{0,12},{1,13},{2,14},{3,15},{4,0},{5,1},{6,2},{7,3},{8,4},{9,5},{1... | collective-permute-start | bytes 1425416 | tf_op jit(solution)/shard_map/ppermute | solution.py:92
  67.2 31.5 %collective-permute-start.9 = (bf16[3,192,1024]{2,1,0:T(8,128)(2,1)}, bf16[3,192,1024]{2,1,0:T(8,128)(2,1)S(1)}, u32[]{:S(2)}, u32[]{:S(2)}) collective-permute-start(bf16[3,192,1024]{2,1,0:T(8,128)(2,1)} %get-tuple-element.170), channel_id=1, source_target_pairs={{0,16},{16,0},{1,17},{17,1},{2,18},{18,2},{3,19},{19,3},{4,20},{20... | collective-permute-start | bytes 3538952 | tf_op jit(solution)/shard_map/ppermute | solution.py:31
  77.4 2.6 %collective-permute-start.14 = (bf16[64,3712]{1,0:T(8,128)(2,1)S(1)}, bf16[64,3712]{1,0:T(8,128)(2,1)S(1)}, u32[]{:S(2)}, u32[]{:S(2)}) collective-permute-start(bf16[64,3712]{1,0:T(8,128)(2,1)S(1)} %collective-permute-done.8.refs_3_), channel_id=1, source_target_pairs={{0,1},{1,0},{2,3},{3,2},{4,5},{5,4},{6,7},{7,6},{8,9},{9,8},{10,11... | collective-permute-start | bytes 1425416 | tf_op jit(solution)/shard_map/ppermute | solution.py:92
  77.4 2.7 %collective-permute-start.15 = (bf16[64,3712]{1,0:T(8,128)(2,1)S(1)}, bf16[64,3712]{1,0:T(8,128)(2,1)S(1)}, u32[]{:S(2)}, u32[]{:S(2)}) collective-permute-start(bf16[64,3712]{1,0:T(8,128)(2,1)S(1)} %collective-permute-done.13.refs_4_), channel_id=1, source_target_pairs={{0,1},{1,0},{2,3},{3,2},{4,5},{5,4},{6,7},{7,6},{8,9},{9,8},{10,11... | collective-permute-start | bytes 1425416 | tf_op jit(solution)/shard_map/ppermute | solution.py:92
  77.9 18.7 %copy-start.16 = (bf16[64,3712]{1,0:T(8,128)(2,1)}, bf16[64,3712]{1,0:T(8,128)(2,1)S(1)}, u32[]{:S(2)}) copy-start(bf16[64,3712]{1,0:T(8,128)(2,1)S(1)} %collective-permute-done.10.refs_3_) | copy-start | bytes 1425412
  77.9 18.7 %collective-permute-start.11 = (bf16[64,3712]{1,0:T(8,128)(2,1)S(1)}, bf16[64,3712]{1,0:T(8,128)(2,1)S(1)}, u32[]{:S(2)}, u32[]{:S(2)}) collective-permute-start(bf16[64,3712]{1,0:T(8,128)(2,1)S(1)} %collective-permute-done.10.refs_3_), channel_id=1, source_target_pairs={{0,2},{1,3},{2,0},{3,1},{4,6},{5,7},{6,4},{7,5},{8,10},{9,11},{10,... | collective-permute-start | bytes 1425416 | tf_op jit(solution)/shard_map/ppermute | solution.py:92
  96.7 2.1 collective-permute-start.16
  96.8 2.5 %collective-permute-start.17 = (bf16[64,3712]{1,0:T(8,128)(2,1)S(1)}, bf16[64,3712]{1,0:T(8,128)(2,1)S(1)}, u32[]{:S(2)}, u32[]{:S(2)}) collective-permute-start(bf16[64,3712]{1,0:T(8,128)(2,1)S(1)} %collective-permute-done.11.refs_4_), channel_id=1, source_target_pairs={{0,1},{1,0},{2,3},{3,2},{4,5},{5,4},{6,7},{7,6},{8,9},{9,8},{10,11... | collective-permute-start | bytes 1425416 | tf_op jit(solution)/shard_map/ppermute | solution.py:92
  97.3 29.0 %collective-permute-start.21 = (bf16[3,192,1024]{2,1,0:T(8,128)(2,1)}, bf16[3,192,1024]{2,1,0:T(8,128)(2,1)S(1)}, u32[]{:S(2)}, u32[]{:S(2)}) collective-permute-start(bf16[3,192,1024]{2,1,0:T(8,128)(2,1)} %get-tuple-element.187), channel_id=1, source_target_pairs={{0,16},{16,0},{1,17},{17,1},{2,18},{18,2},{3,19},{19,3},{4,20},{20... | collective-permute-start | bytes 3538952 | tf_op jit(solution)/shard_map/ppermute | solution.py:31
  115.1 2.8 %collective-permute-start.18 = (bf16[128,3712]{1,0:T(8,128)(2,1)}, bf16[128,3712]{1,0:T(8,128)(2,1)S(1)}, u32[]{:S(2)}, u32[]{:S(2)}) collective-permute-start(bf16[128,3712]{1,0:T(8,128)(2,1)} %get-tuple-element.202), channel_id=1, source_target_pairs={{0,1},{1,0},{2,3},{3,2},{4,5},{5,4},{6,7},{7,6},{8,9},{9,8},{10,11... | collective-permute-start | bytes 2850824 | tf_op jit(solution)/shard_map/ppermute | solution.py:92
  115.3 35.4 %collective-permute-start.20 = (bf16[3,192,1024]{2,1,0:T(8,128)(2,1)}, bf16[3,192,1024]{2,1,0:T(8,128)(2,1)S(1)}, u32[]{:S(2)}, u32[]{:S(2)}) collective-permute-start(bf16[3,192,1024]{2,1,0:T(8,128)(2,1)} %get-tuple-element.203), channel_id=1, source_target_pairs={{0,16},{16,0},{1,17},{17,1},{2,18},{18,2},{3,19},{19,3},{4,20},{20... | collective-permute-start | bytes 3538952 | tf_op jit(solution)/shard_map/ppermute | solution.py:31
  127.3 10.9 %copy-start.36 = (bf16[64,3712]{1,0:T(8,128)(2,1)S(1)}, bf16[64,3712]{1,0:T(8,128)(2,1)}, u32[]{:S(2)}) copy-start(bf16[64,3712]{1,0:T(8,128)(2,1)} %get-tuple-element.208) | copy-start | bytes 1425412
  127.3 11.5 %copy-start.31 = (bf16[128,3712]{1,0:T(8,128)(2,1)S(1)}, bf16[128,3712]{1,0:T(8,128)(2,1)}, u32[]{:S(2)}) copy-start(bf16[128,3712]{1,0:T(8,128)(2,1)} %get-tuple-element.189) | copy-start | bytes 2850820
  138.1 2.8 %collective-permute-start.22 = (bf16[128,3712]{1,0:T(8,128)(2,1)}, bf16[128,3712]{1,0:T(8,128)(2,1)S(1)}, u32[]{:S(2)}, u32[]{:S(2)}) collective-permute-start(bf16[128,3712]{1,0:T(8,128)(2,1)} %get-tuple-element.217), channel_id=1, source_target_pairs={{0,1},{1,0},{2,3},{3,2},{4,5},{5,4},{6,7},{7,6},{8,9},{9,8},{10,11... | collective-permute-start | bytes 2850824 | tf_op jit(solution)/shard_map/ppermute | solution.py:92
  138.2 24.4 %collective-permute-start.19 = (bf16[64,3712]{1,0:T(8,128)(2,1)S(1)}, bf16[64,3712]{1,0:T(8,128)(2,1)S(1)}, u32[]{:S(2)}, u32[]{:S(2)}) collective-permute-start(bf16[64,3712]{1,0:T(8,128)(2,1)S(1)} %copy-done.36), channel_id=1, source_target_pairs={{0,2},{1,3},{2,0},{3,1},{4,6},{5,7},{6,4},{7,5},{8,10},{9,11},{10,... | collective-permute-start | bytes 1425416 | tf_op jit(solution)/shard_map/ppermute | solution.py:92
  138.8 40.9 %collective-permute-start.29 = (bf16[128,3712]{1,0:T(8,128)(2,1)S(1)}, bf16[128,3712]{1,0:T(8,128)(2,1)S(1)}, u32[]{:S(2)}, u32[]{:S(2)}) collective-permute-start(bf16[128,3712]{1,0:T(8,128)(2,1)S(1)} %copy-done.31), channel_id=1, source_target_pairs={{0,1},{1,0},{2,3},{3,2},{4,5},{5,4},{6,7},{7,6},{8,9},{9,8},{10,11... | collective-permute-start | bytes 2850824 | tf_op jit(solution)/shard_map/ppermute | solution.py:92
  144.5 21.5 %collective-permute-start.24 = (bf16[64,3712]{1,0:T(8,128)(2,1)}, bf16[64,3712]{1,0:T(8,128)(2,1)S(1)}, u32[]{:S(2)}, u32[]{:S(2)}) collective-permute-start(bf16[64,3712]{1,0:T(8,128)(2,1)} %get-tuple-element.231), channel_id=1, source_target_pairs={{0,2},{1,3},{2,0},{3,1},{4,6},{5,7},{6,4},{7,5},{8,10},{9,11},{10,... | collective-permute-start | bytes 1425416 | tf_op jit(solution)/shard_map/ppermute | solution.py:92
  151.7 10.9 %copy-start.5 = (f32[64,3712]{1,0:T(8,128)S(1)}, f32[64,3712]{1,0:T(8,128)}, u32[]{:S(2)}) copy-start(f32[64,3712]{1,0:T(8,128)} %get-tuple-element.229) | copy-start | bytes 2850820
  151.7 14.2 %copy-start.6 = (f32[64,3712]{1,0:T(8,128)S(1)}, f32[64,3712]{1,0:T(8,128)}, u32[]{:S(2)}) copy-start(f32[64,3712]{1,0:T(8,128)} %get-tuple-element.232) | copy-start | bytes 2850820
  162.5 3.7 %copy-start.10 = (bf16[128,3712]{1,0:T(8,128)(2,1)S(1)}, bf16[128,3712]{1,0:T(8,128)(2,1)}, u32[]{:S(2)}) copy-start(bf16[128,3712]{1,0:T(8,128)(2,1)} %get-tuple-element.234) | copy-start | bytes 2850820
  162.5 3.7 %collective-permute-start.26 = (bf16[128,3712]{1,0:T(8,128)(2,1)}, bf16[128,3712]{1,0:T(8,128)(2,1)S(1)}, u32[]{:S(2)}, u32[]{:S(2)}) collective-permute-start(bf16[128,3712]{1,0:T(8,128)(2,1)} %get-tuple-element.228), channel_id=1, source_target_pairs={{0,1},{1,0},{2,3},{3,2},{4,5},{5,4},{6,7},{7,6},{8,9},{9,8},{10,11... | collective-permute-start | bytes 2850824 | tf_op jit(solution)/shard_map/ppermute | solution.py:92
  162.7 30.1 %collective-permute-start.23 = (bf16[64,3712]{1,0:T(8,128)(2,1)S(1)}, bf16[64,3712]{1,0:T(8,128)(2,1)S(1)}, u32[]{:S(2)}, u32[]{:S(2)}) collective-permute-start(bf16[64,3712]{1,0:T(8,128)(2,1)S(1)} %add_convert_fusion.3), channel_id=1, source_target_pairs={{0,12},{1,13},{2,14},{3,15},{4,0},{5,1},{6,2},{7,3},{8,4},{9,5},{1... | collective-permute-start | bytes 1425416 | tf_op jit(solution)/shard_map/ppermute | solution.py:92
  166.1 39.5 %collective-permute-start.25 = (bf16[64,3712]{1,0:T(8,128)(2,1)S(1)}, bf16[64,3712]{1,0:T(8,128)(2,1)S(1)}, u32[]{:S(2)}, u32[]{:S(2)}) collective-permute-start(bf16[64,3712]{1,0:T(8,128)(2,1)S(1)} %add_convert_fusion.2), channel_id=1, source_target_pairs={{0,8},{1,9},{2,10},{3,11},{4,12},{5,13},{6,14},{7,15},{8,0},{9,1},... | collective-permute-start | bytes 1425416 | tf_op jit(solution)/shard_map/ppermute | solution.py:92
  166.6 13.2 %copy-start.9 = (bf16[128,3712]{1,0:T(8,128)(2,1)S(1)}, bf16[128,3712]{1,0:T(8,128)(2,1)}, u32[]{:S(2)}) copy-start(bf16[128,3712]{1,0:T(8,128)(2,1)} %get-tuple-element.255) | copy-start | bytes 2850820
  166.6 13.0 %collective-permute-start.27 = (bf16[64,3712]{1,0:T(8,128)(2,1)S(1)}, bf16[64,3712]{1,0:T(8,128)(2,1)S(1)}, u32[]{:S(2)}, u32[]{:S(2)}) collective-permute-start(bf16[64,3712]{1,0:T(8,128)(2,1)S(1)} %slice.119), channel_id=1, source_target_pairs={{0,2},{1,3},{2,0},{3,1},{4,6},{5,7},{6,4},{7,5},{8,10},{9,11},{10,... | collective-permute-start | bytes 1425416 | tf_op jit(solution)/shard_map/ppermute | solution.py:92
  180.1 25.6 %collective-permute-start.28 = (bf16[64,3712]{1,0:T(8,128)(2,1)S(1)}, bf16[64,3712]{1,0:T(8,128)(2,1)S(1)}, u32[]{:S(2)}, u32[]{:S(2)}) collective-permute-start(bf16[64,3712]{1,0:T(8,128)(2,1)S(1)} %add_convert_fusion.1), channel_id=1, source_target_pairs={{0,4},{1,5},{2,6},{3,7},{4,8},{5,9},{6,10},{7,11},{8,12},{9,13},{1... | collective-permute-start | bytes 1425416 | tf_op jit(solution)/shard_map/ppermute | solution.py:92
  180.7 11.9 %collective-permute-start.30 = (bf16[64,3712]{1,0:T(8,128)(2,1)S(1)}, bf16[64,3712]{1,0:T(8,128)(2,1)S(1)}, u32[]{:S(2)}, u32[]{:S(2)}) collective-permute-start(bf16[64,3712]{1,0:T(8,128)(2,1)S(1)} %slice.118), channel_id=1, source_target_pairs={{0,2},{1,3},{2,0},{3,1},{4,6},{5,7},{6,4},{7,5},{8,10},{9,11},{10,... | collective-permute-start | bytes 1425416 | tf_op jit(solution)/shard_map/ppermute | solution.py:92
  182.7 4.6 %copy-start.37 = (bf16[192,1024]{1,0:T(8,128)(2,1)S(1)}, bf16[192,1024]{1,0:T(8,128)(2,1)}, u32[]{:S(2)}) copy-start(bf16[192,1024]{1,0:T(8,128)(2,1)} %get-tuple-element.274) | copy-start | bytes 1179652
  182.7 4.6 %copy-start.39 = (bf16[192,1024]{1,0:T(8,128)(2,1)S(1)}, bf16[192,1024]{1,0:T(8,128)(2,1)}, u32[]{:S(2)}) copy-start(bf16[192,1024]{1,0:T(8,128)(2,1)} %get-tuple-element.275) | copy-start | bytes 1179652
  182.7 4.6 %copy-start.42 = (bf16[192,1024]{1,0:T(8,128)(2,1)S(1)}, bf16[192,1024]{1,0:T(8,128)(2,1)}, u32[]{:S(2)}) copy-start(bf16[192,1024]{1,0:T(8,128)(2,1)} %get-tuple-element.276) | copy-start | bytes 1179652
  182.7 4.6 %copy-start.45 = (bf16[192,1024]{1,0:T(8,128)(2,1)S(1)}, bf16[192,1024]{1,0:T(8,128)(2,1)}, u32[]{:S(2)}) copy-start(bf16[192,1024]{1,0:T(8,128)(2,1)} %get-tuple-element.277) | copy-start | bytes 1179652
  187.3 5.4 %slice-start = ((f32[128,3712]{1,0:T(8,128)}), f32[64,3712]{1,0:T(8,128)S(1)}, s32[]{:S(2)}) async-start(f32[128,3712]{1,0:T(8,128)} %copy-done), calls=%async_computation | async-start | bytes 1900544 | tf_op jit(solution)/shard_map/slice | solution.py:183
  192.8 20.9 %copy-start.30 = (s32[32,8]{0,1:T(8,128)S(1)}, s32[32,8]{0,1:T(8,128)}, u32[]{:S(2)}) copy-start(s32[32,8]{0,1:T(8,128)} %param.8) | copy-start | bytes 3076
  206.0 7.4 %collective-permute-start.31 = (bf16[32,3712]{1,0:T(8,128)(2,1)S(1)}, bf16[32,3712]{1,0:T(8,128)(2,1)S(1)}, u32[]{:S(2)}, u32[]{:S(2)}) collective-permute-start(bf16[32,3712]{1,0:T(8,128)(2,1)S(1)} %broadcast_select_fusion.4), channel_id=1, source_target_pairs={{0,16},{16,0},{1,17},{17,1},{2,18},{18,2},{3,19},{19,3},{4,20},{20... | collective-permute-start | bytes 712712 | tf_op jit(solution)/shard_map/ppermute | solution.py:31
  (34 other events, 52.6 us)
where the time goes:
time: 216 us
  Pallas kernels  76.4 us (35%)
  waiting for transfers between devices  74 us (34%)
  starting transfers between devices  29.6 us (14%)
  local copies, waits for them, and re-layouts  14.1 us (7%)
  matrix products  14 us (6%)
  other arithmetic  6.31 us (3%)
    ppermute x26, waiting for transfers between devices, shift_expert(): return lax.ppermute(value, 'expert', pairs)  52.7 us
    pallas_call x2, Pallas kernels, finish_and_project(): pl.pallas_call(body, grid=(hidden // tile,), in_specs=[whole(value.shape)...  30.2 us
    pallas_call x2, Pallas kernels, finish(): pl.pallas_call(lambda *refs: finish_body(len(sent), number_parts, *refs),...  21.6 us
    ppermute x6, waiting for transfers between devices, shift_dp(): lax.ppermute(value, 'dp', [(i, (i + step) % groups) for i in range(groups)])  21.3 us
    pallas_call x2, Pallas kernels, project(): pl.pallas_call(lambda *refs: project_body(len(parts), part, *refs), grid=...  19.3 us
    ppermute x26, starting transfers between devices, shift_expert(): return lax.ppermute(value, 'expert', pairs)  19 us
    dot_general x3, matrix products, dot_tn(): lax.dot_general(first, second, (((0,), (0,)), ((), ())), preferred_elemen...  14 us
    unnamed x101, local copies, waits for them, and re-layouts  11.1 us
  transfers between devices with their start and end apart: 32, of which 13 were waited for; matrix products, arithmetic and copies ran while one was open for 8% of the time, Pallas kernels for 35%

commit v1 on v0

--- a/solution.py
+++ b/solution.py
@@ -184,23 +184,24 @@
     return parts[:1] + [part.astype(BF) for part in parts[1:]]
 
 
-def merge_between(values, pieces):
-    rows, wide = values[0].shape
-    rows = rows // pieces
-    kinds = [F32] + [BF] * (pieces - 1)
+def merge_between(groups, kinds):
+    sizes = [len(group) for group in groups]
 
     def body(*refs):
-        for number in range(pieces):
-            here = slice(number * rows, (number + 1) * rows)
-            total = add_all(refs[0][here].astype(F32), [ref[here] for ref in refs[1 : len(values)]])
-            refs[len(values) + number][...] = total.astype(kinds[number])
+        start = 0
+        for size, out in zip(sizes, refs[sum(sizes) :]):
+            total = add_all(refs[start][...].astype(F32), [ref[...] for ref in refs[start + 1 : start + size]])
+            out[...] = total.astype(out.dtype)
+            start += size
 
     return pl.pallas_call(
         body,
-        out_shape=[jax.ShapeDtypeStruct((rows, wide), kind) for kind in kinds],
+        out_shape=[
+            jax.ShapeDtypeStruct(group[0].shape, kind) for group, kind in zip(groups, kinds)
+        ],
         compiler_params=pltpu.CompilerParams(vmem_limit_bytes=56 * 2**20),
         name="merge",
-    )(*values)
+    )(*[value for group in groups for value in group])
 
 
 def finish_body(number_sent, number_parts, *refs):
@@ -397,6 +398,13 @@
         along[number] = gather_start(mine, 1)
         around[number] = [] if number else [gather_start(mine, 2)]
 
+    def add_up(numbers):
+        if len(numbers):
+            (arrived,) = order.enter([finals.pop(number) for number in numbers])
+            total = add_all(arrived[0].astype(F32), arrived[1:])
+            order.leave(total)
+            finals[numbers[0]] = total
+
     def start_back(number):
         mine, others = held[number]
         (others,) = order.enter(others)
@@ -412,6 +420,9 @@
             gather_start(value, 2) for value in (mine if number else mine[1:])
         ]
 
+    def cuts_of(number):
+        return inner if 0 < number < last else 1
+
     def ready_parts(across):
         return [piece[index] for index in range(core) for piece in across]
 
@@ -422,6 +433,8 @@
             if outer > 3:
                 late, _ = lax.optimization_barrier((payload, tied))
                 pieces[3] = shift_expert(late, 0, 3)
+            along[2] = gather_start(tied, 1)
+            around[2] = []
         projected(
             number, project(ready_parts(across), *tables, slots, gate_w, up_w, down_w)
         )
@@ -435,30 +448,43 @@
     def finished(number, results):
         ends[number] = results[:3]
         back = results[3:]
-        moving[number] = (
-            back[0],
-            [shift_expert(back[step], 2, -step) for step in range(1, core)],
-        )
+        cuts = len(back) // core
+        moving[number] = [
+            (
+                back[cut],
+                [shift_expert(back[step * cuts + cut], 2, -step) for step in range(1, core)],
+            )
+            for cut in range(cuts)
+        ]
 
     def finish_chunk(number, later=None):
         own, arrived, across = order.enter(*sums[number], around.get(later))
+        if number == last:
+            order.leave(*arrived)
+            for earlier in range(1, number - 1):
+                next_outer(earlier)
+            own, arrived = order.enter(own, arrived)
         x_rows, grad, term, weight, pick = picked[number][:5]
         left = (own, arrived, grad, weight, pick, route_cols)
         if later is None:
-            results = finish(*left, gate_w, up_w, down_w, core)
+            results = finish(*left, gate_w, up_w, down_w, core * cuts_of(number))
             order.leave(*results[3:])
             finished(number, results)
         else:
             made, results = finish_and_project(
-                left, ready_parts(across), *tables, slots, gate_w, up_w, down_w, core
+                left, ready_parts(across), *tables, slots, gate_w, up_w, down_w, core * cuts_of(number)
             )
             order.leave(made[6], *results[3:])
             projected(later, made)
             finished(number, results)
 
     def next_inner(number):
-        mine, arrived = order.enter(*moving[number])
-        mine, *others = (merge_between if 0 < number < last else merge)([mine] + arrived, inner)
+        (cuts,) = order.enter(moving[number])
+        if len(cuts) == inner:
+            groups_here = [[mine] + arrived for mine, arrived in cuts]
+            mine, *others = merge_between(groups_here, [F32] + [BF] * (inner - 1))
+        else:
+            mine, *others = merge([cuts[0][0]] + cuts[0][1], inner)
         order.leave(mine, *others)
         held[number] = (mine, others)
         if number or not last:
@@ -487,7 +513,6 @@
         start_core(1)
         partial_sums(1)
     if last > 1:
-        start_inner(2)
         if last > 2:
             start_inner(3)
         start_core(2)
@@ -504,8 +529,9 @@
             finish_chunk(number)
         if 0 < number < last:
             next_inner(number)
-    for number in range(1, last):
-        next_outer(number)
+    add_up(range(1, last - 1))
+    if last > 1:
+        next_outer(last - 1)
     next_inner(last)
 
     def rows_of(table, index):

time: 216 us -> 205 us (0.949)
  waiting for transfers between devices: 74 us -> 66.4 us
  local copies, waits for them, and re-layouts: 14.1 us -> 9.96 us
    ppermute x26 -> x28, waiting for transfers between devices: 52.7 us -> 39.1 us  [shift_expert(): return lax.ppermute(value, 'expert', pairs)]
    ppermute x6, waiting for transfers between devices: 21.3 us -> 27.4 us  [shift_dp(): lax.ppermute(value, 'dp', [(i, (i + step) % groups) for i in range(groups)])]
    unnamed x101 -> x107, local copies, waits for them, and re-layouts: 11.1 us -> 6.97 us
    ppermute x26 -> x28, starting transfers between devices: 19 us -> 20.9 us  [shift_expert(): return lax.ppermute(value, 'expert', pairs)]
  transfers between devices with their start and end apart: 32 -> 34, of which waited for: 13 -> 17; matrix products, arithmetic and copies ran while one was open for 8% -> 8% of each run, Pallas kernels for 35% -> 37%
where the time goes in v1:
time: 205 us
  Pallas kernels  76.3 us (37%)
  waiting for transfers between devices  66.4 us (32%)
  starting transfers between devices  31.6 us (15%)
  matrix products  14 us (7%)
  local copies, waits for them, and re-layouts  9.96 us (5%)
  other arithmetic  5.54 us (3%)
    ppermute x28, waiting for transfers between devices, shift_expert(): return lax.ppermute(value, 'expert', pairs)  39.1 us
    pallas_call x2, Pallas kernels, finish_and_project(): pl.pallas_call(body, grid=(hidden // tile,), in_specs=[whole(value.shape)...  30 us
    ppermute x6, waiting for transfers between devices, shift_dp(): lax.ppermute(value, 'dp', [(i, (i + step) % groups) for i in range(groups)])  27.4 us
    pallas_call x2, Pallas kernels, finish(): pl.pallas_call(lambda *refs: finish_body(len(sent), number_parts, *refs),...  21.6 us
    ppermute x28, starting transfers between devices, shift_expert(): return lax.ppermute(value, 'expert', pairs)  20.9 us
    pallas_call x2, Pallas kernels, project(): pl.pallas_call(lambda *refs: project_body(len(parts), part, *refs), grid=...  19.3 us
    dot_general x3, matrix products, dot_tn(): lax.dot_general(first, second, (((0,), (0,)), ((), ())), preferred_elemen...  14 us
    ppermute x6, starting transfers between devices, shift_dp(): lax.ppermute(value, 'dp', [(i, (i + step) % groups) for i in range(groups)])  10.7 us
  transfers between devices with their start and end apart: 34, of which 17 were waited for; matrix products, arithmetic and copies ran while one was open for 8% of the time, Pallas kernels for 37%

profile of v1, /device:TPU:0, one launch (start us, length us, event | category | flops | bytes accessed | tf_op | source)
XLA Modules:
  0.0 205.1 jit_solution(7654243283738146251)
XLA Ops:
  0.6 0.7 select_reduce_fusion.1
  1.5 1.1 fusion.41
  2.9 3.0 %collective-permute-start = (bf16[32,3712]{1,0:T(8,128)(2,1)S(1)}, bf16[32,3712]{1,0:T(8,128)(2,1)S(1)}, u32[]{:S(2)}, u32[]{:S(2)}) collective-permute-start(bf16[32,3712]{1,0:T(8,128)(2,1)S(1)} %broadcast_select_fusion.5), channel_id=1, source_target_pairs={{0,16},{16,0},{1,17},{17,1},{2,18},{18,2},{3,19},{19,3},{4,20},{20... | collective-permute-start | bytes 712712 | tf_op jit(solution)/shard_map/ppermute | solution.py:31
  5.9 0.8 fusion.32.refs_1_
  6.7 5.0 %collective-permute-done = bf16[32,3712]{1,0:T(8,128)(2,1)S(1)} collective-permute-done((bf16[32,3712]{1,0:T(8,128)(2,1)S(1)}, bf16[32,3712]{1,0:T(8,128)(2,1)S(1)}, u32[]{:S(2)}, u32[]{:S(2)}) %collective-permute-start) | collective-permute-done | bytes 237600 | tf_op jit(solution)/shard_map/ppermute | solution.py:31
  13.0 1.8 collective-permute-start.2
  14.8 1.5 collective-permute-start.1
  16.4 10.5 %collective-permute-done.2.refs_3_ = bf16[64,3712]{1,0:T(8,128)(2,1)S(1)} collective-permute-done((bf16[64,3712]{1,0:T(8,128)(2,1)S(1)}, bf16[64,3712]{1,0:T(8,128)(2,1)S(1)}, u32[]{:S(2)}, u32[]{:S(2)}) %collective-permute-start.2) | collective-permute-done | bytes 475168 | tf_op jit(solution)/shard_map/ppermute | solution.py:92
  26.9 1.6 collective-permute-start.3
  28.5 1.9 collective-permute-start.8
  30.5 0.8 copy-done.26
  31.4 9.6 %project.2 = (bf16[192,1792]{1,0:T(8,128)(2,1)}, bf16[192,1792]{1,0:T(8,128)(2,1)}, bf16[192,1792]{1,0:T(8,128)(2,1)}, f32[192,128]{1,0:T(8,128)}, bf16[192,256]...) custom-call(bf16[8,128]{1,0:T(8,128)(2,1)} %broadcast_in_dim.33.refs_0_, ...), custom_call_target="tpu_custom_call" | custom-call | tf_op jit(solution)/shard_map/project/pallas_call | solution.py:160
  41.7 1.5 collective-permute-start.12
  43.2 9.4 %collective-permute-done.8.refs_3_ = bf16[64,3712]{1,0:T(8,128)(2,1)S(1)} collective-permute-done((bf16[64,3712]{1,0:T(8,128)(2,1)S(1)}, bf16[64,3712]{1,0:T(8,128)(2,1)S(1)}, u32[]{:S(2)}, u32[]{:S(2)}) %collective-permute-start.8) | collective-permute-done | bytes 475168 | tf_op jit(solution)/shard_map/ppermute | solution.py:92
  53.2 1.7 collective-permute-start.10
  54.9 9.7 %project.3 = (bf16[192,1792]{1,0:T(8,128)(2,1)}, bf16[192,1792]{1,0:T(8,128)(2,1)}, bf16[192,1792]{1,0:T(8,128)(2,1)}, f32[192,128]{1,0:T(8,128)}, bf16[192,256]...) custom-call(bf16[8,128]{1,0:T(8,128)(2,1)} %broadcast_in_dim.33.refs_0_, ...), custom_call_target="tpu_custom_call" | custom-call | tf_op jit(solution)/shard_map/project/pallas_call | solution.py:160
  64.6 1.5 collective-permute-start.9
  66.7 1.5 collective-permute-start.11
  68.9 1.8 collective-permute-done.12.refs_8_
  70.7 1.0 copy-done.5
  72.0 15.0 %step.2 = (bf16[192,1792]{1,0:T(8,128)(2,1)}, bf16[192,1792]{1,0:T(8,128)(2,1)}, bf16[192,1792]{1,0:T(8,128)(2,1)}, f32[192,128]{1,0:T(8,128)}, bf16[192,256]{1,...) custom-call(bf16[8,128]{1,0:T(8,128)(2,1)} %broadcast_in_dim.33.refs, ...), custom_call_target="tpu_custom_call" | custom-call | tf_op jit(solution)/shard_map/step/pallas_call | solution.py:310
  87.1 1.6 collective-permute-start.22
  89.2 6.8 %collective-permute-done.9.refs_8_ = bf16[3,192,1024]{2,1,0:T(8,128)(2,1)S(1)} collective-permute-done((bf16[3,192,1024]{2,1,0:T(8,128)(2,1)}, bf16[3,192,1024]{2,1,0:T(8,128)(2,1)S(1)}, u32[]{:S(2)}, u32[]{:S(2)}) %collective-permute-start.9) | collective-permute-done | bytes 1179680 | tf_op jit(solution)/shard_map/ppermute | solution.py:31
  96.0 1.0 copy-done.2
  97.3 15.0 %step.3 = (bf16[192,1792]{1,0:T(8,128)(2,1)}, bf16[192,1792]{1,0:T(8,128)(2,1)}, bf16[192,1792]{1,0:T(8,128)(2,1)}, f32[192,128]{1,0:T(8,128)}, bf16[192,256]{1,...) custom-call(bf16[8,128]{1,0:T(8,128)(2,1)} %broadcast_in_dim.33.refs, ...), custom_call_target="tpu_custom_call" | custom-call | tf_op jit(solution)/shard_map/step/pallas_call | solution.py:310
  112.3 1.6 collective-permute-start.21
  114.4 1.5 collective-permute-done.18.refs_1_
  117.4 2.7 %merge.2 = (f32[64,3712]{1,0:T(8,128)}, bf16[64,3712]{1,0:T(8,128)(2,1)}) custom-call(bf16[64,3712]{1,0:T(8,128)(2,1)} %get-tuple-element.215.refs_0_, bf16[64,3712]{1,0:T(8,128)(2,1)} %copy-done.31, bf16[64,3712]{1,0:T(8,128)(2,1)} %get-tuple-element.217.refs_2_, bf16[64,3712]{1,0:T(8,128)(2,1)} %copy-done.32), custom_call_target="tpu_custom_call" | custom-call | tf_op jit(solution)/shard_map/merge/pallas_call | solution.py:197
  120.1 1.2 collective-permute-done.22.refs_1_
  121.3 1.0 copy-done.4
  122.3 10.8 %finish.2 = (bf16[192,1024]{1,0:T(8,128)(2,1)}, bf16[192,1024]{1,0:T(8,128)(2,1)}, bf16[192,1024]{1,0:T(8,128)(2,1)}, bf16[64,3712]{1,0:T(8,128)(2,1)}, bf16[64,...) custom-call(f32[3,192,1024]{2,1,0:T(8,128)} %get-tuple-element.224.refs_0_, ...), custom_call_target="tpu_custom_call" | custom-call | tf_op jit(solution)/shard_map/finish/pallas_call | solution.py:275
  134.2 0.9 collective-permute-done.23.refs_1_
  136.6 2.7 %merge.3 = (f32[64,3712]{1,0:T(8,128)}, bf16[64,3712]{1,0:T(8,128)(2,1)}) custom-call(bf16[64,3712]{1,0:T(8,128)(2,1)} %get-tuple-element.233.refs_0_, bf16[64,3712]{1,0:T(8,128)(2,1)} %copy-done.29, bf16[64,3712]{1,0:T(8,128)(2,1)} %get-tuple-element.235.refs_2_, bf16[64,3712]{1,0:T(8,128)(2,1)} %copy-done.30), custom_call_target="tpu_custom_call" | custom-call | tf_op jit(solution)/shard_map/merge/pallas_call | solution.py:197
  139.3 6.3 %collective-permute-done.21.refs_1_ = bf16[3,192,1024]{2,1,0:T(8,128)(2,1)S(1)} collective-permute-done((bf16[3,192,1024]{2,1,0:T(8,128)(2,1)}, bf16[3,192,1024]{2,1,0:T(8,128)(2,1)S(1)}, u32[]{:S(2)}, u32[]{:S(2)}) %collective-permute-start.21) | collective-permute-done | bytes 1179680 | tf_op jit(solution)/shard_map/ppermute | solution.py:31
  145.7 0.8 collective-permute-done.20
  146.6 1.6 collective-permute-start.25
  148.2 1.0 collective-permute-start.26
  149.2 10.8 %finish.3 = (bf16[192,1024]{1,0:T(8,128)(2,1)}, bf16[192,1024]{1,0:T(8,128)(2,1)}, bf16[192,1024]{1,0:T(8,128)(2,1)}, bf16[128,3712]{1,0:T(8,128)(2,1)}, bf16[128,3712]{1,0:T(8,128)(2,1)}) custom-call(f32[3,192,1024]{2,1,0:T(8,128)} %get-tuple-element.243.refs_0_, bf16[3,192,1024]{2,1,0:T(8,128)(2,1)} %copy-done.3, ...), custom_call_target="tpu_custom_call" | custom-call | tf_op jit(solution)/shard_map/finish/pallas_call | solution.py:275
  161.6 1.7 collective-permute-done.28
  163.6 1.1 collective-permute-start.29
  164.8 5.0 %fusion = bf16[1,1024,1792]{2,1,0:T(8,128)(2,1)} fusion(bf16[192,1792]{1,0:T(8,128)(2,1)S(1)} %copy-done.38, bf16[192,1792]{1,0:T(8,128)(2,1)S(1)} %copy-done.37, bf16[192,1792]{1,0:T(8,128)(2,1)S(1)} %copy-done.36, bf16[192,1792]{1,0:T(8,128)(2,1)S(1)} %copy-done.35, bf16[192,1024]{1,0:T(8,128)(2,1)S(1)} %copy-done.51, ...), kind=kOutput, calls=%fused_computation.3 | convolution fusion | flops 2837708800 | bytes 7995392 | tf_op jit(solution)/shard_map/dot_general | solution.py:26
  169.7 6.9 %collective-permute-done.29 = bf16[64,3712]{1,0:T(8,128)(2,1)S(1)} collective-permute-done((bf16[64,3712]{1,0:T(8,128)(2,1)S(1)}, bf16[64,3712]{1,0:T(8,128)(2,1)S(1)}, u32[]{:S(2)}, u32[]{:S(2)}) %collective-permute-start.29) | collective-permute-done | bytes 475168 | tf_op jit(solution)/shard_map/ppermute | solution.py:92
  177.4 1.5 collective-permute-start.32
  179.6 4.5 %fusion.2 = bf16[1,1792,1024]{2,1,0:T(8,128)(2,1)} fusion(bf16[768,1792]{1,0:T(8,128)(2,1)S(1)} %constant_dynamic-update-slice_fusion, bf16[192,1024]{1,0:T(8,128)(2,1)S(1)} %copy-done.50, bf16[192,1024]{1,0:T(8,128)(2,1)S(1)} %copy-done.47, bf16[192,1024]{1,0:T(8,128)(2,1)S(1)} %copy-done.44, bf16[192,1024]{1,0:T(8,128)(2,1)S(1)} %copy-done.41), kind=kOutput, calls=%fused_computation.5 | convolution fusion | flops 2826698752 | bytes 7995392 | tf_op jit(solution)/shard_map/dot_general | solution.py:26
  184.2 4.5 %fusion.1 = bf16[1,1792,1024]{2,1,0:T(8,128)(2,1)} fusion(bf16[768,1792]{1,0:T(8,128)(2,1)S(1)} %constant_dynamic-update-slice_fusion, bf16[192,1024]{1,0:T(8,128)(2,1)S(1)} %copy-done.49, bf16[192,1024]{1,0:T(8,128)(2,1)S(1)} %copy-done.46, bf16[192,1024]{1,0:T(8,128)(2,1)S(1)} %copy-done.43, bf16[192,1024]{1,0:T(8,128)(2,1)S(1)} %copy-done.40), kind=kOutput, calls=%fused_computation.4 | convolution fusion | flops 2826698752 | bytes 7995392 | tf_op jit(solution)/shard_map/dot_general | solution.py:26
  189.4 5.4 %collective-permute-done.27 = bf16[64,3712]{1,0:T(8,128)(2,1)S(1)} collective-permute-done((bf16[64,3712]{1,0:T(8,128)(2,1)S(1)}, bf16[64,3712]{1,0:T(8,128)(2,1)S(1)}, u32[]{:S(2)}, u32[]{:S(2)}) %collective-permute-start.27) | collective-permute-done | bytes 475168 | tf_op jit(solution)/shard_map/ppermute | solution.py:92
  195.1 1.5 collective-permute-start.33
  196.6 6.2 %collective-permute-done.33 = bf16[32,3712]{1,0:T(8,128)(2,1)S(1)} collective-permute-done((bf16[32,3712]{1,0:T(8,128)(2,1)S(1)}, bf16[32,3712]{1,0:T(8,128)(2,1)S(1)}, u32[]{:S(2)}, u32[]{:S(2)}) %collective-permute-start.33) | collective-permute-done | bytes 237600 | tf_op jit(solution)/shard_map/ppermute | solution.py:31
  (182 shorter events, 16.7 us)
Async XLA Ops:
  2.9 8.8 %collective-permute-start = (bf16[32,3712]{1,0:T(8,128)(2,1)S(1)}, bf16[32,3712]{1,0:T(8,128)(2,1)S(1)}, u32[]{:S(2)}, u32[]{:S(2)}) collective-permute-start(bf16[32,3712]{1,0:T(8,128)(2,1)S(1)} %broadcast_select_fusion.5), channel_id=1, source_target_pairs={{0,16},{16,0},{1,17},{17,1},{2,18},{18,2},{3,19},{19,3},{4,20},{20... | collective-permute-start | bytes 712712 | tf_op jit(solution)/shard_map/ppermute | solution.py:31
  11.8 18.6 %copy-start.1 = (bf16[64,3712]{1,0:T(8,128)(2,1)}, bf16[64,3712]{1,0:T(8,128)(2,1)S(1)}, u32[]{:S(2)}) copy-start(bf16[64,3712]{1,0:T(8,128)(2,1)S(1)} %pad_maximum_fusion.refs_3_) | copy-start | bytes 1425412
  13.0 13.9 %collective-permute-start.2 = (bf16[64,3712]{1,0:T(8,128)(2,1)S(1)}, bf16[64,3712]{1,0:T(8,128)(2,1)S(1)}, u32[]{:S(2)}, u32[]{:S(2)}) collective-permute-start(bf16[64,3712]{1,0:T(8,128)(2,1)S(1)} %pad_maximum_fusion.refs_3_), channel_id=1, source_target_pairs={{0,4},{1,5},{2,6},{3,7},{4,8},{5,9},{6,10},{7,11},{8,12},{9,13},{1... | collective-permute-start | bytes 1425416 | tf_op jit(solution)/shard_map/ppermute | solution.py:92
  14.8 12.0 %collective-permute-start.1 = (bf16[64,3712]{1,0:T(8,128)(2,1)S(1)}, bf16[64,3712]{1,0:T(8,128)(2,1)S(1)}, u32[]{:S(2)}, u32[]{:S(2)}) collective-permute-start(bf16[64,3712]{1,0:T(8,128)(2,1)S(1)} %pad_maximum_fusion.refs_3_), channel_id=1, source_target_pairs={{0,2},{1,3},{2,0},{3,1},{4,6},{5,7},{6,4},{7,5},{8,10},{9,11},{10,... | collective-permute-start | bytes 1425416 | tf_op jit(solution)/shard_map/ppermute | solution.py:92
  16.4 14.1 %collective-permute-start.4 = (bf16[64,3712]{1,0:T(8,128)(2,1)S(1)}, bf16[64,3712]{1,0:T(8,128)(2,1)S(1)}, u32[]{:S(2)}, u32[]{:S(2)}) collective-permute-start(bf16[64,3712]{1,0:T(8,128)(2,1)S(1)} %pad_maximum_fusion.refs_3_), channel_id=1, source_target_pairs={{0,1},{1,0},{2,3},{3,2},{4,5},{5,4},{6,7},{7,6},{8,9},{9,8},{10,11... | collective-permute-start | bytes 1425416 | tf_op jit(solution)/shard_map/ppermute | solution.py:92
  26.9 14.2 %copy-start.22 = (bf16[64,3712]{1,0:T(8,128)(2,1)}, bf16[64,3712]{1,0:T(8,128)(2,1)S(1)}, u32[]{:S(2)}) copy-start(bf16[64,3712]{1,0:T(8,128)(2,1)S(1)} %collective-permute-done.2.refs_3_) | copy-start | bytes 1425412
  26.9 3.5 %collective-permute-start.5 = (bf16[64,3712]{1,0:T(8,128)(2,1)S(1)}, bf16[64,3712]{1,0:T(8,128)(2,1)S(1)}, u32[]{:S(2)}, u32[]{:S(2)}) collective-permute-start(bf16[64,3712]{1,0:T(8,128)(2,1)S(1)} %collective-permute-done.1.refs_4_), channel_id=1, source_target_pairs={{0,1},{1,0},{2,3},{3,2},{4,5},{5,4},{6,7},{7,6},{8,9},{9,8},{10,11... | collective-permute-start | bytes 1425416 | tf_op jit(solution)/shard_map/ppermute | solution.py:92
  26.9 14.1 %collective-permute-start.3 = (bf16[64,3712]{1,0:T(8,128)(2,1)S(1)}, bf16[64,3712]{1,0:T(8,128)(2,1)S(1)}, u32[]{:S(2)}, u32[]{:S(2)}) collective-permute-start(bf16[64,3712]{1,0:T(8,128)(2,1)S(1)} %collective-permute-done.2.refs_3_), channel_id=1, source_target_pairs={{0,2},{1,3},{2,0},{3,1},{4,6},{5,7},{6,4},{7,5},{8,10},{9,11},{10,... | collective-permute-start | bytes 1425416 | tf_op jit(solution)/shard_map/ppermute | solution.py:92
  28.5 24.0 %collective-permute-start.8 = (bf16[64,3712]{1,0:T(8,128)(2,1)S(1)}, bf16[64,3712]{1,0:T(8,128)(2,1)S(1)}, u32[]{:S(2)}, u32[]{:S(2)}) collective-permute-start(bf16[64,3712]{1,0:T(8,128)(2,1)S(1)} %pad_maximum_fusion.refs_3_), channel_id=1, source_target_pairs={{0,8},{1,9},{2,10},{3,11},{4,12},{5,13},{6,14},{7,15},{8,0},{9,1},... | collective-permute-start | bytes 1425416 | tf_op jit(solution)/shard_map/ppermute | solution.py:92
  41.1 13.8 %copy-start.23 = (bf16[64,3712]{1,0:T(8,128)(2,1)}, bf16[64,3712]{1,0:T(8,128)(2,1)S(1)}, u32[]{:S(2)}) copy-start(bf16[64,3712]{1,0:T(8,128)(2,1)S(1)} %collective-permute-done.3.refs_4_) | copy-start | bytes 1425412
  41.1 11.5 %collective-permute-start.6 = (bf16[64,3712]{1,0:T(8,128)(2,1)S(1)}, bf16[64,3712]{1,0:T(8,128)(2,1)S(1)}, u32[]{:S(2)}, u32[]{:S(2)}) collective-permute-start(bf16[64,3712]{1,0:T(8,128)(2,1)S(1)} %collective-permute-done.2.refs_3_), channel_id=1, source_target_pairs={{0,1},{1,0},{2,3},{3,2},{4,5},{5,4},{6,7},{7,6},{8,9},{9,8},{10,11... | collective-permute-start | bytes 1425416 | tf_op jit(solution)/shard_map/ppermute | solution.py:92
  41.2 11.4 %collective-permute-start.7 = (bf16[64,3712]{1,0:T(8,128)(2,1)S(1)}, bf16[64,3712]{1,0:T(8,128)(2,1)S(1)}, u32[]{:S(2)}, u32[]{:S(2)}) collective-permute-start(bf16[64,3712]{1,0:T(8,128)(2,1)S(1)} %collective-permute-done.3.refs_4_), channel_id=1, source_target_pairs={{0,1},{1,0},{2,3},{3,2},{4,5},{5,4},{6,7},{7,6},{8,9},{9,8},{10,11... | collective-permute-start | bytes 1425416 | tf_op jit(solution)/shard_map/ppermute | solution.py:92
  41.7 29.0 %collective-permute-start.12 = (bf16[3,192,1024]{2,1,0:T(8,128)(2,1)}, bf16[3,192,1024]{2,1,0:T(8,128)(2,1)S(1)}, u32[]{:S(2)}, u32[]{:S(2)}) collective-permute-start(bf16[3,192,1024]{2,1,0:T(8,128)(2,1)} %get-tuple-element.171), channel_id=1, source_target_pairs={{0,16},{16,0},{1,17},{17,1},{2,18},{18,2},{3,19},{19,3},{4,20},{20... | collective-permute-start | bytes 3538952 | tf_op jit(solution)/shard_map/ppermute | solution.py:31
  52.5 13.6 %copy-start.15 = (bf16[64,3712]{1,0:T(8,128)(2,1)}, bf16[64,3712]{1,0:T(8,128)(2,1)S(1)}, u32[]{:S(2)}) copy-start(bf16[64,3712]{1,0:T(8,128)(2,1)S(1)} %collective-permute-done.8.refs_3_) | copy-start | bytes 1425412
  52.6 13.5 %collective-permute-start.13 = (bf16[64,3712]{1,0:T(8,128)(2,1)S(1)}, bf16[64,3712]{1,0:T(8,128)(2,1)S(1)}, u32[]{:S(2)}, u32[]{:S(2)}) collective-permute-start(bf16[64,3712]{1,0:T(8,128)(2,1)S(1)} %collective-permute-done.8.refs_3_), channel_id=1, source_target_pairs={{0,2},{1,3},{2,0},{3,1},{4,6},{5,7},{6,4},{7,5},{8,10},{9,11},{10,... | collective-permute-start | bytes 1425416 | tf_op jit(solution)/shard_map/ppermute | solution.py:92
  53.2 13.5 %collective-permute-start.10 = (bf16[64,3712]{1,0:T(8,128)(2,1)}, bf16[64,3712]{1,0:T(8,128)(2,1)S(1)}, u32[]{:S(2)}, u32[]{:S(2)}) collective-permute-start(bf16[64,3712]{1,0:T(8,128)(2,1)} %copy-done.1), channel_id=1, source_target_pairs={{0,12},{1,13},{2,14},{3,15},{4,0},{5,1},{6,2},{7,3},{8,4},{9,5},{1... | collective-permute-start | bytes 1425416 | tf_op jit(solution)/shard_map/ppermute | solution.py:92
  64.6 31.4 %collective-permute-start.9 = (bf16[3,192,1024]{2,1,0:T(8,128)(2,1)}, bf16[3,192,1024]{2,1,0:T(8,128)(2,1)S(1)}, u32[]{:S(2)}, u32[]{:S(2)}) collective-permute-start(bf16[3,192,1024]{2,1,0:T(8,128)(2,1)} %get-tuple-element.180), channel_id=1, source_target_pairs={{0,16},{16,0},{1,17},{17,1},{2,18},{18,2},{3,19},{19,3},{4,20},{20... | collective-permute-start | bytes 3538952 | tf_op jit(solution)/shard_map/ppermute | solution.py:31
  66.1 4.6 %copy-start.17 = (bf16[64,3712]{1,0:T(8,128)(2,1)}, bf16[64,3712]{1,0:T(8,128)(2,1)S(1)}, u32[]{:S(2)}) copy-start(bf16[64,3712]{1,0:T(8,128)(2,1)S(1)} %collective-permute-done.13.refs_4_) | copy-start | bytes 1425412
  66.1 4.6 %collective-permute-start.14 = (bf16[64,3712]{1,0:T(8,128)(2,1)S(1)}, bf16[64,3712]{1,0:T(8,128)(2,1)S(1)}, u32[]{:S(2)}, u32[]{:S(2)}) collective-permute-start(bf16[64,3712]{1,0:T(8,128)(2,1)S(1)} %collective-permute-done.8.refs_3_), channel_id=1, source_target_pairs={{0,1},{1,0},{2,3},{3,2},{4,5},{5,4},{6,7},{7,6},{8,9},{9,8},{10,11... | collective-permute-start | bytes 1425416 | tf_op jit(solution)/shard_map/ppermute | solution.py:92
  66.2 4.5 %collective-permute-start.15 = (bf16[64,3712]{1,0:T(8,128)(2,1)S(1)}, bf16[64,3712]{1,0:T(8,128)(2,1)S(1)}, u32[]{:S(2)}, u32[]{:S(2)}) collective-permute-start(bf16[64,3712]{1,0:T(8,128)(2,1)S(1)} %collective-permute-done.13.refs_4_), channel_id=1, source_target_pairs={{0,1},{1,0},{2,3},{3,2},{4,5},{5,4},{6,7},{7,6},{8,9},{9,8},{10,11... | collective-permute-start | bytes 1425416 | tf_op jit(solution)/shard_map/ppermute | solution.py:92
  66.7 21.9 %copy-start.14 = (bf16[64,3712]{1,0:T(8,128)(2,1)}, bf16[64,3712]{1,0:T(8,128)(2,1)S(1)}, u32[]{:S(2)}) copy-start(bf16[64,3712]{1,0:T(8,128)(2,1)S(1)} %collective-permute-done.10.refs_3_) | copy-start | bytes 1425412
  66.7 21.9 %collective-permute-start.11 = (bf16[64,3712]{1,0:T(8,128)(2,1)S(1)}, bf16[64,3712]{1,0:T(8,128)(2,1)S(1)}, u32[]{:S(2)}, u32[]{:S(2)}) collective-permute-start(bf16[64,3712]{1,0:T(8,128)(2,1)S(1)} %collective-permute-done.10.refs_3_), channel_id=1, source_target_pairs={{0,2},{1,3},{2,0},{3,1},{4,6},{5,7},{6,4},{7,5},{8,10},{9,11},{10,... | collective-permute-start | bytes 1425416 | tf_op jit(solution)/shard_map/ppermute | solution.py:92
  87.1 34.2 %collective-permute-start.22 = (bf16[3,192,1024]{2,1,0:T(8,128)(2,1)}, bf16[3,192,1024]{2,1,0:T(8,128)(2,1)S(1)}, u32[]{:S(2)}, u32[]{:S(2)}) collective-permute-start(bf16[3,192,1024]{2,1,0:T(8,128)(2,1)} %get-tuple-element.196), channel_id=1, source_target_pairs={{0,16},{16,0},{1,17},{17,1},{2,18},{18,2},{3,19},{19,3},{4,20},{20... | collective-permute-start | bytes 3538952 | tf_op jit(solution)/shard_map/ppermute | solution.py:31
  88.6 7.4 %copy-start.16 = (bf16[64,3712]{1,0:T(8,128)(2,1)}, bf16[64,3712]{1,0:T(8,128)(2,1)S(1)}, u32[]{:S(2)}) copy-start(bf16[64,3712]{1,0:T(8,128)(2,1)S(1)} %collective-permute-done.11.refs_4_) | copy-start | bytes 1425412
  88.6 7.4 %collective-permute-start.16 = (bf16[64,3712]{1,0:T(8,128)(2,1)S(1)}, bf16[64,3712]{1,0:T(8,128)(2,1)S(1)}, u32[]{:S(2)}, u32[]{:S(2)}) collective-permute-start(bf16[64,3712]{1,0:T(8,128)(2,1)S(1)} %collective-permute-done.10.refs_3_), channel_id=1, source_target_pairs={{0,1},{1,0},{2,3},{3,2},{4,5},{5,4},{6,7},{7,6},{8,9},{9,8},{10,11... | collective-permute-start | bytes 1425416 | tf_op jit(solution)/shard_map/ppermute | solution.py:92
  88.7 7.3 %collective-permute-start.17 = (bf16[64,3712]{1,0:T(8,128)(2,1)S(1)}, bf16[64,3712]{1,0:T(8,128)(2,1)S(1)}, u32[]{:S(2)}, u32[]{:S(2)}) collective-permute-start(bf16[64,3712]{1,0:T(8,128)(2,1)S(1)} %collective-permute-done.11.refs_4_), channel_id=1, source_target_pairs={{0,1},{1,0},{2,3},{3,2},{4,5},{5,4},{6,7},{7,6},{8,9},{9,8},{10,11... | collective-permute-start | bytes 1425416 | tf_op jit(solution)/shard_map/ppermute | solution.py:92
  112.3 33.4 %collective-permute-start.21 = (bf16[3,192,1024]{2,1,0:T(8,128)(2,1)}, bf16[3,192,1024]{2,1,0:T(8,128)(2,1)S(1)}, u32[]{:S(2)}, u32[]{:S(2)}) collective-permute-start(bf16[3,192,1024]{2,1,0:T(8,128)(2,1)} %get-tuple-element.214), channel_id=1, source_target_pairs={{0,16},{16,0},{1,17},{17,1},{2,18},{18,2},{3,19},{19,3},{4,20},{20... | collective-permute-start | bytes 3538952 | tf_op jit(solution)/shard_map/ppermute | solution.py:31
  113.9 2.1 collective-permute-start.18
  113.9 2.7 %collective-permute-start.19 = (bf16[64,3712]{1,0:T(8,128)(2,1)}, bf16[64,3712]{1,0:T(8,128)(2,1)S(1)}, u32[]{:S(2)}, u32[]{:S(2)}) collective-permute-start(bf16[64,3712]{1,0:T(8,128)(2,1)} %get-tuple-element.213), channel_id=1, source_target_pairs={{0,1},{1,0},{2,3},{3,2},{4,5},{5,4},{6,7},{7,6},{8,9},{9,8},{10,11... | collective-permute-start | bytes 1425416 | tf_op jit(solution)/shard_map/ppermute | solution.py:92
  122.3 11.4 %copy-start.39 = (bf16[64,3712]{1,0:T(8,128)(2,1)S(1)}, bf16[64,3712]{1,0:T(8,128)(2,1)}, u32[]{:S(2)}) copy-start(bf16[64,3712]{1,0:T(8,128)(2,1)} %get-tuple-element.221) | copy-start | bytes 1425412
  122.3 24.2 %copy-start.6 = (f32[64,3712]{1,0:T(8,128)S(1)}, f32[64,3712]{1,0:T(8,128)}, u32[]{:S(2)}) copy-start(f32[64,3712]{1,0:T(8,128)} %get-tuple-element.240) | copy-start | bytes 2850820
  133.1 2.1 %collective-permute-start.23 = (bf16[64,3712]{1,0:T(8,128)(2,1)}, bf16[64,3712]{1,0:T(8,128)(2,1)S(1)}, u32[]{:S(2)}, u32[]{:S(2)}) collective-permute-start(bf16[64,3712]{1,0:T(8,128)(2,1)} %get-tuple-element.230), channel_id=1, source_target_pairs={{0,1},{1,0},{2,3},{3,2},{4,5},{5,4},{6,7},{7,6},{8,9},{9,8},{10,11... | collective-permute-start | bytes 1425416 | tf_op jit(solution)/shard_map/ppermute | solution.py:92
  133.1 2.7 %collective-permute-start.24 = (bf16[64,3712]{1,0:T(8,128)(2,1)}, bf16[64,3712]{1,0:T(8,128)(2,1)S(1)}, u32[]{:S(2)}, u32[]{:S(2)}) collective-permute-start(bf16[64,3712]{1,0:T(8,128)(2,1)} %get-tuple-element.232), channel_id=1, source_target_pairs={{0,1},{1,0},{2,3},{3,2},{4,5},{5,4},{6,7},{7,6},{8,9},{9,8},{10,11... | collective-permute-start | bytes 1425416 | tf_op jit(solution)/shard_map/ppermute | solution.py:92
  133.6 12.9 %collective-permute-start.20 = (bf16[64,3712]{1,0:T(8,128)(2,1)S(1)}, bf16[64,3712]{1,0:T(8,128)(2,1)S(1)}, u32[]{:S(2)}, u32[]{:S(2)}) collective-permute-start(bf16[64,3712]{1,0:T(8,128)(2,1)S(1)} %copy-done.39), channel_id=1, source_target_pairs={{0,2},{1,3},{2,0},{3,1},{4,6},{5,7},{6,4},{7,5},{8,10},{9,11},{10,... | collective-permute-start | bytes 1425416 | tf_op jit(solution)/shard_map/ppermute | solution.py:92
  146.6 14.0 %collective-permute-start.25 = (bf16[64,3712]{1,0:T(8,128)(2,1)S(1)}, bf16[64,3712]{1,0:T(8,128)(2,1)S(1)}, u32[]{:S(2)}, u32[]{:S(2)}) collective-permute-start(bf16[64,3712]{1,0:T(8,128)(2,1)S(1)} %add_convert_fusion.3), channel_id=1, source_target_pairs={{0,12},{1,13},{2,14},{3,15},{4,0},{5,1},{6,2},{7,3},{8,4},{9,5},{1... | collective-permute-start | bytes 1425416 | tf_op jit(solution)/shard_map/ppermute | solution.py:92
  148.2 12.4 %collective-permute-start.26 = (bf16[64,3712]{1,0:T(8,128)(2,1)}, bf16[64,3712]{1,0:T(8,128)(2,1)S(1)}, u32[]{:S(2)}, u32[]{:S(2)}) collective-permute-start(bf16[64,3712]{1,0:T(8,128)(2,1)} %get-tuple-element.251), channel_id=1, source_target_pairs={{0,2},{1,3},{2,0},{3,1},{4,6},{5,7},{6,4},{7,5},{8,10},{9,11},{10,... | collective-permute-start | bytes 1425416 | tf_op jit(solution)/shard_map/ppermute | solution.py:92
  149.2 10.9 %copy-start.34 = (bf16[128,3712]{1,0:T(8,128)(2,1)S(1)}, bf16[128,3712]{1,0:T(8,128)(2,1)}, u32[]{:S(2)}) copy-start(bf16[128,3712]{1,0:T(8,128)(2,1)} %get-tuple-element.198) | copy-start | bytes 2850820
  149.2 11.5 %copy-start.7 = (f32[64,3712]{1,0:T(8,128)S(1)}, f32[64,3712]{1,0:T(8,128)}, u32[]{:S(2)}) copy-start(f32[64,3712]{1,0:T(8,128)} %get-tuple-element.252) | copy-start | bytes 2850820
  160.0 3.3 %collective-permute-start.28 = (bf16[128,3712]{1,0:T(8,128)(2,1)}, bf16[128,3712]{1,0:T(8,128)(2,1)S(1)}, u32[]{:S(2)}, u32[]{:S(2)}) collective-permute-start(bf16[128,3712]{1,0:T(8,128)(2,1)} %get-tuple-element.249), channel_id=1, source_target_pairs={{0,1},{1,0},{2,3},{3,2},{4,5},{5,4},{6,7},{7,6},{8,9},{9,8},{10,11... | collective-permute-start | bytes 2850824 | tf_op jit(solution)/shard_map/ppermute | solution.py:92
  160.1 16.6 %collective-permute-start.31 = (bf16[128,3712]{1,0:T(8,128)(2,1)S(1)}, bf16[128,3712]{1,0:T(8,128)(2,1)S(1)}, u32[]{:S(2)}, u32[]{:S(2)}) collective-permute-start(bf16[128,3712]{1,0:T(8,128)(2,1)S(1)} %copy-done.34), channel_id=1, source_target_pairs={{0,1},{1,0},{2,3},{3,2},{4,5},{5,4},{6,7},{7,6},{8,9},{9,8},{10,11... | collective-permute-start | bytes 2850824 | tf_op jit(solution)/shard_map/ppermute | solution.py:92
  160.9 33.9 %collective-permute-start.27 = (bf16[64,3712]{1,0:T(8,128)(2,1)S(1)}, bf16[64,3712]{1,0:T(8,128)(2,1)S(1)}, u32[]{:S(2)}, u32[]{:S(2)}) collective-permute-start(bf16[64,3712]{1,0:T(8,128)(2,1)S(1)} %add_convert_fusion.2), channel_id=1, source_target_pairs={{0,8},{1,9},{2,10},{3,11},{4,12},{5,13},{6,14},{7,15},{8,0},{9,1},... | collective-permute-start | bytes 1425416 | tf_op jit(solution)/shard_map/ppermute | solution.py:92
  163.6 13.1 %copy-start.8 = (bf16[128,3712]{1,0:T(8,128)(2,1)S(1)}, bf16[128,3712]{1,0:T(8,128)(2,1)}, u32[]{:S(2)}) copy-start(bf16[128,3712]{1,0:T(8,128)(2,1)} %get-tuple-element.275) | copy-start | bytes 2850820
  163.6 13.0 %collective-permute-start.29 = (bf16[64,3712]{1,0:T(8,128)(2,1)S(1)}, bf16[64,3712]{1,0:T(8,128)(2,1)S(1)}, u32[]{:S(2)}, u32[]{:S(2)}) collective-permute-start(bf16[64,3712]{1,0:T(8,128)(2,1)S(1)} %slice.119), channel_id=1, source_target_pairs={{0,2},{1,3},{2,0},{3,1},{4,6},{5,7},{6,4},{7,5},{8,10},{9,11},{10,... | collective-permute-start | bytes 1425416 | tf_op jit(solution)/shard_map/ppermute | solution.py:92
  177.0 17.8 %collective-permute-start.30 = (bf16[64,3712]{1,0:T(8,128)(2,1)S(1)}, bf16[64,3712]{1,0:T(8,128)(2,1)S(1)}, u32[]{:S(2)}, u32[]{:S(2)}) collective-permute-start(bf16[64,3712]{1,0:T(8,128)(2,1)S(1)} %add_convert_fusion.1), channel_id=1, source_target_pairs={{0,4},{1,5},{2,6},{3,7},{4,8},{5,9},{6,10},{7,11},{8,12},{9,13},{1... | collective-permute-start | bytes 1425416 | tf_op jit(solution)/shard_map/ppermute | solution.py:92
  177.4 11.9 %collective-permute-start.32 = (bf16[64,3712]{1,0:T(8,128)(2,1)S(1)}, bf16[64,3712]{1,0:T(8,128)(2,1)S(1)}, u32[]{:S(2)}, u32[]{:S(2)}) collective-permute-start(bf16[64,3712]{1,0:T(8,128)(2,1)S(1)} %slice.118), channel_id=1, source_target_pairs={{0,2},{1,3},{2,0},{3,1},{4,6},{5,7},{6,4},{7,5},{8,10},{9,11},{10,... | collective-permute-start | bytes 1425416 | tf_op jit(solution)/shard_map/ppermute | solution.py:92
  184.2 5.1 %slice-start = ((f32[128,3712]{1,0:T(8,128)}), f32[64,3712]{1,0:T(8,128)S(1)}, s32[]{:S(2)}) async-start(f32[128,3712]{1,0:T(8,128)} %copy-done), calls=%async_computation | async-start | bytes 1900544 | tf_op jit(solution)/shard_map/slice | solution.py:183
  189.4 13.7 %copy-start.33 = (s32[32,8]{0,1:T(8,128)S(1)}, s32[32,8]{0,1:T(8,128)}, u32[]{:S(2)}) copy-start(s32[32,8]{0,1:T(8,128)} %param.8) | copy-start | bytes 3076
  195.1 7.8 %collective-permute-start.33 = (bf16[32,3712]{1,0:T(8,128)(2,1)S(1)}, bf16[32,3712]{1,0:T(8,128)(2,1)S(1)}, u32[]{:S(2)}, u32[]{:S(2)}) collective-permute-start(bf16[32,3712]{1,0:T(8,128)(2,1)S(1)} %broadcast_select_fusion.4), channel_id=1, source_target_pairs={{0,16},{16,0},{1,17},{17,1},{2,18},{18,2},{3,19},{19,3},{4,20},{20... | collective-permute-start | bytes 712712 | tf_op jit(solution)/shard_map/ppermute | solution.py:31
  (39 other events, 96.6 us)

commit v2 on v1

--- a/solution.py
+++ b/solution.py
@@ -1,5 +1,6 @@
 import jax
 import jax.numpy as jnp
+import numpy as np
 from jax import lax
 from jax.experimental import pallas as pl
 from jax.experimental.pallas import tpu as pltpu
@@ -92,6 +93,18 @@
     return lax.ppermute(value, "expert", pairs)
 
 
+def shift_to_owner(value, dp_step, outer_step):
+    groups, experts = lax.axis_size("dp"), lax.axis_size("expert")
+    outer, inner, core = factors(experts)
+    pairs = []
+    for group in range(groups):
+        for source in range(experts):
+            place = source // (inner * core)
+            target = source + ((place + outer_step) % outer - place) * inner * core
+            pairs.append((group * experts + source, (group + dp_step) % groups * experts + target))
+    return lax.ppermute(value, ("dp", "expert"), pairs)
+
+
 def level_size(level):
     return factors(lax.axis_size("expert"))[level]
 
@@ -111,7 +124,7 @@
     return jnp.concatenate(values, axis=0) if len(values) > 1 else values[0]
 
 
-def project_body(number_parts, part, *refs):
+def project_body(number_parts, part, experts, *refs):
     mask_ref, order_ref, base_ref = refs[:3]
     part_refs = refs[3 : 3 + number_parts]
     gate_ref, up_ref, down_ref = refs[3 + number_parts : 6 + number_parts]
@@ -122,7 +135,12 @@
         slots = x_ref.shape[0]
         arrived = stacked_rows([ref[...] for ref in part_refs])
         count = arrived.shape[0]
-        mask = mask_ref[...]
+        column = lax.broadcasted_iota(jnp.int32, (8, arrived.shape[1] - 2 * part), 1)
+        expert = mask_ref[0, 0]
+        mask = jnp.zeros(column.shape, F32)
+        for number in range(3):
+            mask = mask + jnp.where(column == number * experts + expert, 1.0, 0.0)
+        mask = mask.astype(BF)
         weight = dot_nt(mask, arrived[:, 2 * part :])
         live = weight > 0.0
         place = dot_nn(jnp.where(live, 1.0, 0.0).astype(BF), order_ref[...])
@@ -150,6 +168,7 @@
 
 
 def project(parts, mask, order, base, slots, gate_w, up_w, down_w):
+    experts = lax.axis_size("expert")
     part, hidden = gate_w.shape
     tile = min(256, hidden)
     count = sum(value.shape[0] for value in parts)
@@ -158,9 +177,9 @@
     stacked = pl.BlockSpec((3, slots, tile), lambda j: (0, 0, j))
     row_out = jax.ShapeDtypeStruct((slots, part), BF)
     return pl.pallas_call(
-        lambda *refs: project_body(len(parts), part, *refs),
+        lambda *refs: project_body(len(parts), part, experts, *refs),
         grid=(hidden // tile,),
-        in_specs=[whole(mask.shape), whole(order.shape), whole(base.shape)]
+        in_specs=[pl.BlockSpec(memory_space=pltpu.SMEM), whole(order.shape), whole(base.shape)]
         + [whole(value.shape) for value in parts]
         + [columns(part), columns(part), pl.BlockSpec((tile, part), lambda j: (j, 0))],
         out_specs=[whole((slots, part))] * 3
@@ -289,6 +308,7 @@
 
 def finish_and_project(left, parts, mask, order, base, slots, gate_w, up_w, down_w, number_parts):
     own, sent, grad, weight, pick, route = left
+    experts = lax.axis_size("expert")
     part, hidden = gate_w.shape
     tile = min(256, hidden)
     count = sum(value.shape[0] for value in parts)
@@ -305,12 +325,13 @@
         outs = refs[weights : weights + 7]
         ends = refs[weights + 7 :]
         finish_body(len(sent), number_parts, *refs[first:weights], *ends)
-        project_body(len(parts), part, *refs[:first], *refs[second:weights], *outs)
+        project_body(len(parts), part, experts, *refs[:first], *refs[second:weights], *outs)
 
     results = pl.pallas_call(
         body,
         grid=(hidden // tile,),
-        in_specs=[whole(value.shape) for value in (mask, order, base, *parts)]
+        in_specs=[pl.BlockSpec(memory_space=pltpu.SMEM)]
+        + [whole(value.shape) for value in (order, base, *parts)]
         + [stacked] * (1 + len(sent))
         + [whole(value.shape) for value in (grad, weight, pick, route)]
         + [columns(part), columns(part), pl.BlockSpec((tile, part), lambda j: (j, 0))],
@@ -338,6 +359,7 @@
     experts = lax.axis_size("expert")
     groups = lax.axis_size("dp")
     my_expert = lax.axis_index("expert")
+    mine_dp = lax.axis_index("dp")
     outer, inner, core = factors(experts)
     rows, width = tokens.shape
     hidden_width = gate_weight.shape[2]
@@ -370,9 +392,6 @@
     )
 
     column = jnp.arange(extra, dtype=jnp.int32)[None, :]
-    mask = jnp.broadcast_to(
-        (column % experts == my_expert) & (column < 3 * experts), (8, extra)
-    ).astype(BF)
     route_cols = (
         column == jnp.arange(8, dtype=jnp.int32)[:, None] * experts + my_expert
     ) & (jnp.arange(8)[:, None] < 3)
@@ -380,10 +399,15 @@
     last = outer - 1
     count = inner * core * groups * rows
     slots = inner * core * groups * most
-    token = jnp.arange(count, dtype=jnp.int32)
+    token = np.arange(count)
     block = token // rows
     before = (block[:, None] == block[None, :]) & (token[:, None] <= token[None, :])
-    tables = (mask, before.astype(BF), jnp.broadcast_to((block * most).astype(F32)[None], (8, count)))
+    base = np.tile((block * most).astype(np.float32)[None], (8, 1))
+    tables = (
+        my_expert.astype(jnp.int32).reshape(1, 1),
+        jnp.asarray(before.astype(np.float32), BF),
+        jnp.asarray(base),
+    )
     order = Order()
     pieces, along, around, picked, sums, ends = {0: payload}, {}, {}, {}, {}, {}
     moving, finals, held = {}, {}, {}
@@ -493,6 +517,15 @@
     def next_outer(number):
         mine, arrived = order.enter(*moving[number])
         (total,) = merge([mine] + arrived, 1)
+        if number and number == last:
+            total = total.astype(BF)
+            order.leave(total)
+            parts = [total[g * rows : (g + 1) * rows] for g in range(groups)]
+            finals[number] = [
+                shift_to_owner(choose(parts, (mine_dp + step) % groups), step, -number)
+                for step in range(groups)
+            ]
+            return
         if number:
             total = total.astype(BF)
         order.leave(total)
@@ -547,18 +580,28 @@
     if last:
         next_inner(0)
         start_back(0)
-    x_all, gate_all, up_all = order.enter(
-        rows_of(picked, 0), rows_of(ends, 1), rows_of(ends, 2)
-    )
+    x_all, gate_all = order.enter(rows_of(picked, 0), rows_of(ends, 1))
     x_all = joined(x_all)
     gate_grad = dot_tn(x_all, joined(gate_all)).astype(BF)[None]
-    up_grad = dot_tn(x_all, joined(up_all)).astype(BF)[None]
-    order.leave(gate_grad, up_grad)
+    order.leave(gate_grad)
     if last:
         next_outer(0)
+    straight = finals.pop(last) if last else None
     (arrived,) = order.enter(list(finals.values()))
-    final = add_all(arrived[0].astype(F32), arrived[1:]).astype(BF)
-    parts = swap_groups([final[g * rows : (g + 1) * rows] for g in range(groups)])
+    total = add_all(arrived[0].astype(F32), arrived[1:])
+    sums_here = [total[g * rows : (g + 1) * rows] for g in range(groups)]
+    by_step = [choose(sums_here, mine_dp)]
+    for step in range(1, groups):
+        by_step.append(shift_dp(choose(sums_here, (mine_dp + step) % groups).astype(BF), step))
+    order.leave(total)
+    x_all, up_all = order.enter(x_all, rows_of(ends, 2))
+    up_grad = dot_tn(x_all, joined(up_all)).astype(BF)[None]
+    order.leave(up_grad)
+    if last:
+        by_step, straight = order.enter(by_step, straight)
+        by_step = [value.astype(F32) + add.astype(F32) for value, add in zip(by_step, straight)]
+    by_step = [value.astype(BF) for value in by_step]
+    parts = [choose(by_step, (mine_dp - g) % groups) for g in range(groups)]
     mixed = jnp.concatenate([value[:, :part] for value in parts], axis=1)
     tokens_grad = jnp.concatenate([value[:, part + extra :] for value in parts], axis=1)
     route_table = jnp.zeros((), F32)

time: 205 us -> 204 us (level)
    ppermute x6, waiting for transfers between devices: 27.4 us -> 23.5 us  [shift_dp(): lax.ppermute(value, 'dp', [(i, (i + step) % groups) for i in range(groups)])]
    ppermute x28 -> x27, waiting for transfers between devices: 39.1 us -> 42.7 us  [shift_expert(): return lax.ppermute(value, 'expert', pairs)]
    ppermute x0 -> x2, starting transfers between devices: none -> 2.25 us  [shift_to_owner(): return lax.ppermute(value, ('dp', 'expert'), pairs)]
    ppermute x28 -> x27, starting transfers between devices: 20.9 us -> 20 us  [shift_expert(): return lax.ppermute(value, 'expert', pairs)]
  transfers between devices with their start and end apart: 34 -> 35, of which waited for: 17 -> 17; matrix products, arithmetic and copies ran while one was open for 8% -> 8% of each run, Pallas kernels for 37% -> 37%
where the time goes in v2:
time: 204 us
  Pallas kernels  76.3 us (37%)
  waiting for transfers between devices  66.3 us (32%)
  starting transfers between devices  33 us (16%)
  matrix products  14 us (7%)
  local copies, waits for them, and re-layouts  8.2 us (4%)
  other arithmetic  4.88 us (2%)
    ppermute x27, waiting for transfers between devices, shift_expert(): return lax.ppermute(value, 'expert', pairs)  42.7 us
    pallas_call x2, Pallas kernels, finish_and_project(): pl.pallas_call(body, grid=(hidden // tile,), in_specs=[pl.BlockSpec(memor...  30.1 us
    ppermute x6, waiting for transfers between devices, shift_dp(): lax.ppermute(value, 'dp', [(i, (i + step) % groups) for i in range(groups)])  23.5 us
    pallas_call x2, Pallas kernels, finish(): pl.pallas_call(lambda *refs: finish_body(len(sent), number_parts, *refs),...  21.6 us
    ppermute x27, starting transfers between devices, shift_expert(): return lax.ppermute(value, 'expert', pairs)  20 us
    pallas_call x2, Pallas kernels, project(): pl.pallas_call(lambda *refs: project_body(len(parts), part, experts, *ref...  19.3 us
    dot_general x3, matrix products, dot_tn(): lax.dot_general(first, second, (((0,), (0,)), ((), ())), preferred_elemen...  14 us
    ppermute x6, starting transfers between devices, shift_dp(): lax.ppermute(value, 'dp', [(i, (i + step) % groups) for i in range(groups)])  10.7 us
  transfers between devices with their start and end apart: 35, of which 17 were waited for; matrix products, arithmetic and copies ran while one was open for 8% of the time, Pallas kernels for 37%

profile of v2, /device:TPU:0, one launch (start us, length us, event | category | flops | bytes accessed | tf_op | source)
XLA Modules:
  0.0 204.0 jit_solution(17953827548319272734)
XLA Ops:
  1.5 1.1 fusion.39
  2.9 3.0 %collective-permute-start = (bf16[32,3712]{1,0:T(8,128)(2,1)S(1)}, bf16[32,3712]{1,0:T(8,128)(2,1)S(1)}, u32[]{:S(2)}, u32[]{:S(2)}) collective-permute-start(bf16[32,3712]{1,0:T(8,128)(2,1)S(1)} %broadcast_select_fusion.3), channel_id=1, source_target_pairs={{0,16},{16,0},{1,17},{17,1},{2,18},{18,2},{3,19},{19,3},{4,20},{20... | collective-permute-start | bytes 712712 | tf_op jit(solution)/shard_map/ppermute | solution.py:32
  5.9 5.8 %collective-permute-done = bf16[32,3712]{1,0:T(8,128)(2,1)S(1)} collective-permute-done((bf16[32,3712]{1,0:T(8,128)(2,1)S(1)}, bf16[32,3712]{1,0:T(8,128)(2,1)S(1)}, u32[]{:S(2)}, u32[]{:S(2)}) %collective-permute-start) | collective-permute-done | bytes 237600 | tf_op jit(solution)/shard_map/ppermute | solution.py:32
  11.8 1.9 collective-permute-start.2
  13.7 1.5 collective-permute-start.1
  15.2 10.5 %collective-permute-done.2.refs_3_ = bf16[64,3712]{1,0:T(8,128)(2,1)S(1)} collective-permute-done((bf16[64,3712]{1,0:T(8,128)(2,1)S(1)}, bf16[64,3712]{1,0:T(8,128)(2,1)S(1)}, u32[]{:S(2)}, u32[]{:S(2)}) %collective-permute-start.2) | collective-permute-done | bytes 475168 | tf_op jit(solution)/shard_map/ppermute | solution.py:93
  25.8 1.6 collective-permute-start.3
  27.4 1.9 collective-permute-start.8
  30.3 9.6 %project.2 = (bf16[192,1792]{1,0:T(8,128)(2,1)}, bf16[192,1792]{1,0:T(8,128)(2,1)}, bf16[192,1792]{1,0:T(8,128)(2,1)}, f32[192,128]{1,0:T(8,128)}, bf16[192,256]...) custom-call(s32[1,1]{1,0:T(1,128)} %bitcast.refs_0_, ...), custom_call_target="tpu_custom_call" | custom-call | tf_op jit(solution)/shard_map/project/pallas_call | solution.py:179
  40.5 1.5 collective-permute-start.12
  42.0 9.4 %collective-permute-done.8.refs_3_ = bf16[64,3712]{1,0:T(8,128)(2,1)S(1)} collective-permute-done((bf16[64,3712]{1,0:T(8,128)(2,1)S(1)}, bf16[64,3712]{1,0:T(8,128)(2,1)S(1)}, u32[]{:S(2)}, u32[]{:S(2)}) %collective-permute-start.8) | collective-permute-done | bytes 475168 | tf_op jit(solution)/shard_map/ppermute | solution.py:93
  52.0 1.7 collective-permute-start.10
  53.7 9.7 %project.3 = (bf16[192,1792]{1,0:T(8,128)(2,1)}, bf16[192,1792]{1,0:T(8,128)(2,1)}, bf16[192,1792]{1,0:T(8,128)(2,1)}, f32[192,128]{1,0:T(8,128)}, bf16[192,256]...) custom-call(s32[1,1]{1,0:T(1,128)} %bitcast.refs_0_, ...), custom_call_target="tpu_custom_call" | custom-call | tf_op jit(solution)/shard_map/project/pallas_call | solution.py:179
  63.4 1.5 collective-permute-start.9
  65.5 1.5 collective-permute-start.11
  67.7 1.8 collective-permute-done.12.refs_8_
  69.6 1.0 copy-done.5
  70.9 15.1 %step.2 = (bf16[192,1792]{1,0:T(8,128)(2,1)}, bf16[192,1792]{1,0:T(8,128)(2,1)}, bf16[192,1792]{1,0:T(8,128)(2,1)}, f32[192,128]{1,0:T(8,128)}, bf16[192,256]{1,...) custom-call(s32[1,1]{1,0:T(1,128)} %bitcast.refs_0_, ...), custom_call_target="tpu_custom_call" | custom-call | tf_op jit(solution)/shard_map/step/pallas_call | solution.py:330
  85.9 1.6 collective-permute-start.22
  88.1 6.7 %collective-permute-done.9.refs_8_ = bf16[3,192,1024]{2,1,0:T(8,128)(2,1)S(1)} collective-permute-done((bf16[3,192,1024]{2,1,0:T(8,128)(2,1)}, bf16[3,192,1024]{2,1,0:T(8,128)(2,1)S(1)}, u32[]{:S(2)}, u32[]{:S(2)}) %collective-permute-start.9) | collective-permute-done | bytes 1179680 | tf_op jit(solution)/shard_map/ppermute | solution.py:32
  94.8 1.0 copy-done.4
  96.1 15.1 %step.3 = (bf16[192,1792]{1,0:T(8,128)(2,1)}, bf16[192,1792]{1,0:T(8,128)(2,1)}, bf16[192,1792]{1,0:T(8,128)(2,1)}, f32[192,128]{1,0:T(8,128)}, bf16[192,256]{1,...) custom-call(s32[1,1]{1,0:T(1,128)} %bitcast.refs_0_, ...), custom_call_target="tpu_custom_call" | custom-call | tf_op jit(solution)/shard_map/step/pallas_call | solution.py:330
  111.2 1.6 collective-permute-start.21
  113.3 1.5 collective-permute-done.18.refs_1_
  116.3 2.6 %merge.2 = (f32[64,3712]{1,0:T(8,128)}, bf16[64,3712]{1,0:T(8,128)(2,1)}) custom-call(bf16[64,3712]{1,0:T(8,128)(2,1)} %get-tuple-element.219.refs_0_, bf16[64,3712]{1,0:T(8,128)(2,1)} %copy-done.31, bf16[64,3712]{1,0:T(8,128)(2,1)} %get-tuple-element.221.refs_2_, bf16[64,3712]{1,0:T(8,128)(2,1)} %copy-done.32), custom_call_target="tpu_custom_call" | custom-call | tf_op jit(solution)/shard_map/merge/pallas_call | solution.py:216
  118.9 1.2 collective-permute-done.22.refs_1_
  120.1 1.0 copy-done.3
  121.1 10.8 %finish.2 = (bf16[192,1024]{1,0:T(8,128)(2,1)}, bf16[192,1024]{1,0:T(8,128)(2,1)}, bf16[192,1024]{1,0:T(8,128)(2,1)}, bf16[64,3712]{1,0:T(8,128)(2,1)}, bf16[64,...) custom-call(f32[3,192,1024]{2,1,0:T(8,128)} %get-tuple-element.228.refs_0_, ...), custom_call_target="tpu_custom_call" | custom-call | tf_op jit(solution)/shard_map/finish/pallas_call | solution.py:294
  133.1 0.9 collective-permute-done.23.refs_1_
  135.5 2.7 %merge.3 = (f32[64,3712]{1,0:T(8,128)}, bf16[64,3712]{1,0:T(8,128)(2,1)}) custom-call(bf16[64,3712]{1,0:T(8,128)(2,1)} %get-tuple-element.237.refs_0_, bf16[64,3712]{1,0:T(8,128)(2,1)} %copy-done.29, bf16[64,3712]{1,0:T(8,128)(2,1)} %get-tuple-element.239.refs_2_, bf16[64,3712]{1,0:T(8,128)(2,1)} %copy-done.30), custom_call_target="tpu_custom_call" | custom-call | tf_op jit(solution)/shard_map/merge/pallas_call | solution.py:216
  138.1 6.4 %collective-permute-done.21.refs_1_ = bf16[3,192,1024]{2,1,0:T(8,128)(2,1)S(1)} collective-permute-done((bf16[3,192,1024]{2,1,0:T(8,128)(2,1)}, bf16[3,192,1024]{2,1,0:T(8,128)(2,1)S(1)}, u32[]{:S(2)}, u32[]{:S(2)}) %collective-permute-start.21) | collective-permute-done | bytes 1179680 | tf_op jit(solution)/shard_map/ppermute | solution.py:32
  144.5 0.8 collective-permute-done.20
  145.4 1.6 collective-permute-start.25
  147.0 1.0 collective-permute-start.26
  148.0 10.8 %finish.3 = (bf16[192,1024]{1,0:T(8,128)(2,1)}, bf16[192,1024]{1,0:T(8,128)(2,1)}, bf16[192,1024]{1,0:T(8,128)(2,1)}, bf16[128,3712]{1,0:T(8,128)(2,1)}, bf16[128,3712]{1,0:T(8,128)(2,1)}) custom-call(f32[3,192,1024]{2,1,0:T(8,128)} %get-tuple-element.247.refs_0_, bf16[3,192,1024]{2,1,0:T(8,128)(2,1)} %copy-done.2, ...), custom_call_target="tpu_custom_call" | custom-call | tf_op jit(solution)/shard_map/finish/pallas_call | solution.py:294
  160.4 1.7 collective-permute-done.29
  162.4 1.1 collective-permute-start.30
  163.6 5.0 %fusion = bf16[1,1024,1792]{2,1,0:T(8,128)(2,1)} fusion(bf16[192,1792]{1,0:T(8,128)(2,1)S(1)} %copy-done.38, bf16[192,1792]{1,0:T(8,128)(2,1)S(1)} %copy-done.37, bf16[192,1792]{1,0:T(8,128)(2,1)S(1)} %copy-done.36, bf16[192,1792]{1,0:T(8,128)(2,1)S(1)} %copy-done.35, bf16[192,1024]{1,0:T(8,128)(2,1)S(1)} %copy-done.51, ...), kind=kOutput, calls=%fused_computation.3 | convolution fusion | flops 2837708800 | bytes 7995392 | tf_op jit(solution)/shard_map/dot_general | solution.py:27
  168.6 6.9 %collective-permute-done.30 = bf16[64,3712]{1,0:T(8,128)(2,1)S(1)} collective-permute-done((bf16[64,3712]{1,0:T(8,128)(2,1)S(1)}, bf16[64,3712]{1,0:T(8,128)(2,1)S(1)}, u32[]{:S(2)}, u32[]{:S(2)}) %collective-permute-start.30) | collective-permute-done | bytes 475168 | tf_op jit(solution)/shard_map/ppermute | solution.py:93
  175.9 1.3 collective-permute-start.34
  177.2 1.0 collective-permute-start.33
  178.2 0.9 collective-permute-start.31
  179.4 4.5 %fusion.1 = bf16[1,1792,1024]{2,1,0:T(8,128)(2,1)} fusion(bf16[768,1792]{1,0:T(8,128)(2,1)S(1)} %constant_dynamic-update-slice_fusion, bf16[192,1024]{1,0:T(8,128)(2,1)S(1)} %copy-done.50, bf16[192,1024]{1,0:T(8,128)(2,1)S(1)} %copy-done.47, bf16[192,1024]{1,0:T(8,128)(2,1)S(1)} %copy-done.43, bf16[192,1024]{1,0:T(8,128)(2,1)S(1)} %copy-done.41), kind=kOutput, calls=%fused_computation.4 | convolution fusion | flops 2826698752 | bytes 7995392 | tf_op jit(solution)/shard_map/dot_general | solution.py:27
  183.9 5.8 %collective-permute-done.31 = bf16[64,3712]{1,0:T(8,128)(2,1)S(1)} collective-permute-done((bf16[64,3712]{1,0:T(8,128)(2,1)S(1)}, bf16[64,3712]{1,0:T(8,128)(2,1)S(1)}, u32[]{:S(2)}, u32[]{:S(2)}) %collective-permute-start.31) | collective-permute-done | bytes 475168 | tf_op jit(solution)/shard_map/ppermute | solution.py:93
  189.8 3.8 %collective-permute-done.27 = bf16[64,3712]{1,0:T(8,128)(2,1)S(1)} collective-permute-done((bf16[64,3712]{1,0:T(8,128)(2,1)S(1)}, bf16[64,3712]{1,0:T(8,128)(2,1)S(1)}, u32[]{:S(2)}, u32[]{:S(2)}) %collective-permute-start.27) | collective-permute-done | bytes 475168 | tf_op jit(solution)/shard_map/ppermute | solution.py:93
  193.9 1.6 collective-permute-start.32
  195.5 4.5 %fusion.2 = bf16[1,1792,1024]{2,1,0:T(8,128)(2,1)} fusion(bf16[768,1792]{1,0:T(8,128)(2,1)S(1)} %constant_dynamic-update-slice_fusion, bf16[192,1024]{1,0:T(8,128)(2,1)S(1)} %copy-done.48, bf16[192,1024]{1,0:T(8,128)(2,1)S(1)} %copy-done.45, bf16[192,1024]{1,0:T(8,128)(2,1)S(1)} %copy-done.42, bf16[192,1024]{1,0:T(8,128)(2,1)S(1)} %copy-done.40), kind=kOutput, calls=%fused_computation.5 | convolution fusion | flops 2826698752 | bytes 7995392 | tf_op jit(solution)/shard_map/dot_general | solution.py:27
  200.0 1.7 collective-permute-done.32
  (180 shorter events, 15.7 us)
Async XLA Ops:
  2.9 8.8 %collective-permute-start = (bf16[32,3712]{1,0:T(8,128)(2,1)S(1)}, bf16[32,3712]{1,0:T(8,128)(2,1)S(1)}, u32[]{:S(2)}, u32[]{:S(2)}) collective-permute-start(bf16[32,3712]{1,0:T(8,128)(2,1)S(1)} %broadcast_select_fusion.3), channel_id=1, source_target_pairs={{0,16},{16,0},{1,17},{17,1},{2,18},{18,2},{3,19},{19,3},{4,20},{20... | collective-permute-start | bytes 712712 | tf_op jit(solution)/shard_map/ppermute | solution.py:32
  11.8 17.5 %copy-start.1 = (bf16[64,3712]{1,0:T(8,128)(2,1)}, bf16[64,3712]{1,0:T(8,128)(2,1)S(1)}, u32[]{:S(2)}) copy-start(bf16[64,3712]{1,0:T(8,128)(2,1)S(1)} %pad_maximum_fusion.refs_3_) | copy-start | bytes 1425412
  11.8 13.9 %collective-permute-start.2 = (bf16[64,3712]{1,0:T(8,128)(2,1)S(1)}, bf16[64,3712]{1,0:T(8,128)(2,1)S(1)}, u32[]{:S(2)}, u32[]{:S(2)}) collective-permute-start(bf16[64,3712]{1,0:T(8,128)(2,1)S(1)} %pad_maximum_fusion.refs_3_), channel_id=1, source_target_pairs={{0,4},{1,5},{2,6},{3,7},{4,8},{5,9},{6,10},{7,11},{8,12},{9,13},{1... | collective-permute-start | bytes 1425416 | tf_op jit(solution)/shard_map/ppermute | solution.py:93
  13.7 12.0 %collective-permute-start.1 = (bf16[64,3712]{1,0:T(8,128)(2,1)S(1)}, bf16[64,3712]{1,0:T(8,128)(2,1)S(1)}, u32[]{:S(2)}, u32[]{:S(2)}) collective-permute-start(bf16[64,3712]{1,0:T(8,128)(2,1)S(1)} %pad_maximum_fusion.refs_3_), channel_id=1, source_target_pairs={{0,2},{1,3},{2,0},{3,1},{4,6},{5,7},{6,4},{7,5},{8,10},{9,11},{10,... | collective-permute-start | bytes 1425416 | tf_op jit(solution)/shard_map/ppermute | solution.py:93
  15.2 14.1 %collective-permute-start.4 = (bf16[64,3712]{1,0:T(8,128)(2,1)S(1)}, bf16[64,3712]{1,0:T(8,128)(2,1)S(1)}, u32[]{:S(2)}, u32[]{:S(2)}) collective-permute-start(bf16[64,3712]{1,0:T(8,128)(2,1)S(1)} %pad_maximum_fusion.refs_3_), channel_id=1, source_target_pairs={{0,1},{1,0},{2,3},{3,2},{4,5},{5,4},{6,7},{7,6},{8,9},{9,8},{10,11... | collective-permute-start | bytes 1425416 | tf_op jit(solution)/shard_map/ppermute | solution.py:93
  25.7 14.2 %copy-start.17 = (bf16[64,3712]{1,0:T(8,128)(2,1)}, bf16[64,3712]{1,0:T(8,128)(2,1)S(1)}, u32[]{:S(2)}) copy-start(bf16[64,3712]{1,0:T(8,128)(2,1)S(1)} %collective-permute-done.2.refs_3_) | copy-start | bytes 1425412
  25.7 3.5 %collective-permute-start.5 = (bf16[64,3712]{1,0:T(8,128)(2,1)S(1)}, bf16[64,3712]{1,0:T(8,128)(2,1)S(1)}, u32[]{:S(2)}, u32[]{:S(2)}) collective-permute-start(bf16[64,3712]{1,0:T(8,128)(2,1)S(1)} %collective-permute-done.1.refs_4_), channel_id=1, source_target_pairs={{0,1},{1,0},{2,3},{3,2},{4,5},{5,4},{6,7},{7,6},{8,9},{9,8},{10,11... | collective-permute-start | bytes 1425416 | tf_op jit(solution)/shard_map/ppermute | solution.py:93
  25.8 14.1 %collective-permute-start.3 = (bf16[64,3712]{1,0:T(8,128)(2,1)S(1)}, bf16[64,3712]{1,0:T(8,128)(2,1)S(1)}, u32[]{:S(2)}, u32[]{:S(2)}) collective-permute-start(bf16[64,3712]{1,0:T(8,128)(2,1)S(1)} %collective-permute-done.2.refs_3_), channel_id=1, source_target_pairs={{0,2},{1,3},{2,0},{3,1},{4,6},{5,7},{6,4},{7,5},{8,10},{9,11},{10,... | collective-permute-start | bytes 1425416 | tf_op jit(solution)/shard_map/ppermute | solution.py:93
  27.4 24.0 %collective-permute-start.8 = (bf16[64,3712]{1,0:T(8,128)(2,1)S(1)}, bf16[64,3712]{1,0:T(8,128)(2,1)S(1)}, u32[]{:S(2)}, u32[]{:S(2)}) collective-permute-start(bf16[64,3712]{1,0:T(8,128)(2,1)S(1)} %pad_maximum_fusion.refs_3_), channel_id=1, source_target_pairs={{0,8},{1,9},{2,10},{3,11},{4,12},{5,13},{6,14},{7,15},{8,0},{9,1},... | collective-permute-start | bytes 1425416 | tf_op jit(solution)/shard_map/ppermute | solution.py:93
  39.9 13.8 %copy-start.19 = (bf16[64,3712]{1,0:T(8,128)(2,1)}, bf16[64,3712]{1,0:T(8,128)(2,1)S(1)}, u32[]{:S(2)}) copy-start(bf16[64,3712]{1,0:T(8,128)(2,1)S(1)} %collective-permute-done.3.refs_4_) | copy-start | bytes 1425412
  39.9 11.5 %collective-permute-start.6 = (bf16[64,3712]{1,0:T(8,128)(2,1)S(1)}, bf16[64,3712]{1,0:T(8,128)(2,1)S(1)}, u32[]{:S(2)}, u32[]{:S(2)}) collective-permute-start(bf16[64,3712]{1,0:T(8,128)(2,1)S(1)} %collective-permute-done.2.refs_3_), channel_id=1, source_target_pairs={{0,1},{1,0},{2,3},{3,2},{4,5},{5,4},{6,7},{7,6},{8,9},{9,8},{10,11... | collective-permute-start | bytes 1425416 | tf_op jit(solution)/shard_map/ppermute | solution.py:93
  40.0 11.4 %collective-permute-start.7 = (bf16[64,3712]{1,0:T(8,128)(2,1)S(1)}, bf16[64,3712]{1,0:T(8,128)(2,1)S(1)}, u32[]{:S(2)}, u32[]{:S(2)}) collective-permute-start(bf16[64,3712]{1,0:T(8,128)(2,1)S(1)} %collective-permute-done.3.refs_4_), channel_id=1, source_target_pairs={{0,1},{1,0},{2,3},{3,2},{4,5},{5,4},{6,7},{7,6},{8,9},{9,8},{10,11... | collective-permute-start | bytes 1425416 | tf_op jit(solution)/shard_map/ppermute | solution.py:93
  40.5 29.0 %collective-permute-start.12 = (bf16[3,192,1024]{2,1,0:T(8,128)(2,1)}, bf16[3,192,1024]{2,1,0:T(8,128)(2,1)S(1)}, u32[]{:S(2)}, u32[]{:S(2)}) collective-permute-start(bf16[3,192,1024]{2,1,0:T(8,128)(2,1)} %get-tuple-element.175), channel_id=1, source_target_pairs={{0,16},{16,0},{1,17},{17,1},{2,18},{18,2},{3,19},{19,3},{4,20},{20... | collective-permute-start | bytes 3538952 | tf_op jit(solution)/shard_map/ppermute | solution.py:32
  51.4 13.6 %copy-start.15 = (bf16[64,3712]{1,0:T(8,128)(2,1)}, bf16[64,3712]{1,0:T(8,128)(2,1)S(1)}, u32[]{:S(2)}) copy-start(bf16[64,3712]{1,0:T(8,128)(2,1)S(1)} %collective-permute-done.8.refs_3_) | copy-start | bytes 1425412
  51.4 13.5 %collective-permute-start.13 = (bf16[64,3712]{1,0:T(8,128)(2,1)S(1)}, bf16[64,3712]{1,0:T(8,128)(2,1)S(1)}, u32[]{:S(2)}, u32[]{:S(2)}) collective-permute-start(bf16[64,3712]{1,0:T(8,128)(2,1)S(1)} %collective-permute-done.8.refs_3_), channel_id=1, source_target_pairs={{0,2},{1,3},{2,0},{3,1},{4,6},{5,7},{6,4},{7,5},{8,10},{9,11},{10,... | collective-permute-start | bytes 1425416 | tf_op jit(solution)/shard_map/ppermute | solution.py:93
  52.0 13.5 %collective-permute-start.10 = (bf16[64,3712]{1,0:T(8,128)(2,1)}, bf16[64,3712]{1,0:T(8,128)(2,1)S(1)}, u32[]{:S(2)}, u32[]{:S(2)}) collective-permute-start(bf16[64,3712]{1,0:T(8,128)(2,1)} %copy-done.1), channel_id=1, source_target_pairs={{0,12},{1,13},{2,14},{3,15},{4,0},{5,1},{6,2},{7,3},{8,4},{9,5},{1... | collective-permute-start | bytes 1425416 | tf_op jit(solution)/shard_map/ppermute | solution.py:93
  63.4 31.4 %collective-permute-start.9 = (bf16[3,192,1024]{2,1,0:T(8,128)(2,1)}, bf16[3,192,1024]{2,1,0:T(8,128)(2,1)S(1)}, u32[]{:S(2)}, u32[]{:S(2)}) collective-permute-start(bf16[3,192,1024]{2,1,0:T(8,128)(2,1)} %get-tuple-element.184), channel_id=1, source_target_pairs={{0,16},{16,0},{1,17},{17,1},{2,18},{18,2},{3,19},{19,3},{4,20},{20... | collective-permute-start | bytes 3538952 | tf_op jit(solution)/shard_map/ppermute | solution.py:32
  64.9 4.6 %collective-permute-start.14 = (bf16[64,3712]{1,0:T(8,128)(2,1)S(1)}, bf16[64,3712]{1,0:T(8,128)(2,1)S(1)}, u32[]{:S(2)}, u32[]{:S(2)}) collective-permute-start(bf16[64,3712]{1,0:T(8,128)(2,1)S(1)} %collective-permute-done.8.refs_3_), channel_id=1, source_target_pairs={{0,1},{1,0},{2,3},{3,2},{4,5},{5,4},{6,7},{7,6},{8,9},{9,8},{10,11... | collective-permute-start | bytes 1425416 | tf_op jit(solution)/shard_map/ppermute | solution.py:93
  65.0 4.5 %collective-permute-start.15 = (bf16[64,3712]{1,0:T(8,128)(2,1)S(1)}, bf16[64,3712]{1,0:T(8,128)(2,1)S(1)}, u32[]{:S(2)}, u32[]{:S(2)}) collective-permute-start(bf16[64,3712]{1,0:T(8,128)(2,1)S(1)} %collective-permute-done.13.refs_4_), channel_id=1, source_target_pairs={{0,1},{1,0},{2,3},{3,2},{4,5},{5,4},{6,7},{7,6},{8,9},{9,8},{10,11... | collective-permute-start | bytes 1425416 | tf_op jit(solution)/shard_map/ppermute | solution.py:93
  65.5 22.0 %copy-start.14 = (bf16[64,3712]{1,0:T(8,128)(2,1)}, bf16[64,3712]{1,0:T(8,128)(2,1)S(1)}, u32[]{:S(2)}) copy-start(bf16[64,3712]{1,0:T(8,128)(2,1)S(1)} %collective-permute-done.10.refs_3_) | copy-start | bytes 1425412
  65.5 22.0 %collective-permute-start.11 = (bf16[64,3712]{1,0:T(8,128)(2,1)S(1)}, bf16[64,3712]{1,0:T(8,128)(2,1)S(1)}, u32[]{:S(2)}, u32[]{:S(2)}) collective-permute-start(bf16[64,3712]{1,0:T(8,128)(2,1)S(1)} %collective-permute-done.10.refs_3_), channel_id=1, source_target_pairs={{0,2},{1,3},{2,0},{3,1},{4,6},{5,7},{6,4},{7,5},{8,10},{9,11},{10,... | collective-permute-start | bytes 1425416 | tf_op jit(solution)/shard_map/ppermute | solution.py:93
  85.9 34.1 %collective-permute-start.22 = (bf16[3,192,1024]{2,1,0:T(8,128)(2,1)}, bf16[3,192,1024]{2,1,0:T(8,128)(2,1)S(1)}, u32[]{:S(2)}, u32[]{:S(2)}) collective-permute-start(bf16[3,192,1024]{2,1,0:T(8,128)(2,1)} %get-tuple-element.200), channel_id=1, source_target_pairs={{0,16},{16,0},{1,17},{17,1},{2,18},{18,2},{3,19},{19,3},{4,20},{20... | collective-permute-start | bytes 3538952 | tf_op jit(solution)/shard_map/ppermute | solution.py:32
  87.5 7.3 %copy-start.16 = (bf16[64,3712]{1,0:T(8,128)(2,1)}, bf16[64,3712]{1,0:T(8,128)(2,1)S(1)}, u32[]{:S(2)}) copy-start(bf16[64,3712]{1,0:T(8,128)(2,1)S(1)} %collective-permute-done.11.refs_4_) | copy-start | bytes 1425412
  87.5 7.3 %collective-permute-start.16 = (bf16[64,3712]{1,0:T(8,128)(2,1)S(1)}, bf16[64,3712]{1,0:T(8,128)(2,1)S(1)}, u32[]{:S(2)}, u32[]{:S(2)}) collective-permute-start(bf16[64,3712]{1,0:T(8,128)(2,1)S(1)} %collective-permute-done.10.refs_3_), channel_id=1, source_target_pairs={{0,1},{1,0},{2,3},{3,2},{4,5},{5,4},{6,7},{7,6},{8,9},{9,8},{10,11... | collective-permute-start | bytes 1425416 | tf_op jit(solution)/shard_map/ppermute | solution.py:93
  87.6 7.2 %collective-permute-start.17 = (bf16[64,3712]{1,0:T(8,128)(2,1)S(1)}, bf16[64,3712]{1,0:T(8,128)(2,1)S(1)}, u32[]{:S(2)}, u32[]{:S(2)}) collective-permute-start(bf16[64,3712]{1,0:T(8,128)(2,1)S(1)} %collective-permute-done.11.refs_4_), channel_id=1, source_target_pairs={{0,1},{1,0},{2,3},{3,2},{4,5},{5,4},{6,7},{7,6},{8,9},{9,8},{10,11... | collective-permute-start | bytes 1425416 | tf_op jit(solution)/shard_map/ppermute | solution.py:93
  111.2 33.3 %collective-permute-start.21 = (bf16[3,192,1024]{2,1,0:T(8,128)(2,1)}, bf16[3,192,1024]{2,1,0:T(8,128)(2,1)S(1)}, u32[]{:S(2)}, u32[]{:S(2)}) collective-permute-start(bf16[3,192,1024]{2,1,0:T(8,128)(2,1)} %get-tuple-element.218), channel_id=1, source_target_pairs={{0,16},{16,0},{1,17},{17,1},{2,18},{18,2},{3,19},{19,3},{4,20},{20... | collective-permute-start | bytes 3538952 | tf_op jit(solution)/shard_map/ppermute | solution.py:32
  112.7 2.1 %collective-permute-start.18 = (bf16[64,3712]{1,0:T(8,128)(2,1)}, bf16[64,3712]{1,0:T(8,128)(2,1)S(1)}, u32[]{:S(2)}, u32[]{:S(2)}) collective-permute-start(bf16[64,3712]{1,0:T(8,128)(2,1)} %get-tuple-element.215), channel_id=1, source_target_pairs={{0,1},{1,0},{2,3},{3,2},{4,5},{5,4},{6,7},{7,6},{8,9},{9,8},{10,11... | collective-permute-start | bytes 1425416 | tf_op jit(solution)/shard_map/ppermute | solution.py:93
  112.7 2.7 %collective-permute-start.19 = (bf16[64,3712]{1,0:T(8,128)(2,1)}, bf16[64,3712]{1,0:T(8,128)(2,1)S(1)}, u32[]{:S(2)}, u32[]{:S(2)}) collective-permute-start(bf16[64,3712]{1,0:T(8,128)(2,1)} %get-tuple-element.217), channel_id=1, source_target_pairs={{0,1},{1,0},{2,3},{3,2},{4,5},{5,4},{6,7},{7,6},{8,9},{9,8},{10,11... | collective-permute-start | bytes 1425416 | tf_op jit(solution)/shard_map/ppermute | solution.py:93
  121.1 11.4 %copy-start.39 = (bf16[64,3712]{1,0:T(8,128)(2,1)S(1)}, bf16[64,3712]{1,0:T(8,128)(2,1)}, u32[]{:S(2)}) copy-start(bf16[64,3712]{1,0:T(8,128)(2,1)} %get-tuple-element.225) | copy-start | bytes 1425412
  121.1 24.2 %copy-start.6 = (f32[64,3712]{1,0:T(8,128)S(1)}, f32[64,3712]{1,0:T(8,128)}, u32[]{:S(2)}) copy-start(f32[64,3712]{1,0:T(8,128)} %get-tuple-element.244) | copy-start | bytes 2850820
  131.9 2.1 %collective-permute-start.23 = (bf16[64,3712]{1,0:T(8,128)(2,1)}, bf16[64,3712]{1,0:T(8,128)(2,1)S(1)}, u32[]{:S(2)}, u32[]{:S(2)}) collective-permute-start(bf16[64,3712]{1,0:T(8,128)(2,1)} %get-tuple-element.234), channel_id=1, source_target_pairs={{0,1},{1,0},{2,3},{3,2},{4,5},{5,4},{6,7},{7,6},{8,9},{9,8},{10,11... | collective-permute-start | bytes 1425416 | tf_op jit(solution)/shard_map/ppermute | solution.py:93
  132.0 2.7 %collective-permute-start.24 = (bf16[64,3712]{1,0:T(8,128)(2,1)}, bf16[64,3712]{1,0:T(8,128)(2,1)S(1)}, u32[]{:S(2)}, u32[]{:S(2)}) collective-permute-start(bf16[64,3712]{1,0:T(8,128)(2,1)} %get-tuple-element.236), channel_id=1, source_target_pairs={{0,1},{1,0},{2,3},{3,2},{4,5},{5,4},{6,7},{7,6},{8,9},{9,8},{10,11... | collective-permute-start | bytes 1425416 | tf_op jit(solution)/shard_map/ppermute | solution.py:93
  132.5 12.9 %collective-permute-start.20 = (bf16[64,3712]{1,0:T(8,128)(2,1)S(1)}, bf16[64,3712]{1,0:T(8,128)(2,1)S(1)}, u32[]{:S(2)}, u32[]{:S(2)}) collective-permute-start(bf16[64,3712]{1,0:T(8,128)(2,1)S(1)} %copy-done.39), channel_id=1, source_target_pairs={{0,2},{1,3},{2,0},{3,1},{4,6},{5,7},{6,4},{7,5},{8,10},{9,11},{10,... | collective-permute-start | bytes 1425416 | tf_op jit(solution)/shard_map/ppermute | solution.py:93
  145.4 14.0 %collective-permute-start.25 = (bf16[64,3712]{1,0:T(8,128)(2,1)S(1)}, bf16[64,3712]{1,0:T(8,128)(2,1)S(1)}, u32[]{:S(2)}, u32[]{:S(2)}) collective-permute-start(bf16[64,3712]{1,0:T(8,128)(2,1)S(1)} %add_convert_fusion.2), channel_id=1, source_target_pairs={{0,12},{1,13},{2,14},{3,15},{4,0},{5,1},{6,2},{7,3},{8,4},{9,5},{1... | collective-permute-start | bytes 1425416 | tf_op jit(solution)/shard_map/ppermute | solution.py:93
  147.0 12.5 %collective-permute-start.26 = (bf16[64,3712]{1,0:T(8,128)(2,1)}, bf16[64,3712]{1,0:T(8,128)(2,1)S(1)}, u32[]{:S(2)}, u32[]{:S(2)}) collective-permute-start(bf16[64,3712]{1,0:T(8,128)(2,1)} %get-tuple-element.255), channel_id=1, source_target_pairs={{0,2},{1,3},{2,0},{3,1},{4,6},{5,7},{6,4},{7,5},{8,10},{9,11},{10,... | collective-permute-start | bytes 1425416 | tf_op jit(solution)/shard_map/ppermute | solution.py:93
  148.0 10.9 %copy-start.34 = (bf16[128,3712]{1,0:T(8,128)(2,1)S(1)}, bf16[128,3712]{1,0:T(8,128)(2,1)}, u32[]{:S(2)}) copy-start(bf16[128,3712]{1,0:T(8,128)(2,1)} %get-tuple-element.202) | copy-start | bytes 2850820
  148.0 11.5 %copy-start.7 = (f32[64,3712]{1,0:T(8,128)S(1)}, f32[64,3712]{1,0:T(8,128)}, u32[]{:S(2)}) copy-start(f32[64,3712]{1,0:T(8,128)} %get-tuple-element.256) | copy-start | bytes 2850820
  158.8 3.3 %collective-permute-start.29 = (bf16[128,3712]{1,0:T(8,128)(2,1)}, bf16[128,3712]{1,0:T(8,128)(2,1)S(1)}, u32[]{:S(2)}, u32[]{:S(2)}) collective-permute-start(bf16[128,3712]{1,0:T(8,128)(2,1)} %get-tuple-element.253), channel_id=1, source_target_pairs={{0,1},{1,0},{2,3},{3,2},{4,5},{5,4},{6,7},{7,6},{8,9},{9,8},{10,11... | collective-permute-start | bytes 2850824 | tf_op jit(solution)/shard_map/ppermute | solution.py:93
  158.9 16.6 %collective-permute-start.28 = (bf16[128,3712]{1,0:T(8,128)(2,1)S(1)}, bf16[128,3712]{1,0:T(8,128)(2,1)S(1)}, u32[]{:S(2)}, u32[]{:S(2)}) collective-permute-start(bf16[128,3712]{1,0:T(8,128)(2,1)S(1)} %copy-done.34), channel_id=1, source_target_pairs={{0,1},{1,0},{2,3},{3,2},{4,5},{5,4},{6,7},{7,6},{8,9},{9,8},{10,11... | collective-permute-start | bytes 2850824 | tf_op jit(solution)/shard_map/ppermute | solution.py:93
  159.7 33.9 %collective-permute-start.27 = (bf16[64,3712]{1,0:T(8,128)(2,1)S(1)}, bf16[64,3712]{1,0:T(8,128)(2,1)S(1)}, u32[]{:S(2)}, u32[]{:S(2)}) collective-permute-start(bf16[64,3712]{1,0:T(8,128)(2,1)S(1)} %add_convert_fusion.1), channel_id=1, source_target_pairs={{0,8},{1,9},{2,10},{3,11},{4,12},{5,13},{6,14},{7,15},{8,0},{9,1},... | collective-permute-start | bytes 1425416 | tf_op jit(solution)/shard_map/ppermute | solution.py:93
  162.4 13.1 %copy-start.8 = (bf16[128,3712]{1,0:T(8,128)(2,1)S(1)}, bf16[128,3712]{1,0:T(8,128)(2,1)}, u32[]{:S(2)}) copy-start(bf16[128,3712]{1,0:T(8,128)(2,1)} %get-tuple-element.279) | copy-start | bytes 2850820
  162.4 13.0 %collective-permute-start.30 = (bf16[64,3712]{1,0:T(8,128)(2,1)S(1)}, bf16[64,3712]{1,0:T(8,128)(2,1)S(1)}, u32[]{:S(2)}, u32[]{:S(2)}) collective-permute-start(bf16[64,3712]{1,0:T(8,128)(2,1)S(1)} %slice.125), channel_id=1, source_target_pairs={{0,2},{1,3},{2,0},{3,1},{4,6},{5,7},{6,4},{7,5},{8,10},{9,11},{10,... | collective-permute-start | bytes 1425416 | tf_op jit(solution)/shard_map/ppermute | solution.py:93
  175.9 24.1 %collective-permute-start.34 = (bf16[32,3712]{1,0:T(8,128)(2,1)S(1)}, bf16[32,3712]{1,0:T(8,128)(2,1)S(1)}, u32[]{:S(2)}, u32[]{:S(2)}) collective-permute-start(bf16[32,3712]{1,0:T(8,128)(2,1)S(1)} %get-tuple-element.320), channel_id=1, source_target_pairs={{0,20},{1,21},{2,22},{3,23},{4,24},{5,25},{6,26},{7,27},{8,28},{9,... | collective-permute-start | bytes 712712 | tf_op jit(solution)/shard_map/ppermute | solution.py:105
  177.2 22.8 %collective-permute-start.33 = (bf16[32,3712]{1,0:T(8,128)(2,1)S(1)}, bf16[32,3712]{1,0:T(8,128)(2,1)S(1)}, u32[]{:S(2)}, u32[]{:S(2)}) collective-permute-start(bf16[32,3712]{1,0:T(8,128)(2,1)S(1)} %get-tuple-element.321), channel_id=1, source_target_pairs={{0,4},{1,5},{2,6},{3,7},{4,8},{5,9},{6,10},{7,11},{8,12},{9,13},{1... | collective-permute-start | bytes 712712 | tf_op jit(solution)/shard_map/ppermute | solution.py:105
  178.2 11.5 %collective-permute-start.31 = (bf16[64,3712]{1,0:T(8,128)(2,1)S(1)}, bf16[64,3712]{1,0:T(8,128)(2,1)S(1)}, u32[]{:S(2)}, u32[]{:S(2)}) collective-permute-start(bf16[64,3712]{1,0:T(8,128)(2,1)S(1)} %slice.124), channel_id=1, source_target_pairs={{0,2},{1,3},{2,0},{3,1},{4,6},{5,7},{6,4},{7,5},{8,10},{9,11},{10,... | collective-permute-start | bytes 1425416 | tf_op jit(solution)/shard_map/ppermute | solution.py:93
  179.4 10.3 %slice-start = ((f32[128,3712]{1,0:T(8,128)}), f32[64,3712]{1,0:T(8,128)S(1)}, s32[]{:S(2)}) async-start(f32[128,3712]{1,0:T(8,128)} %copy-done), calls=%async_computation | async-start | bytes 1900544 | tf_op jit(solution)/shard_map/slice | solution.py:202
  193.9 8.1 %copy-start.33 = (s32[32,8]{0,1:T(8,128)S(1)}, s32[32,8]{0,1:T(8,128)}, u32[]{:S(2)}) copy-start(s32[32,8]{0,1:T(8,128)} %param.10) | copy-start | bytes 3076
  193.9 7.8 %collective-permute-start.32 = (bf16[32,3712]{1,0:T(8,128)(2,1)S(1)}, bf16[32,3712]{1,0:T(8,128)(2,1)S(1)}, u32[]{:S(2)}, u32[]{:S(2)}) collective-permute-start(bf16[32,3712]{1,0:T(8,128)(2,1)S(1)} %select_convert_fusion), channel_id=1, source_target_pairs={{0,16},{16,0},{1,17},{17,1},{2,18},{18,2},{3,19},{19,3},{4,20},{20... | collective-permute-start | bytes 712712 | tf_op jit(solution)/shard_map/ppermute | solution.py:32
  (40 other events, 112.3 us)

commit v3 on v2

--- a/solution.py
+++ b/solution.py
@@ -445,7 +445,7 @@
         ]
 
     def cuts_of(number):
-        return inner if 0 < number < last else 1
+        return inner if number < last else 1
 
     def ready_parts(across):
         return [piece[index] for index in range(core) for piece in across]
@@ -511,8 +511,7 @@
             mine, *others = merge([cuts[0][0]] + cuts[0][1], inner)
         order.leave(mine, *others)
         held[number] = (mine, others)
-        if number or not last:
-            start_back(number)
+        start_back(number)
 
     def next_outer(number):
         mine, arrived = order.enter(*moving[number])
@@ -560,7 +559,9 @@
                 start_outer(later + 2)
         else:
             finish_chunk(number)
-        if 0 < number < last:
+        if 0 < number == last - 1:
+            next_outer(0)
+        if number < last:
             next_inner(number)
     add_up(range(1, last - 1))
     if last > 1:
@@ -577,15 +578,10 @@
     down_grad = dot_tn(joined(hidden_all), joined(out_all)).astype(BF)[None]
     order.leave(down_grad)
     next_outer(last)
-    if last:
-        next_inner(0)
-        start_back(0)
     x_all, gate_all = order.enter(rows_of(picked, 0), rows_of(ends, 1))
     x_all = joined(x_all)
     gate_grad = dot_tn(x_all, joined(gate_all)).astype(BF)[None]
     order.leave(gate_grad)
-    if last:
-        next_outer(0)
     straight = finals.pop(last) if last else None
     (arrived,) = order.enter(list(finals.values()))
     total = add_all(arrived[0].astype(F32), arrived[1:])

time: 204 us -> 201 us (0.985)
  waiting for transfers between devices: 66.3 us -> 61.1 us
  Pallas kernels: 76.3 us -> 78.9 us
  starting transfers between devices: 33 us -> 30.4 us
    ppermute x2, waiting for transfers between devices: 0.01 us -> 9.41 us  [shift_to_owner(): return lax.ppermute(value, ('dp', 'expert'), pairs)]
    ppermute x27 -> x28, waiting for transfers between devices: 42.7 us -> 34.8 us  [shift_expert(): return lax.ppermute(value, 'expert', pairs)]
    ppermute x6, waiting for transfers between devices: 23.5 us -> 16.9 us  [shift_dp(): lax.ppermute(value, 'dp', [(i, (i + step) % groups) for i in range(groups)])]
    pallas_call x2 -> x3, Pallas kernels: 5.3 us -> 7.93 us  [merge_between(): pl.pallas_call(body, out_shape=[jax.ShapeDtypeStruct(group[0].shape, kind...]
    ppermute x27 -> x28, starting transfers between devices: 20 us -> 19.6 us  [shift_expert(): return lax.ppermute(value, 'expert', pairs)]
  transfers between devices with their start and end apart: 35 -> 36, of which waited for: 17 -> 17; matrix products, arithmetic and copies ran while one was open for 8% -> 8% of each run, Pallas kernels for 37% -> 39%
where the time goes in v3:
time: 201 us
  Pallas kernels  78.9 us (39%)
  waiting for transfers between devices  61.1 us (30%)
  starting transfers between devices  30.4 us (15%)
  matrix products  14 us (7%)
  local copies, waits for them, and re-layouts  10.1 us (5%)
  other arithmetic  4.78 us (2%)
    ppermute x28, waiting for transfers between devices, shift_expert(): return lax.ppermute(value, 'expert', pairs)  34.8 us
    pallas_call x2, Pallas kernels, finish_and_project(): pl.pallas_call(body, grid=(hidden // tile,), in_specs=[pl.BlockSpec(memor...  30.1 us
    pallas_call x2, Pallas kernels, finish(): pl.pallas_call(lambda *refs: finish_body(len(sent), number_parts, *refs),...  21.5 us
    ppermute x28, starting transfers between devices, shift_expert(): return lax.ppermute(value, 'expert', pairs)  19.6 us
    pallas_call x2, Pallas kernels, project(): pl.pallas_call(lambda *refs: project_body(len(parts), part, experts, *ref...  19.3 us
    ppermute x6, waiting for transfers between devices, shift_dp(): lax.ppermute(value, 'dp', [(i, (i + step) % groups) for i in range(groups)])  16.9 us
    dot_general x3, matrix products, dot_tn(): lax.dot_general(first, second, (((0,), (0,)), ((), ())), preferred_elemen...  14 us
    ppermute x6, starting transfers between devices, shift_dp(): lax.ppermute(value, 'dp', [(i, (i + step) % groups) for i in range(groups)])  9.65 us
  transfers between devices with their start and end apart: 36, of which 17 were waited for; matrix products, arithmetic and copies ran while one was open for 8% of the time, Pallas kernels for 39%

profile of v3, /device:TPU:0, one launch (start us, length us, event | category | flops | bytes accessed | tf_op | source)
XLA Modules:
  0.0 200.6 jit_solution(79120306099265117)
XLA Ops:
  1.5 1.1 fusion.39
  2.9 3.0 %collective-permute-start = (bf16[32,3712]{1,0:T(8,128)(2,1)S(1)}, bf16[32,3712]{1,0:T(8,128)(2,1)S(1)}, u32[]{:S(2)}, u32[]{:S(2)}) collective-permute-start(bf16[32,3712]{1,0:T(8,128)(2,1)S(1)} %broadcast_select_fusion.3), channel_id=1, source_target_pairs={{0,16},{16,0},{1,17},{17,1},{2,18},{18,2},{3,19},{19,3},{4,20},{20... | collective-permute-start | bytes 712712 | tf_op jit(solution)/shard_map/ppermute | solution.py:32
  5.9 5.8 %collective-permute-done = bf16[32,3712]{1,0:T(8,128)(2,1)S(1)} collective-permute-done((bf16[32,3712]{1,0:T(8,128)(2,1)S(1)}, bf16[32,3712]{1,0:T(8,128)(2,1)S(1)}, u32[]{:S(2)}, u32[]{:S(2)}) %collective-permute-start) | collective-permute-done | bytes 237600 | tf_op jit(solution)/shard_map/ppermute | solution.py:32
  11.8 1.9 collective-permute-start.3
  13.7 1.5 collective-permute-start.2
  15.2 10.5 %collective-permute-done.3.refs_3_ = bf16[64,3712]{1,0:T(8,128)(2,1)S(1)} collective-permute-done((bf16[64,3712]{1,0:T(8,128)(2,1)S(1)}, bf16[64,3712]{1,0:T(8,128)(2,1)S(1)}, u32[]{:S(2)}, u32[]{:S(2)}) %collective-permute-start.3) | collective-permute-done | bytes 475168 | tf_op jit(solution)/shard_map/ppermute | solution.py:93
  25.8 1.6 collective-permute-start.6
  27.4 1.9 collective-permute-start.9
  30.2 9.6 %project.2 = (bf16[192,1792]{1,0:T(8,128)(2,1)}, bf16[192,1792]{1,0:T(8,128)(2,1)}, bf16[192,1792]{1,0:T(8,128)(2,1)}, f32[192,128]{1,0:T(8,128)}, bf16[192,256]...) custom-call(s32[1,1]{1,0:T(1,128)} %bitcast.refs_0_, ...), custom_call_target="tpu_custom_call" | custom-call | tf_op jit(solution)/shard_map/project/pallas_call | solution.py:179
  40.4 1.5 collective-permute-start.5
  41.9 9.4 %collective-permute-done.9.refs_3_ = bf16[64,3712]{1,0:T(8,128)(2,1)S(1)} collective-permute-done((bf16[64,3712]{1,0:T(8,128)(2,1)S(1)}, bf16[64,3712]{1,0:T(8,128)(2,1)S(1)}, u32[]{:S(2)}, u32[]{:S(2)}) %collective-permute-start.9) | collective-permute-done | bytes 475168 | tf_op jit(solution)/shard_map/ppermute | solution.py:93
  52.0 1.7 collective-permute-start.15
  53.7 9.7 %project.3 = (bf16[192,1792]{1,0:T(8,128)(2,1)}, bf16[192,1792]{1,0:T(8,128)(2,1)}, bf16[192,1792]{1,0:T(8,128)(2,1)}, f32[192,128]{1,0:T(8,128)}, bf16[192,256]...) custom-call(s32[1,1]{1,0:T(1,128)} %bitcast.refs_0_, ...), custom_call_target="tpu_custom_call" | custom-call | tf_op jit(solution)/shard_map/project/pallas_call | solution.py:179
  64.4 1.5 collective-permute-start.19
  66.6 1.1 collective-permute-start.16
  67.7 1.8 collective-permute-done.5.refs_8_
  69.5 1.0 copy-done.4
  70.8 15.0 %step.2 = (bf16[192,1792]{1,0:T(8,128)(2,1)}, bf16[192,1792]{1,0:T(8,128)(2,1)}, bf16[192,1792]{1,0:T(8,128)(2,1)}, f32[192,128]{1,0:T(8,128)}, bf16[192,256]{1,...) custom-call(s32[1,1]{1,0:T(1,128)} %bitcast.refs_0_, ...), custom_call_target="tpu_custom_call" | custom-call | tf_op jit(solution)/shard_map/step/pallas_call | solution.py:330
  85.9 1.6 collective-permute-start.18
  88.3 1.3 collective-permute-done.14.refs_3_
  90.3 2.7 %merge.3 = (f32[64,3712]{1,0:T(8,128)}, bf16[64,3712]{1,0:T(8,128)(2,1)}) custom-call(bf16[64,3712]{1,0:T(8,128)(2,1)} %get-tuple-element.212.refs_0_, bf16[64,3712]{1,0:T(8,128)(2,1)} %copy-done.27, bf16[64,3712]{1,0:T(8,128)(2,1)} %get-tuple-element.214.refs_2_, bf16[64,3712]{1,0:T(8,128)(2,1)} %copy-done.28), custom_call_target="tpu_custom_call" | custom-call | tf_op jit(solution)/shard_map/merge/pallas_call | solution.py:216
  93.0 1.8 collective-permute-done.19.refs_8_
  94.8 1.0 copy-done.3
  96.1 15.1 %step.3 = (bf16[192,1792]{1,0:T(8,128)(2,1)}, bf16[192,1792]{1,0:T(8,128)(2,1)}, bf16[192,1792]{1,0:T(8,128)(2,1)}, f32[192,128]{1,0:T(8,128)}, bf16[192,256]{1,...) custom-call(s32[1,1]{1,0:T(1,128)} %bitcast.refs_0_, ...), custom_call_target="tpu_custom_call" | custom-call | tf_op jit(solution)/shard_map/step/pallas_call | solution.py:330
  112.3 1.5 collective-permute-start.25
  114.7 2.6 %merge.4 = (f32[64,3712]{1,0:T(8,128)}, bf16[64,3712]{1,0:T(8,128)(2,1)}) custom-call(bf16[64,3712]{1,0:T(8,128)(2,1)} %get-tuple-element.235.refs_0_, bf16[64,3712]{1,0:T(8,128)(2,1)} %copy-done.29, bf16[64,3712]{1,0:T(8,128)(2,1)} %get-tuple-element.237.refs_2_, bf16[64,3712]{1,0:T(8,128)(2,1)} %copy-done.32), custom_call_target="tpu_custom_call" | custom-call | tf_op jit(solution)/shard_map/merge/pallas_call | solution.py:216
  117.3 1.5 collective-permute-start.24
  118.8 1.3 collective-permute-done.18.refs_1_
  120.0 1.0 copy-done.1
  121.1 10.8 %finish.2 = (bf16[192,1024]{1,0:T(8,128)(2,1)}, bf16[192,1024]{1,0:T(8,128)(2,1)}, bf16[192,1024]{1,0:T(8,128)(2,1)}, bf16[64,3712]{1,0:T(8,128)(2,1)}, bf16[64,...) custom-call(f32[3,192,1024]{2,1,0:T(8,128)} %get-tuple-element.241.refs_0_, ...), custom_call_target="tpu_custom_call" | custom-call | tf_op jit(solution)/shard_map/finish/pallas_call | solution.py:294
  132.5 1.5 collective-permute-done.26.refs_1_
  134.7 0.8 copy-done.33
  135.5 2.6 %merge.5 = (f32[64,3712]{1,0:T(8,128)}, bf16[64,3712]{1,0:T(8,128)(2,1)}) custom-call(bf16[64,3712]{1,0:T(8,128)(2,1)} %get-tuple-element.254.refs_0_, bf16[64,3712]{1,0:T(8,128)(2,1)} %copy-done.31, bf16[64,3712]{1,0:T(8,128)(2,1)} %get-tuple-element.256.refs_2_, bf16[64,3712]{1,0:T(8,128)(2,1)} %copy-done.33), custom_call_target="tpu_custom_call" | custom-call | tf_op jit(solution)/shard_map/merge/pallas_call | solution.py:216
  138.1 6.3 %collective-permute-done.25.refs_1_ = bf16[3,192,1024]{2,1,0:T(8,128)(2,1)S(1)} collective-permute-done((bf16[3,192,1024]{2,1,0:T(8,128)(2,1)}, bf16[3,192,1024]{2,1,0:T(8,128)(2,1)S(1)}, u32[]{:S(2)}, u32[]{:S(2)}) %collective-permute-start.25) | collective-permute-done | bytes 1179680 | tf_op jit(solution)/shard_map/ppermute | solution.py:32
  144.5 1.4 collective-permute-start.28
  146.0 1.0 collective-permute-start.29
  147.0 10.7 %finish.3 = (bf16[192,1024]{1,0:T(8,128)(2,1)}, bf16[192,1024]{1,0:T(8,128)(2,1)}, bf16[192,1024]{1,0:T(8,128)(2,1)}, bf16[128,3712]{1,0:T(8,128)(2,1)}, bf16[128,3712]{1,0:T(8,128)(2,1)}) custom-call(f32[3,192,1024]{2,1,0:T(8,128)} %get-tuple-element.264.refs_0_, bf16[3,192,1024]{2,1,0:T(8,128)(2,1)} %copy-done.2, ...), custom_call_target="tpu_custom_call" | custom-call | tf_op jit(solution)/shard_map/finish/pallas_call | solution.py:294
  158.8 1.7 collective-permute-done.31
  161.0 1.1 collective-permute-start.32
  162.1 5.0 %fusion = bf16[1,1024,1792]{2,1,0:T(8,128)(2,1)} fusion(bf16[192,1792]{1,0:T(8,128)(2,1)S(1)} %copy-done.38, bf16[192,1792]{1,0:T(8,128)(2,1)S(1)} %copy-done.37, bf16[192,1792]{1,0:T(8,128)(2,1)S(1)} %copy-done.36, bf16[192,1792]{1,0:T(8,128)(2,1)S(1)} %copy-done.35, bf16[192,1024]{1,0:T(8,128)(2,1)S(1)} %copy-done.51, ...), kind=kOutput, calls=%fused_computation.3 | convolution fusion | flops 2837708800 | bytes 7995392 | tf_op jit(solution)/shard_map/dot_general | solution.py:27
  167.0 6.9 %collective-permute-done.32 = bf16[64,3712]{1,0:T(8,128)(2,1)S(1)} collective-permute-done((bf16[64,3712]{1,0:T(8,128)(2,1)S(1)}, bf16[64,3712]{1,0:T(8,128)(2,1)S(1)}, u32[]{:S(2)}, u32[]{:S(2)}) %collective-permute-start.32) | collective-permute-done | bytes 475168 | tf_op jit(solution)/shard_map/ppermute | solution.py:93
  174.3 0.8 copy-done.12
  175.6 4.5 %fusion.1 = bf16[1,1792,1024]{2,1,0:T(8,128)(2,1)} fusion(bf16[768,1792]{1,0:T(8,128)(2,1)S(1)} %constant_dynamic-update-slice_fusion, bf16[192,1024]{1,0:T(8,128)(2,1)S(1)} %copy-done.50, bf16[192,1024]{1,0:T(8,128)(2,1)S(1)} %copy-done.47, bf16[192,1024]{1,0:T(8,128)(2,1)S(1)} %copy-done.44, bf16[192,1024]{1,0:T(8,128)(2,1)S(1)} %copy-done.41), kind=kOutput, calls=%fused_computation.4 | convolution fusion | flops 2826698752 | bytes 7995392 | tf_op jit(solution)/shard_map/dot_general | solution.py:27
  180.1 2.1 %collective-permute-done.30 = bf16[64,3712]{1,0:T(8,128)(2,1)S(1)} collective-permute-done((bf16[64,3712]{1,0:T(8,128)(2,1)S(1)}, bf16[64,3712]{1,0:T(8,128)(2,1)S(1)}, u32[]{:S(2)}, u32[]{:S(2)}) %collective-permute-start.30) | collective-permute-done | bytes 475168 | tf_op jit(solution)/shard_map/ppermute | solution.py:93
  182.6 1.1 collective-permute-start.34
  184.2 4.5 %fusion.2 = bf16[1,1792,1024]{2,1,0:T(8,128)(2,1)} fusion(bf16[768,1792]{1,0:T(8,128)(2,1)S(1)} %constant_dynamic-update-slice_fusion, bf16[192,1024]{1,0:T(8,128)(2,1)S(1)} %copy-done.48, bf16[192,1024]{1,0:T(8,128)(2,1)S(1)} %copy-done.45, bf16[192,1024]{1,0:T(8,128)(2,1)S(1)} %copy-done.43, bf16[192,1024]{1,0:T(8,128)(2,1)S(1)} %copy-done.40), kind=kOutput, calls=%fused_computation.5 | convolution fusion | flops 2826698752 | bytes 7995392 | tf_op jit(solution)/shard_map/dot_general | solution.py:27
  188.8 5.2 %collective-permute-done.35 = bf16[32,3712]{1,0:T(8,128)(2,1)S(1)} collective-permute-done((bf16[32,3712]{1,0:T(8,128)(2,1)S(1)}, bf16[32,3712]{1,0:T(8,128)(2,1)S(1)}, u32[]{:S(2)}, u32[]{:S(2)}) %collective-permute-start.35) | collective-permute-done | bytes 237600 | tf_op jit(solution)/shard_map/ppermute | solution.py:105
  193.9 4.2 %collective-permute-done.34 = bf16[32,3712]{1,0:T(8,128)(2,1)S(1)} collective-permute-done((bf16[32,3712]{1,0:T(8,128)(2,1)S(1)}, bf16[32,3712]{1,0:T(8,128)(2,1)S(1)}, u32[]{:S(2)}, u32[]{:S(2)}) %collective-permute-start.34) | collective-permute-done | bytes 237600 | tf_op jit(solution)/shard_map/ppermute | solution.py:105
  (179 shorter events, 16.3 us)
Async XLA Ops:
  2.9 8.8 %collective-permute-start = (bf16[32,3712]{1,0:T(8,128)(2,1)S(1)}, bf16[32,3712]{1,0:T(8,128)(2,1)S(1)}, u32[]{:S(2)}, u32[]{:S(2)}) collective-permute-start(bf16[32,3712]{1,0:T(8,128)(2,1)S(1)} %broadcast_select_fusion.3), channel_id=1, source_target_pairs={{0,16},{16,0},{1,17},{17,1},{2,18},{18,2},{3,19},{19,3},{4,20},{20... | collective-permute-start | bytes 712712 | tf_op jit(solution)/shard_map/ppermute | solution.py:32
  11.8 17.5 %copy-start = (bf16[64,3712]{1,0:T(8,128)(2,1)}, bf16[64,3712]{1,0:T(8,128)(2,1)S(1)}, u32[]{:S(2)}) copy-start(bf16[64,3712]{1,0:T(8,128)(2,1)S(1)} %pad_maximum_fusion.refs_3_) | copy-start | bytes 1425412
  11.8 13.9 %collective-permute-start.3 = (bf16[64,3712]{1,0:T(8,128)(2,1)S(1)}, bf16[64,3712]{1,0:T(8,128)(2,1)S(1)}, u32[]{:S(2)}, u32[]{:S(2)}) collective-permute-start(bf16[64,3712]{1,0:T(8,128)(2,1)S(1)} %pad_maximum_fusion.refs_3_), channel_id=1, source_target_pairs={{0,4},{1,5},{2,6},{3,7},{4,8},{5,9},{6,10},{7,11},{8,12},{9,13},{1... | collective-permute-start | bytes 1425416 | tf_op jit(solution)/shard_map/ppermute | solution.py:93
  13.7 12.0 %collective-permute-start.2 = (bf16[64,3712]{1,0:T(8,128)(2,1)S(1)}, bf16[64,3712]{1,0:T(8,128)(2,1)S(1)}, u32[]{:S(2)}, u32[]{:S(2)}) collective-permute-start(bf16[64,3712]{1,0:T(8,128)(2,1)S(1)} %pad_maximum_fusion.refs_3_), channel_id=1, source_target_pairs={{0,2},{1,3},{2,0},{3,1},{4,6},{5,7},{6,4},{7,5},{8,10},{9,11},{10,... | collective-permute-start | bytes 1425416 | tf_op jit(solution)/shard_map/ppermute | solution.py:93
  15.2 14.1 %collective-permute-start.1 = (bf16[64,3712]{1,0:T(8,128)(2,1)S(1)}, bf16[64,3712]{1,0:T(8,128)(2,1)S(1)}, u32[]{:S(2)}, u32[]{:S(2)}) collective-permute-start(bf16[64,3712]{1,0:T(8,128)(2,1)S(1)} %pad_maximum_fusion.refs_3_), channel_id=1, source_target_pairs={{0,1},{1,0},{2,3},{3,2},{4,5},{5,4},{6,7},{7,6},{8,9},{9,8},{10,11... | collective-permute-start | bytes 1425416 | tf_op jit(solution)/shard_map/ppermute | solution.py:93
  25.7 14.2 %copy-start.16 = (bf16[64,3712]{1,0:T(8,128)(2,1)}, bf16[64,3712]{1,0:T(8,128)(2,1)S(1)}, u32[]{:S(2)}) copy-start(bf16[64,3712]{1,0:T(8,128)(2,1)S(1)} %collective-permute-done.3.refs_3_) | copy-start | bytes 1425412
  25.7 3.5 %collective-permute-start.4 = (bf16[64,3712]{1,0:T(8,128)(2,1)S(1)}, bf16[64,3712]{1,0:T(8,128)(2,1)S(1)}, u32[]{:S(2)}, u32[]{:S(2)}) collective-permute-start(bf16[64,3712]{1,0:T(8,128)(2,1)S(1)} %collective-permute-done.2.refs_4_), channel_id=1, source_target_pairs={{0,1},{1,0},{2,3},{3,2},{4,5},{5,4},{6,7},{7,6},{8,9},{9,8},{10,11... | collective-permute-start | bytes 1425416 | tf_op jit(solution)/shard_map/ppermute | solution.py:93
  25.8 14.1 %collective-permute-start.6 = (bf16[64,3712]{1,0:T(8,128)(2,1)S(1)}, bf16[64,3712]{1,0:T(8,128)(2,1)S(1)}, u32[]{:S(2)}, u32[]{:S(2)}) collective-permute-start(bf16[64,3712]{1,0:T(8,128)(2,1)S(1)} %collective-permute-done.3.refs_3_), channel_id=1, source_target_pairs={{0,2},{1,3},{2,0},{3,1},{4,6},{5,7},{6,4},{7,5},{8,10},{9,11},{10,... | collective-permute-start | bytes 1425416 | tf_op jit(solution)/shard_map/ppermute | solution.py:93
  27.4 24.0 %collective-permute-start.9 = (bf16[64,3712]{1,0:T(8,128)(2,1)S(1)}, bf16[64,3712]{1,0:T(8,128)(2,1)S(1)}, u32[]{:S(2)}, u32[]{:S(2)}) collective-permute-start(bf16[64,3712]{1,0:T(8,128)(2,1)S(1)} %pad_maximum_fusion.refs_3_), channel_id=1, source_target_pairs={{0,8},{1,9},{2,10},{3,11},{4,12},{5,13},{6,14},{7,15},{8,0},{9,1},... | collective-permute-start | bytes 1425416 | tf_op jit(solution)/shard_map/ppermute | solution.py:93
  39.9 13.9 %copy-start.18 = (bf16[64,3712]{1,0:T(8,128)(2,1)}, bf16[64,3712]{1,0:T(8,128)(2,1)S(1)}, u32[]{:S(2)}) copy-start(bf16[64,3712]{1,0:T(8,128)(2,1)S(1)} %collective-permute-done.6.refs_4_) | copy-start | bytes 1425412
  39.9 11.5 %collective-permute-start.7 = (bf16[64,3712]{1,0:T(8,128)(2,1)S(1)}, bf16[64,3712]{1,0:T(8,128)(2,1)S(1)}, u32[]{:S(2)}, u32[]{:S(2)}) collective-permute-start(bf16[64,3712]{1,0:T(8,128)(2,1)S(1)} %collective-permute-done.3.refs_3_), channel_id=1, source_target_pairs={{0,1},{1,0},{2,3},{3,2},{4,5},{5,4},{6,7},{7,6},{8,9},{9,8},{10,11... | collective-permute-start | bytes 1425416 | tf_op jit(solution)/shard_map/ppermute | solution.py:93
  40.0 11.4 %collective-permute-start.8 = (bf16[64,3712]{1,0:T(8,128)(2,1)S(1)}, bf16[64,3712]{1,0:T(8,128)(2,1)S(1)}, u32[]{:S(2)}, u32[]{:S(2)}) collective-permute-start(bf16[64,3712]{1,0:T(8,128)(2,1)S(1)} %collective-permute-done.6.refs_4_), channel_id=1, source_target_pairs={{0,1},{1,0},{2,3},{3,2},{4,5},{5,4},{6,7},{7,6},{8,9},{9,8},{10,11... | collective-permute-start | bytes 1425416 | tf_op jit(solution)/shard_map/ppermute | solution.py:93
  40.4 29.0 %collective-permute-start.5 = (bf16[3,192,1024]{2,1,0:T(8,128)(2,1)}, bf16[3,192,1024]{2,1,0:T(8,128)(2,1)S(1)}, u32[]{:S(2)}, u32[]{:S(2)}) collective-permute-start(bf16[3,192,1024]{2,1,0:T(8,128)(2,1)} %get-tuple-element.180), channel_id=1, source_target_pairs={{0,16},{16,0},{1,17},{17,1},{2,18},{18,2},{3,19},{19,3},{4,20},{20... | collective-permute-start | bytes 3538952 | tf_op jit(solution)/shard_map/ppermute | solution.py:32
  51.4 12.5 %copy-start.14 = (bf16[64,3712]{1,0:T(8,128)(2,1)}, bf16[64,3712]{1,0:T(8,128)(2,1)S(1)}, u32[]{:S(2)}) copy-start(bf16[64,3712]{1,0:T(8,128)(2,1)S(1)} %collective-permute-done.9.refs_3_) | copy-start | bytes 1425412
  51.4 12.5 %collective-permute-start.10 = (bf16[64,3712]{1,0:T(8,128)(2,1)S(1)}, bf16[64,3712]{1,0:T(8,128)(2,1)S(1)}, u32[]{:S(2)}, u32[]{:S(2)}) collective-permute-start(bf16[64,3712]{1,0:T(8,128)(2,1)S(1)} %collective-permute-done.9.refs_3_), channel_id=1, source_target_pairs={{0,2},{1,3},{2,0},{3,1},{4,6},{5,7},{6,4},{7,5},{8,10},{9,11},{10,... | collective-permute-start | bytes 1425416 | tf_op jit(solution)/shard_map/ppermute | solution.py:93
  52.0 14.6 %collective-permute-start.15 = (bf16[64,3712]{1,0:T(8,128)(2,1)}, bf16[64,3712]{1,0:T(8,128)(2,1)S(1)}, u32[]{:S(2)}, u32[]{:S(2)}) collective-permute-start(bf16[64,3712]{1,0:T(8,128)(2,1)} %copy-done), channel_id=1, source_target_pairs={{0,12},{1,13},{2,14},{3,15},{4,0},{5,1},{6,2},{7,3},{8,4},{9,5},{1... | collective-permute-start | bytes 1425416 | tf_op jit(solution)/shard_map/ppermute | solution.py:93
  63.9 5.6 %collective-permute-start.11 = (bf16[64,3712]{1,0:T(8,128)(2,1)S(1)}, bf16[64,3712]{1,0:T(8,128)(2,1)S(1)}, u32[]{:S(2)}, u32[]{:S(2)}) collective-permute-start(bf16[64,3712]{1,0:T(8,128)(2,1)S(1)} %collective-permute-done.9.refs_3_), channel_id=1, source_target_pairs={{0,1},{1,0},{2,3},{3,2},{4,5},{5,4},{6,7},{7,6},{8,9},{9,8},{10,11... | collective-permute-start | bytes 1425416 | tf_op jit(solution)/shard_map/ppermute | solution.py:93
  63.9 5.6 %collective-permute-start.12 = (bf16[64,3712]{1,0:T(8,128)(2,1)S(1)}, bf16[64,3712]{1,0:T(8,128)(2,1)S(1)}, u32[]{:S(2)}, u32[]{:S(2)}) collective-permute-start(bf16[64,3712]{1,0:T(8,128)(2,1)S(1)} %collective-permute-done.10.refs_4_), channel_id=1, source_target_pairs={{0,1},{1,0},{2,3},{3,2},{4,5},{5,4},{6,7},{7,6},{8,9},{9,8},{10,11... | collective-permute-start | bytes 1425416 | tf_op jit(solution)/shard_map/ppermute | solution.py:93
  64.4 30.3 %collective-permute-start.19 = (bf16[3,192,1024]{2,1,0:T(8,128)(2,1)}, bf16[3,192,1024]{2,1,0:T(8,128)(2,1)S(1)}, u32[]{:S(2)}, u32[]{:S(2)}) collective-permute-start(bf16[3,192,1024]{2,1,0:T(8,128)(2,1)} %get-tuple-element.191), channel_id=1, source_target_pairs={{0,16},{16,0},{1,17},{17,1},{2,18},{18,2},{3,19},{19,3},{4,20},{20... | collective-permute-start | bytes 3538952 | tf_op jit(solution)/shard_map/ppermute | solution.py:32
  66.6 21.1 %copy-start.13 = (bf16[64,3712]{1,0:T(8,128)(2,1)}, bf16[64,3712]{1,0:T(8,128)(2,1)S(1)}, u32[]{:S(2)}) copy-start(bf16[64,3712]{1,0:T(8,128)(2,1)S(1)} %collective-permute-done.15.refs_3_) | copy-start | bytes 1425412
  66.6 21.1 %collective-permute-start.16 = (bf16[64,3712]{1,0:T(8,128)(2,1)S(1)}, bf16[64,3712]{1,0:T(8,128)(2,1)S(1)}, u32[]{:S(2)}, u32[]{:S(2)}) collective-permute-start(bf16[64,3712]{1,0:T(8,128)(2,1)S(1)} %collective-permute-done.15.refs_3_), channel_id=1, source_target_pairs={{0,2},{1,3},{2,0},{3,1},{4,6},{5,7},{6,4},{7,5},{8,10},{9,11},{10,... | collective-permute-start | bytes 1425416 | tf_op jit(solution)/shard_map/ppermute | solution.py:93
  85.9 2.2 %collective-permute-start.13 = (bf16[64,3712]{1,0:T(8,128)(2,1)}, bf16[64,3712]{1,0:T(8,128)(2,1)S(1)}, u32[]{:S(2)}, u32[]{:S(2)}) collective-permute-start(bf16[64,3712]{1,0:T(8,128)(2,1)} %get-tuple-element.204), channel_id=1, source_target_pairs={{0,1},{1,0},{2,3},{3,2},{4,5},{5,4},{6,7},{7,6},{8,9},{9,8},{10,11... | collective-permute-start | bytes 1425416 | tf_op jit(solution)/shard_map/ppermute | solution.py:93
  85.9 34.1 %collective-permute-start.18 = (bf16[3,192,1024]{2,1,0:T(8,128)(2,1)}, bf16[3,192,1024]{2,1,0:T(8,128)(2,1)S(1)}, u32[]{:S(2)}, u32[]{:S(2)}) collective-permute-start(bf16[3,192,1024]{2,1,0:T(8,128)(2,1)} %get-tuple-element.209), channel_id=1, source_target_pairs={{0,16},{16,0},{1,17},{17,1},{2,18},{18,2},{3,19},{19,3},{4,20},{20... | collective-permute-start | bytes 3538952 | tf_op jit(solution)/shard_map/ppermute | solution.py:32
  87.5 2.1 %collective-permute-start.14 = (bf16[64,3712]{1,0:T(8,128)(2,1)}, bf16[64,3712]{1,0:T(8,128)(2,1)S(1)}, u32[]{:S(2)}, u32[]{:S(2)}) collective-permute-start(bf16[64,3712]{1,0:T(8,128)(2,1)} %get-tuple-element.206), channel_id=1, source_target_pairs={{0,1},{1,0},{2,3},{3,2},{4,5},{5,4},{6,7},{7,6},{8,9},{9,8},{10,11... | collective-permute-start | bytes 1425416 | tf_op jit(solution)/shard_map/ppermute | solution.py:93
  87.7 7.1 %collective-permute-start.20 = (bf16[64,3712]{1,0:T(8,128)(2,1)S(1)}, bf16[64,3712]{1,0:T(8,128)(2,1)S(1)}, u32[]{:S(2)}, u32[]{:S(2)}) collective-permute-start(bf16[64,3712]{1,0:T(8,128)(2,1)S(1)} %collective-permute-done.15.refs_3_), channel_id=1, source_target_pairs={{0,1},{1,0},{2,3},{3,2},{4,5},{5,4},{6,7},{7,6},{8,9},{9,8},{10,11... | collective-permute-start | bytes 1425416 | tf_op jit(solution)/shard_map/ppermute | solution.py:93
  88.1 6.7 %collective-permute-start.21 = (bf16[64,3712]{1,0:T(8,128)(2,1)S(1)}, bf16[64,3712]{1,0:T(8,128)(2,1)S(1)}, u32[]{:S(2)}, u32[]{:S(2)}) collective-permute-start(bf16[64,3712]{1,0:T(8,128)(2,1)S(1)} %collective-permute-done.16.refs_4_), channel_id=1, source_target_pairs={{0,1},{1,0},{2,3},{3,2},{4,5},{5,4},{6,7},{7,6},{8,9},{9,8},{10,11... | collective-permute-start | bytes 1425416 | tf_op jit(solution)/shard_map/ppermute | solution.py:93
  96.1 15.6 %copy-start.39 = (bf16[64,3712]{1,0:T(8,128)(2,1)S(1)}, bf16[64,3712]{1,0:T(8,128)(2,1)}, u32[]{:S(2)}) copy-start(bf16[64,3712]{1,0:T(8,128)(2,1)} %get-tuple-element.218) | copy-start | bytes 1425412
  111.1 2.6 %collective-permute-start.22 = (bf16[64,3712]{1,0:T(8,128)(2,1)}, bf16[64,3712]{1,0:T(8,128)(2,1)S(1)}, u32[]{:S(2)}, u32[]{:S(2)}) collective-permute-start(bf16[64,3712]{1,0:T(8,128)(2,1)} %get-tuple-element.231), channel_id=1, source_target_pairs={{0,1},{1,0},{2,3},{3,2},{4,5},{5,4},{6,7},{7,6},{8,9},{9,8},{10,11... | collective-permute-start | bytes 1425416 | tf_op jit(solution)/shard_map/ppermute | solution.py:93
  111.2 2.7 %collective-permute-start.23 = (bf16[64,3712]{1,0:T(8,128)(2,1)}, bf16[64,3712]{1,0:T(8,128)(2,1)S(1)}, u32[]{:S(2)}, u32[]{:S(2)}) collective-permute-start(bf16[64,3712]{1,0:T(8,128)(2,1)} %get-tuple-element.233), channel_id=1, source_target_pairs={{0,1},{1,0},{2,3},{3,2},{4,5},{5,4},{6,7},{7,6},{8,9},{9,8},{10,11... | collective-permute-start | bytes 1425416 | tf_op jit(solution)/shard_map/ppermute | solution.py:93
  111.7 20.7 %collective-permute-start.17 = (bf16[64,3712]{1,0:T(8,128)(2,1)S(1)}, bf16[64,3712]{1,0:T(8,128)(2,1)S(1)}, u32[]{:S(2)}, u32[]{:S(2)}) collective-permute-start(bf16[64,3712]{1,0:T(8,128)(2,1)S(1)} %copy-done.39), channel_id=1, source_target_pairs={{0,2},{1,3},{2,0},{3,1},{4,6},{5,7},{6,4},{7,5},{8,10},{9,11},{10,... | collective-permute-start | bytes 1425416 | tf_op jit(solution)/shard_map/ppermute | solution.py:93
  112.3 32.2 %collective-permute-start.25 = (bf16[3,192,1024]{2,1,0:T(8,128)(2,1)}, bf16[3,192,1024]{2,1,0:T(8,128)(2,1)S(1)}, u32[]{:S(2)}, u32[]{:S(2)}) collective-permute-start(bf16[3,192,1024]{2,1,0:T(8,128)(2,1)} %get-tuple-element.234), channel_id=1, source_target_pairs={{0,16},{16,0},{1,17},{17,1},{2,18},{18,2},{3,19},{19,3},{4,20},{20... | collective-permute-start | bytes 3538952 | tf_op jit(solution)/shard_map/ppermute | solution.py:32
  117.3 27.1 %collective-permute-start.24 = (bf16[64,3712]{1,0:T(8,128)(2,1)}, bf16[64,3712]{1,0:T(8,128)(2,1)S(1)}, u32[]{:S(2)}, u32[]{:S(2)}) collective-permute-start(bf16[64,3712]{1,0:T(8,128)(2,1)} %get-tuple-element.252), channel_id=1, source_target_pairs={{0,2},{1,3},{2,0},{3,1},{4,6},{5,7},{6,4},{7,5},{8,10},{9,11},{10,... | collective-permute-start | bytes 1425416 | tf_op jit(solution)/shard_map/ppermute | solution.py:93
  121.1 11.4 %copy-start.5 = (f32[64,3712]{1,0:T(8,128)S(1)}, f32[64,3712]{1,0:T(8,128)}, u32[]{:S(2)}) copy-start(f32[64,3712]{1,0:T(8,128)} %get-tuple-element.250) | copy-start | bytes 2850820
  131.8 12.6 %copy-start.6 = (f32[64,3712]{1,0:T(8,128)S(1)}, f32[64,3712]{1,0:T(8,128)}, u32[]{:S(2)}) copy-start(f32[64,3712]{1,0:T(8,128)} %get-tuple-element.261) | copy-start | bytes 2850820
  131.8 2.1 %collective-permute-start.26 = (bf16[64,3712]{1,0:T(8,128)(2,1)}, bf16[64,3712]{1,0:T(8,128)(2,1)S(1)}, u32[]{:S(2)}, u32[]{:S(2)}) collective-permute-start(bf16[64,3712]{1,0:T(8,128)(2,1)} %get-tuple-element.248), channel_id=1, source_target_pairs={{0,1},{1,0},{2,3},{3,2},{4,5},{5,4},{6,7},{7,6},{8,9},{9,8},{10,11... | collective-permute-start | bytes 1425416 | tf_op jit(solution)/shard_map/ppermute | solution.py:93
  131.9 2.7 %collective-permute-start.27 = (bf16[64,3712]{1,0:T(8,128)(2,1)}, bf16[64,3712]{1,0:T(8,128)(2,1)S(1)}, u32[]{:S(2)}, u32[]{:S(2)}) collective-permute-start(bf16[64,3712]{1,0:T(8,128)(2,1)} %get-tuple-element.249), channel_id=1, source_target_pairs={{0,1},{1,0},{2,3},{3,2},{4,5},{5,4},{6,7},{7,6},{8,9},{9,8},{10,11... | collective-permute-start | bytes 1425416 | tf_op jit(solution)/shard_map/ppermute | solution.py:93
  144.5 13.3 %collective-permute-start.28 = (bf16[64,3712]{1,0:T(8,128)(2,1)S(1)}, bf16[64,3712]{1,0:T(8,128)(2,1)S(1)}, u32[]{:S(2)}, u32[]{:S(2)}) collective-permute-start(bf16[64,3712]{1,0:T(8,128)(2,1)S(1)} %add_convert_fusion.2), channel_id=1, source_target_pairs={{0,12},{1,13},{2,14},{3,15},{4,0},{5,1},{6,2},{7,3},{8,4},{9,5},{1... | collective-permute-start | bytes 1425416 | tf_op jit(solution)/shard_map/ppermute | solution.py:93
  146.0 12.0 %collective-permute-start.29 = (bf16[64,3712]{1,0:T(8,128)(2,1)}, bf16[64,3712]{1,0:T(8,128)(2,1)S(1)}, u32[]{:S(2)}, u32[]{:S(2)}) collective-permute-start(bf16[64,3712]{1,0:T(8,128)(2,1)} %get-tuple-element.272), channel_id=1, source_target_pairs={{0,2},{1,3},{2,0},{3,1},{4,6},{5,7},{6,4},{7,5},{8,10},{9,11},{10,... | collective-permute-start | bytes 1425416 | tf_op jit(solution)/shard_map/ppermute | solution.py:93
  147.0 10.9 %copy-start.7 = (f32[64,3712]{1,0:T(8,128)S(1)}, f32[64,3712]{1,0:T(8,128)}, u32[]{:S(2)}) copy-start(f32[64,3712]{1,0:T(8,128)} %get-tuple-element.273) | copy-start | bytes 2850820
  157.7 2.8 %collective-permute-start.31 = (bf16[128,3712]{1,0:T(8,128)(2,1)}, bf16[128,3712]{1,0:T(8,128)(2,1)S(1)}, u32[]{:S(2)}, u32[]{:S(2)}) collective-permute-start(bf16[128,3712]{1,0:T(8,128)(2,1)} %get-tuple-element.270), channel_id=1, source_target_pairs={{0,1},{1,0},{2,3},{3,2},{4,5},{5,4},{6,7},{7,6},{8,9},{9,8},{10,11... | collective-permute-start | bytes 2850824 | tf_op jit(solution)/shard_map/ppermute | solution.py:93
  158.1 24.1 %collective-permute-start.30 = (bf16[64,3712]{1,0:T(8,128)(2,1)S(1)}, bf16[64,3712]{1,0:T(8,128)(2,1)S(1)}, u32[]{:S(2)}, u32[]{:S(2)}) collective-permute-start(bf16[64,3712]{1,0:T(8,128)(2,1)S(1)} %add_convert_fusion.1), channel_id=1, source_target_pairs={{0,8},{1,9},{2,10},{3,11},{4,12},{5,13},{6,14},{7,15},{8,0},{9,1},... | collective-permute-start | bytes 1425416 | tf_op jit(solution)/shard_map/ppermute | solution.py:93
  161.0 13.0 %collective-permute-start.32 = (bf16[64,3712]{1,0:T(8,128)(2,1)S(1)}, bf16[64,3712]{1,0:T(8,128)(2,1)S(1)}, u32[]{:S(2)}, u32[]{:S(2)}) collective-permute-start(bf16[64,3712]{1,0:T(8,128)(2,1)S(1)} %slice.112), channel_id=1, source_target_pairs={{0,2},{1,3},{2,0},{3,1},{4,6},{5,7},{6,4},{7,5},{8,10},{9,11},{10,... | collective-permute-start | bytes 1425416 | tf_op jit(solution)/shard_map/ppermute | solution.py:93
  167.0 7.2 %copy-start.10 = (bf16[192,1792]{1,0:T(8,128)(2,1)S(1)}, bf16[192,1792]{1,0:T(8,128)(2,1)}, u32[]{:S(2)}) copy-start(bf16[192,1792]{1,0:T(8,128)(2,1)} %get-tuple-element.305) | copy-start | bytes 2064388
  167.0 7.2 %copy-start.11 = (bf16[192,1792]{1,0:T(8,128)(2,1)S(1)}, bf16[192,1792]{1,0:T(8,128)(2,1)}, u32[]{:S(2)}) copy-start(bf16[192,1792]{1,0:T(8,128)(2,1)} %get-tuple-element.306) | copy-start | bytes 2064388
  182.5 11.4 %collective-permute-start.35 = (bf16[32,3712]{1,0:T(8,128)(2,1)S(1)}, bf16[32,3712]{1,0:T(8,128)(2,1)S(1)}, u32[]{:S(2)}, u32[]{:S(2)}) collective-permute-start(bf16[32,3712]{1,0:T(8,128)(2,1)S(1)} %get-tuple-element.332), channel_id=1, source_target_pairs={{0,20},{1,21},{2,22},{3,23},{4,24},{5,25},{6,26},{7,27},{8,28},{9,... | collective-permute-start | bytes 712712 | tf_op jit(solution)/shard_map/ppermute | solution.py:105
  182.6 15.6 %collective-permute-start.34 = (bf16[32,3712]{1,0:T(8,128)(2,1)S(1)}, bf16[32,3712]{1,0:T(8,128)(2,1)S(1)}, u32[]{:S(2)}, u32[]{:S(2)}) collective-permute-start(bf16[32,3712]{1,0:T(8,128)(2,1)S(1)} %get-tuple-element.333), channel_id=1, source_target_pairs={{0,4},{1,5},{2,6},{3,7},{4,8},{5,9},{6,10},{7,11},{8,12},{9,13},{1... | collective-permute-start | bytes 712712 | tf_op jit(solution)/shard_map/ppermute | solution.py:105
  183.6 14.9 %copy-start.34 = (s32[32,8]{0,1:T(8,128)S(1)}, s32[32,8]{0,1:T(8,128)}, u32[]{:S(2)}) copy-start(s32[32,8]{0,1:T(8,128)} %param.10) | copy-start | bytes 3076
  183.6 14.6 %collective-permute-start.33 = (bf16[32,3712]{1,0:T(8,128)(2,1)S(1)}, bf16[32,3712]{1,0:T(8,128)(2,1)S(1)}, u32[]{:S(2)}, u32[]{:S(2)}) collective-permute-start(bf16[32,3712]{1,0:T(8,128)(2,1)S(1)} %select_convert_fusion), channel_id=1, source_target_pairs={{0,16},{16,0},{1,17},{17,1},{2,18},{18,2},{3,19},{19,3},{4,20},{20... | collective-permute-start | bytes 712712 | tf_op jit(solution)/shard_map/ppermute | solution.py:32
  (40 other events, 102.9 us)

commit v4 on v3

--- a/solution.py
+++ b/solution.py
@@ -516,7 +516,7 @@
     def next_outer(number):
         mine, arrived = order.enter(*moving[number])
         (total,) = merge([mine] + arrived, 1)
-        if number and number == last:
+        if number and number >= last - 1:
             total = total.astype(BF)
             order.leave(total)
             parts = [total[g * rows : (g + 1) * rows] for g in range(groups)]
@@ -564,6 +564,13 @@
         if number < last:
             next_inner(number)
     add_up(range(1, last - 1))
+    (arrived,) = order.enter([finals[k] for k in sorted(finals) if k < max(1, last - 1)])
+    total = add_all(arrived[0].astype(F32), arrived[1:])
+    sums_here = [total[g * rows : (g + 1) * rows] for g in range(groups)]
+    by_step = [choose(sums_here, mine_dp)]
+    for step in range(1, groups):
+        by_step.append(shift_dp(choose(sums_here, (mine_dp + step) % groups).astype(BF), step))
+    order.leave(total)
     if last > 1:
         next_outer(last - 1)
     next_inner(last)
@@ -582,20 +589,15 @@
     x_all = joined(x_all)
     gate_grad = dot_tn(x_all, joined(gate_all)).astype(BF)[None]
     order.leave(gate_grad)
-    straight = finals.pop(last) if last else None
-    (arrived,) = order.enter(list(finals.values()))
-    total = add_all(arrived[0].astype(F32), arrived[1:])
-    sums_here = [total[g * rows : (g + 1) * rows] for g in range(groups)]
-    by_step = [choose(sums_here, mine_dp)]
-    for step in range(1, groups):
-        by_step.append(shift_dp(choose(sums_here, (mine_dp + step) % groups).astype(BF), step))
-    order.leave(total)
+    arrivals = [finals.pop(number) for number in range(max(1, last - 1), last + 1)]
     x_all, up_all = order.enter(x_all, rows_of(ends, 2))
     up_grad = dot_tn(x_all, joined(up_all)).astype(BF)[None]
     order.leave(up_grad)
-    if last:
-        by_step, straight = order.enter(by_step, straight)
-        by_step = [value.astype(F32) + add.astype(F32) for value, add in zip(by_step, straight)]
+    by_step, arrivals = order.enter(by_step, arrivals)
+    by_step = [
+        add_all(value.astype(F32), [sent[step] for sent in arrivals])
+        for step, value in enumerate(by_step)
+    ]
     by_step = [value.astype(BF) for value in by_step]
     parts = [choose(by_step, (mine_dp - g) % groups) for g in range(groups)]
     mixed = jnp.concatenate([value[:, :part] for value in parts], axis=1)

time: 201 us -> 197 us (0.980)
  waiting for transfers between devices: 61.1 us -> 52.7 us
  starting transfers between devices: 30.4 us -> 35 us
    ppermute x28 -> x27, waiting for transfers between devices: 34.8 us -> 29.7 us  [shift_expert(): return lax.ppermute(value, 'expert', pairs)]
    ppermute x2 -> x4, starting transfers between devices: 1.11 us -> 5.43 us  [shift_to_owner(): return lax.ppermute(value, ('dp', 'expert'), pairs)]
    ppermute x2 -> x4, waiting for transfers between devices: 9.41 us -> 6.18 us  [shift_to_owner(): return lax.ppermute(value, ('dp', 'expert'), pairs)]
    ppermute x28 -> x27, starting transfers between devices: 19.6 us -> 18.9 us  [shift_expert(): return lax.ppermute(value, 'expert', pairs)]
  transfers between devices with their start and end apart: 36 -> 37, of which waited for: 17 -> 14; matrix products, arithmetic and copies ran while one was open for 8% -> 8% of each run, Pallas kernels for 39% -> 40%
where the time goes in v4:
time: 197 us; the launch traced here: 196 us
  Pallas kernels  78.8 us (40%)
  waiting for transfers between devices  52.7 us (27%)
  starting transfers between devices  35 us (18%)
  matrix products  14 us (7%)
  local copies, waits for them, and re-layouts  9.71 us (5%)
  other arithmetic  4.86 us (2%)
    pallas_call x2, Pallas kernels, finish_and_project(): pl.pallas_call(body, grid=(hidden // tile,), in_specs=[pl.BlockSpec(memor...  30.1 us
    ppermute x27, waiting for transfers between devices, shift_expert(): return lax.ppermute(value, 'expert', pairs)  29.7 us
    pallas_call x2, Pallas kernels, finish(): pl.pallas_call(lambda *refs: finish_body(len(sent), number_parts, *refs),...  21.5 us
    pallas_call x2, Pallas kernels, project(): pl.pallas_call(lambda *refs: project_body(len(parts), part, experts, *ref...  19.3 us
    ppermute x27, starting transfers between devices, shift_expert(): return lax.ppermute(value, 'expert', pairs)  18.9 us
    ppermute x6, waiting for transfers between devices, shift_dp(): lax.ppermute(value, 'dp', [(i, (i + step) % groups) for i in range(groups)])  16.9 us
    dot_general x3, matrix products, dot_tn(): lax.dot_general(first, second, (((0,), (0,)), ((), ())), preferred_elemen...  14 us
    ppermute x6, starting transfers between devices, shift_dp(): lax.ppermute(value, 'dp', [(i, (i + step) % groups) for i in range(groups)])  10.6 us
  transfers between devices with their start and end apart: 37, of which 14 were waited for; matrix products, arithmetic and copies ran while one was open for 8% of the time, Pallas kernels for 40%

profile of v4, /device:TPU:0, one launch (start us, length us, event | category | flops | bytes accessed | tf_op | source)
XLA Modules:
  0.0 196.3 jit_solution(18441546625993534394)
XLA Ops:
  1.5 1.1 fusion.39
  2.9 3.0 %collective-permute-start = (bf16[32,3712]{1,0:T(8,128)(2,1)S(1)}, bf16[32,3712]{1,0:T(8,128)(2,1)S(1)}, u32[]{:S(2)}, u32[]{:S(2)}) collective-permute-start(bf16[32,3712]{1,0:T(8,128)(2,1)S(1)} %broadcast_select_fusion.4), channel_id=1, source_target_pairs={{0,16},{16,0},{1,17},{17,1},{2,18},{18,2},{3,19},{19,3},{4,20},{20... | collective-permute-start | bytes 712712 | tf_op jit(solution)/shard_map/ppermute | solution.py:32
  5.9 5.8 %collective-permute-done = bf16[32,3712]{1,0:T(8,128)(2,1)S(1)} collective-permute-done((bf16[32,3712]{1,0:T(8,128)(2,1)S(1)}, bf16[32,3712]{1,0:T(8,128)(2,1)S(1)}, u32[]{:S(2)}, u32[]{:S(2)}) %collective-permute-start) | collective-permute-done | bytes 237600 | tf_op jit(solution)/shard_map/ppermute | solution.py:32
  11.8 1.9 collective-permute-start.3
  13.7 1.5 collective-permute-start.2
  15.2 10.5 %collective-permute-done.3.refs_3_ = bf16[64,3712]{1,0:T(8,128)(2,1)S(1)} collective-permute-done((bf16[64,3712]{1,0:T(8,128)(2,1)S(1)}, bf16[64,3712]{1,0:T(8,128)(2,1)S(1)}, u32[]{:S(2)}, u32[]{:S(2)}) %collective-permute-start.3) | collective-permute-done | bytes 475168 | tf_op jit(solution)/shard_map/ppermute | solution.py:93
  25.8 1.6 collective-permute-start.6
  27.4 1.9 collective-permute-start.9
  30.2 9.6 %project.2 = (bf16[192,1792]{1,0:T(8,128)(2,1)}, bf16[192,1792]{1,0:T(8,128)(2,1)}, bf16[192,1792]{1,0:T(8,128)(2,1)}, f32[192,128]{1,0:T(8,128)}, bf16[192,256]...) custom-call(s32[1,1]{1,0:T(1,128)} %bitcast.refs_0_, ...), custom_call_target="tpu_custom_call" | custom-call | tf_op jit(solution)/shard_map/project/pallas_call | solution.py:179
  40.5 1.5 collective-permute-start.5
  42.0 9.4 %collective-permute-done.9.refs_3_ = bf16[64,3712]{1,0:T(8,128)(2,1)S(1)} collective-permute-done((bf16[64,3712]{1,0:T(8,128)(2,1)S(1)}, bf16[64,3712]{1,0:T(8,128)(2,1)S(1)}, u32[]{:S(2)}, u32[]{:S(2)}) %collective-permute-start.9) | collective-permute-done | bytes 475168 | tf_op jit(solution)/shard_map/ppermute | solution.py:93
  52.0 1.7 collective-permute-start.15
  53.7 9.7 %project.3 = (bf16[192,1792]{1,0:T(8,128)(2,1)}, bf16[192,1792]{1,0:T(8,128)(2,1)}, bf16[192,1792]{1,0:T(8,128)(2,1)}, f32[192,128]{1,0:T(8,128)}, bf16[192,256]...) custom-call(s32[1,1]{1,0:T(1,128)} %bitcast.refs_0_, ...), custom_call_target="tpu_custom_call" | custom-call | tf_op jit(solution)/shard_map/project/pallas_call | solution.py:179
  64.4 1.5 collective-permute-start.19
  66.6 1.1 collective-permute-start.16
  67.7 1.8 collective-permute-done.5.refs_8_
  69.5 1.0 copy-done.4
  70.8 15.1 %step.2 = (bf16[192,1792]{1,0:T(8,128)(2,1)}, bf16[192,1792]{1,0:T(8,128)(2,1)}, bf16[192,1792]{1,0:T(8,128)(2,1)}, f32[192,128]{1,0:T(8,128)}, bf16[192,256]{1,...) custom-call(s32[1,1]{1,0:T(1,128)} %bitcast.refs_0_, ...), custom_call_target="tpu_custom_call" | custom-call | tf_op jit(solution)/shard_map/step/pallas_call | solution.py:330
  86.0 1.6 collective-permute-start.18
  88.3 1.3 collective-permute-done.14.refs_3_
  89.6 0.8 copy-done.28
  90.4 2.7 %merge.3 = (f32[64,3712]{1,0:T(8,128)}, bf16[64,3712]{1,0:T(8,128)(2,1)}) custom-call(bf16[64,3712]{1,0:T(8,128)(2,1)} %get-tuple-element.213.refs_0_, bf16[64,3712]{1,0:T(8,128)(2,1)} %copy-done.27, bf16[64,3712]{1,0:T(8,128)(2,1)} %get-tuple-element.215.refs_2_, bf16[64,3712]{1,0:T(8,128)(2,1)} %copy-done.28), custom_call_target="tpu_custom_call" | custom-call | tf_op jit(solution)/shard_map/merge/pallas_call | solution.py:216
  93.0 1.7 collective-permute-done.19.refs_8_
  94.8 1.0 copy-done.3
  96.1 15.1 %step.3 = (bf16[192,1792]{1,0:T(8,128)(2,1)}, bf16[192,1792]{1,0:T(8,128)(2,1)}, bf16[192,1792]{1,0:T(8,128)(2,1)}, f32[192,128]{1,0:T(8,128)}, bf16[192,256]{1,...) custom-call(s32[1,1]{1,0:T(1,128)} %bitcast.refs_0_, ...), custom_call_target="tpu_custom_call" | custom-call | tf_op jit(solution)/shard_map/step/pallas_call | solution.py:330
  112.3 1.5 collective-permute-start.25
  114.7 2.6 %merge.4 = (f32[64,3712]{1,0:T(8,128)}, bf16[64,3712]{1,0:T(8,128)(2,1)}) custom-call(bf16[64,3712]{1,0:T(8,128)(2,1)} %get-tuple-element.236.refs_0_, bf16[64,3712]{1,0:T(8,128)(2,1)} %copy-done.29, bf16[64,3712]{1,0:T(8,128)(2,1)} %get-tuple-element.238.refs_2_, bf16[64,3712]{1,0:T(8,128)(2,1)} %copy-done.32), custom_call_target="tpu_custom_call" | custom-call | tf_op jit(solution)/shard_map/merge/pallas_call | solution.py:216
  117.4 1.5 collective-permute-start.24
  118.8 1.2 collective-permute-done.18.refs_1_
  120.1 1.0 copy-done.1
  121.1 10.8 %finish.2 = (bf16[192,1024]{1,0:T(8,128)(2,1)}, bf16[192,1024]{1,0:T(8,128)(2,1)}, bf16[192,1024]{1,0:T(8,128)(2,1)}, bf16[64,3712]{1,0:T(8,128)(2,1)}, bf16[64,...) custom-call(f32[3,192,1024]{2,1,0:T(8,128)} %get-tuple-element.242.refs_0_, ...), custom_call_target="tpu_custom_call" | custom-call | tf_op jit(solution)/shard_map/finish/pallas_call | solution.py:294
  132.5 1.5 collective-permute-done.26.refs_1_
  135.5 2.6 %merge.5 = (f32[64,3712]{1,0:T(8,128)}, bf16[64,3712]{1,0:T(8,128)(2,1)}) custom-call(bf16[64,3712]{1,0:T(8,128)(2,1)} %get-tuple-element.255.refs_0_, bf16[64,3712]{1,0:T(8,128)(2,1)} %copy-done.31, bf16[64,3712]{1,0:T(8,128)(2,1)} %get-tuple-element.257.refs_2_, bf16[64,3712]{1,0:T(8,128)(2,1)} %copy-done.33), custom_call_target="tpu_custom_call" | custom-call | tf_op jit(solution)/shard_map/merge/pallas_call | solution.py:216
  138.1 6.3 %collective-permute-done.25.refs_1_ = bf16[3,192,1024]{2,1,0:T(8,128)(2,1)S(1)} collective-permute-done((bf16[3,192,1024]{2,1,0:T(8,128)(2,1)}, bf16[3,192,1024]{2,1,0:T(8,128)(2,1)S(1)}, u32[]{:S(2)}, u32[]{:S(2)}) %collective-permute-start.25) | collective-permute-done | bytes 1179680 | tf_op jit(solution)/shard_map/ppermute | solution.py:32
  144.6 1.4 collective-permute-start.28
  146.0 1.0 collective-permute-start.30
  147.0 10.7 %finish.3 = (bf16[192,1024]{1,0:T(8,128)(2,1)}, bf16[192,1024]{1,0:T(8,128)(2,1)}, bf16[192,1024]{1,0:T(8,128)(2,1)}, bf16[128,3712]{1,0:T(8,128)(2,1)}, bf16[128,3712]{1,0:T(8,128)(2,1)}) custom-call(f32[3,192,1024]{2,1,0:T(8,128)} %get-tuple-element.265.refs_0_, bf16[3,192,1024]{2,1,0:T(8,128)(2,1)} %copy-done.2, ...), custom_call_target="tpu_custom_call" | custom-call | tf_op jit(solution)/shard_map/finish/pallas_call | solution.py:294
  158.0 1.5 collective-permute-start.29
  159.7 0.9 collective-permute-start.32
  160.7 2.3 %collective-permute-start.31 = (bf16[32,3712]{1,0:T(8,128)(2,1)S(1)}, bf16[32,3712]{1,0:T(8,128)(2,1)S(1)}, u32[]{:S(2)}, u32[]{:S(2)}) collective-permute-start(bf16[32,3712]{1,0:T(8,128)(2,1)S(1)} %get-tuple-element.337), channel_id=1, source_target_pairs={{0,8},{1,9},{2,10},{3,11},{4,12},{5,13},{6,14},{7,15},{8,0},{9,1},... | collective-permute-start | bytes 712712 | tf_op jit(solution)/shard_map/ppermute | solution.py:105
  163.4 1.1 collective-permute-start.34
  165.2 4.9 %fusion = bf16[1,1024,1792]{2,1,0:T(8,128)(2,1)} fusion(bf16[192,1792]{1,0:T(8,128)(2,1)S(1)} %copy-done.38, bf16[192,1792]{1,0:T(8,128)(2,1)S(1)} %copy-done.37, bf16[192,1792]{1,0:T(8,128)(2,1)S(1)} %copy-done.36, bf16[192,1792]{1,0:T(8,128)(2,1)S(1)} %copy-done.35, bf16[192,1024]{1,0:T(8,128)(2,1)S(1)} %copy-done.51, ...), kind=kOutput, calls=%fused_computation.3 | convolution fusion | flops 2837708800 | bytes 7995392 | tf_op jit(solution)/shard_map/dot_general | solution.py:27
  170.1 5.6 %collective-permute-done.34 = bf16[64,3712]{1,0:T(8,128)(2,1)S(1)} collective-permute-done((bf16[64,3712]{1,0:T(8,128)(2,1)S(1)}, bf16[64,3712]{1,0:T(8,128)(2,1)S(1)}, u32[]{:S(2)}, u32[]{:S(2)}) %collective-permute-start.34) | collective-permute-done | bytes 475168 | tf_op jit(solution)/shard_map/ppermute | solution.py:93
  175.8 1.3 collective-permute-start.36
  177.1 1.0 collective-permute-start.35
  178.5 4.5 %fusion.1 = bf16[1,1792,1024]{2,1,0:T(8,128)(2,1)} fusion(bf16[768,1792]{1,0:T(8,128)(2,1)S(1)} %constant_dynamic-update-slice_fusion, bf16[192,1024]{1,0:T(8,128)(2,1)S(1)} %copy-done.50, bf16[192,1024]{1,0:T(8,128)(2,1)S(1)} %copy-done.47, bf16[192,1024]{1,0:T(8,128)(2,1)S(1)} %copy-done.44, bf16[192,1024]{1,0:T(8,128)(2,1)S(1)} %copy-done.41), kind=kOutput, calls=%fused_computation.4 | convolution fusion | flops 2826698752 | bytes 7995392 | tf_op jit(solution)/shard_map/dot_general | solution.py:27
  183.0 4.5 %fusion.2 = bf16[1,1792,1024]{2,1,0:T(8,128)(2,1)} fusion(bf16[768,1792]{1,0:T(8,128)(2,1)S(1)} %constant_dynamic-update-slice_fusion, bf16[192,1024]{1,0:T(8,128)(2,1)S(1)} %copy-done.49, bf16[192,1024]{1,0:T(8,128)(2,1)S(1)} %copy-done.46, bf16[192,1024]{1,0:T(8,128)(2,1)S(1)} %copy-done.43, bf16[192,1024]{1,0:T(8,128)(2,1)S(1)} %copy-done.40), kind=kOutput, calls=%fused_computation.5 | convolution fusion | flops 2826698752 | bytes 7995392 | tf_op jit(solution)/shard_map/dot_general | solution.py:27
  187.6 6.2 %collective-permute-done.31 = bf16[32,3712]{1,0:T(8,128)(2,1)S(1)} collective-permute-done((bf16[32,3712]{1,0:T(8,128)(2,1)S(1)}, bf16[32,3712]{1,0:T(8,128)(2,1)S(1)}, u32[]{:S(2)}, u32[]{:S(2)}) %collective-permute-start.31) | collective-permute-done | bytes 237600 | tf_op jit(solution)/shard_map/ppermute | solution.py:105
  (183 shorter events, 15.4 us)
Async XLA Ops:
  2.9 8.8 %collective-permute-start = (bf16[32,3712]{1,0:T(8,128)(2,1)S(1)}, bf16[32,3712]{1,0:T(8,128)(2,1)S(1)}, u32[]{:S(2)}, u32[]{:S(2)}) collective-permute-start(bf16[32,3712]{1,0:T(8,128)(2,1)S(1)} %broadcast_select_fusion.4), channel_id=1, source_target_pairs={{0,16},{16,0},{1,17},{17,1},{2,18},{18,2},{3,19},{19,3},{4,20},{20... | collective-permute-start | bytes 712712 | tf_op jit(solution)/shard_map/ppermute | solution.py:32
  11.8 17.5 %copy-start = (bf16[64,3712]{1,0:T(8,128)(2,1)}, bf16[64,3712]{1,0:T(8,128)(2,1)S(1)}, u32[]{:S(2)}) copy-start(bf16[64,3712]{1,0:T(8,128)(2,1)S(1)} %pad_maximum_fusion.refs_3_) | copy-start | bytes 1425412
  11.8 13.9 %collective-permute-start.3 = (bf16[64,3712]{1,0:T(8,128)(2,1)S(1)}, bf16[64,3712]{1,0:T(8,128)(2,1)S(1)}, u32[]{:S(2)}, u32[]{:S(2)}) collective-permute-start(bf16[64,3712]{1,0:T(8,128)(2,1)S(1)} %pad_maximum_fusion.refs_3_), channel_id=1, source_target_pairs={{0,4},{1,5},{2,6},{3,7},{4,8},{5,9},{6,10},{7,11},{8,12},{9,13},{1... | collective-permute-start | bytes 1425416 | tf_op jit(solution)/shard_map/ppermute | solution.py:93
  13.7 12.0 %collective-permute-start.2 = (bf16[64,3712]{1,0:T(8,128)(2,1)S(1)}, bf16[64,3712]{1,0:T(8,128)(2,1)S(1)}, u32[]{:S(2)}, u32[]{:S(2)}) collective-permute-start(bf16[64,3712]{1,0:T(8,128)(2,1)S(1)} %pad_maximum_fusion.refs_3_), channel_id=1, source_target_pairs={{0,2},{1,3},{2,0},{3,1},{4,6},{5,7},{6,4},{7,5},{8,10},{9,11},{10,... | collective-permute-start | bytes 1425416 | tf_op jit(solution)/shard_map/ppermute | solution.py:93
  15.2 14.1 %collective-permute-start.1 = (bf16[64,3712]{1,0:T(8,128)(2,1)S(1)}, bf16[64,3712]{1,0:T(8,128)(2,1)S(1)}, u32[]{:S(2)}, u32[]{:S(2)}) collective-permute-start(bf16[64,3712]{1,0:T(8,128)(2,1)S(1)} %pad_maximum_fusion.refs_3_), channel_id=1, source_target_pairs={{0,1},{1,0},{2,3},{3,2},{4,5},{5,4},{6,7},{7,6},{8,9},{9,8},{10,11... | collective-permute-start | bytes 1425416 | tf_op jit(solution)/shard_map/ppermute | solution.py:93
  25.7 14.2 %copy-start.16 = (bf16[64,3712]{1,0:T(8,128)(2,1)}, bf16[64,3712]{1,0:T(8,128)(2,1)S(1)}, u32[]{:S(2)}) copy-start(bf16[64,3712]{1,0:T(8,128)(2,1)S(1)} %collective-permute-done.3.refs_3_) | copy-start | bytes 1425412
  25.7 3.5 %collective-permute-start.4 = (bf16[64,3712]{1,0:T(8,128)(2,1)S(1)}, bf16[64,3712]{1,0:T(8,128)(2,1)S(1)}, u32[]{:S(2)}, u32[]{:S(2)}) collective-permute-start(bf16[64,3712]{1,0:T(8,128)(2,1)S(1)} %collective-permute-done.2.refs_4_), channel_id=1, source_target_pairs={{0,1},{1,0},{2,3},{3,2},{4,5},{5,4},{6,7},{7,6},{8,9},{9,8},{10,11... | collective-permute-start | bytes 1425416 | tf_op jit(solution)/shard_map/ppermute | solution.py:93
  25.8 14.1 %collective-permute-start.6 = (bf16[64,3712]{1,0:T(8,128)(2,1)S(1)}, bf16[64,3712]{1,0:T(8,128)(2,1)S(1)}, u32[]{:S(2)}, u32[]{:S(2)}) collective-permute-start(bf16[64,3712]{1,0:T(8,128)(2,1)S(1)} %collective-permute-done.3.refs_3_), channel_id=1, source_target_pairs={{0,2},{1,3},{2,0},{3,1},{4,6},{5,7},{6,4},{7,5},{8,10},{9,11},{10,... | collective-permute-start | bytes 1425416 | tf_op jit(solution)/shard_map/ppermute | solution.py:93
  27.4 24.0 %collective-permute-start.9 = (bf16[64,3712]{1,0:T(8,128)(2,1)S(1)}, bf16[64,3712]{1,0:T(8,128)(2,1)S(1)}, u32[]{:S(2)}, u32[]{:S(2)}) collective-permute-start(bf16[64,3712]{1,0:T(8,128)(2,1)S(1)} %pad_maximum_fusion.refs_3_), channel_id=1, source_target_pairs={{0,8},{1,9},{2,10},{3,11},{4,12},{5,13},{6,14},{7,15},{8,0},{9,1},... | collective-permute-start | bytes 1425416 | tf_op jit(solution)/shard_map/ppermute | solution.py:93
  39.9 13.9 %copy-start.18 = (bf16[64,3712]{1,0:T(8,128)(2,1)}, bf16[64,3712]{1,0:T(8,128)(2,1)S(1)}, u32[]{:S(2)}) copy-start(bf16[64,3712]{1,0:T(8,128)(2,1)S(1)} %collective-permute-done.6.refs_4_) | copy-start | bytes 1425412
  39.9 11.5 %collective-permute-start.7 = (bf16[64,3712]{1,0:T(8,128)(2,1)S(1)}, bf16[64,3712]{1,0:T(8,128)(2,1)S(1)}, u32[]{:S(2)}, u32[]{:S(2)}) collective-permute-start(bf16[64,3712]{1,0:T(8,128)(2,1)S(1)} %collective-permute-done.3.refs_3_), channel_id=1, source_target_pairs={{0,1},{1,0},{2,3},{3,2},{4,5},{5,4},{6,7},{7,6},{8,9},{9,8},{10,11... | collective-permute-start | bytes 1425416 | tf_op jit(solution)/shard_map/ppermute | solution.py:93
  40.0 11.4 %collective-permute-start.8 = (bf16[64,3712]{1,0:T(8,128)(2,1)S(1)}, bf16[64,3712]{1,0:T(8,128)(2,1)S(1)}, u32[]{:S(2)}, u32[]{:S(2)}) collective-permute-start(bf16[64,3712]{1,0:T(8,128)(2,1)S(1)} %collective-permute-done.6.refs_4_), channel_id=1, source_target_pairs={{0,1},{1,0},{2,3},{3,2},{4,5},{5,4},{6,7},{7,6},{8,9},{9,8},{10,11... | collective-permute-start | bytes 1425416 | tf_op jit(solution)/shard_map/ppermute | solution.py:93
  40.5 29.0 %collective-permute-start.5 = (bf16[3,192,1024]{2,1,0:T(8,128)(2,1)}, bf16[3,192,1024]{2,1,0:T(8,128)(2,1)S(1)}, u32[]{:S(2)}, u32[]{:S(2)}) collective-permute-start(bf16[3,192,1024]{2,1,0:T(8,128)(2,1)} %get-tuple-element.181), channel_id=1, source_target_pairs={{0,16},{16,0},{1,17},{17,1},{2,18},{18,2},{3,19},{19,3},{4,20},{20... | collective-permute-start | bytes 3538952 | tf_op jit(solution)/shard_map/ppermute | solution.py:32
  51.4 12.5 %copy-start.14 = (bf16[64,3712]{1,0:T(8,128)(2,1)}, bf16[64,3712]{1,0:T(8,128)(2,1)S(1)}, u32[]{:S(2)}) copy-start(bf16[64,3712]{1,0:T(8,128)(2,1)S(1)} %collective-permute-done.9.refs_3_) | copy-start | bytes 1425412
  51.4 12.5 %collective-permute-start.10 = (bf16[64,3712]{1,0:T(8,128)(2,1)S(1)}, bf16[64,3712]{1,0:T(8,128)(2,1)S(1)}, u32[]{:S(2)}, u32[]{:S(2)}) collective-permute-start(bf16[64,3712]{1,0:T(8,128)(2,1)S(1)} %collective-permute-done.9.refs_3_), channel_id=1, source_target_pairs={{0,2},{1,3},{2,0},{3,1},{4,6},{5,7},{6,4},{7,5},{8,10},{9,11},{10,... | collective-permute-start | bytes 1425416 | tf_op jit(solution)/shard_map/ppermute | solution.py:93
  52.0 14.6 %collective-permute-start.15 = (bf16[64,3712]{1,0:T(8,128)(2,1)}, bf16[64,3712]{1,0:T(8,128)(2,1)S(1)}, u32[]{:S(2)}, u32[]{:S(2)}) collective-permute-start(bf16[64,3712]{1,0:T(8,128)(2,1)} %copy-done), channel_id=1, source_target_pairs={{0,12},{1,13},{2,14},{3,15},{4,0},{5,1},{6,2},{7,3},{8,4},{9,5},{1... | collective-permute-start | bytes 1425416 | tf_op jit(solution)/shard_map/ppermute | solution.py:93
  63.9 5.6 %collective-permute-start.11 = (bf16[64,3712]{1,0:T(8,128)(2,1)S(1)}, bf16[64,3712]{1,0:T(8,128)(2,1)S(1)}, u32[]{:S(2)}, u32[]{:S(2)}) collective-permute-start(bf16[64,3712]{1,0:T(8,128)(2,1)S(1)} %collective-permute-done.9.refs_3_), channel_id=1, source_target_pairs={{0,1},{1,0},{2,3},{3,2},{4,5},{5,4},{6,7},{7,6},{8,9},{9,8},{10,11... | collective-permute-start | bytes 1425416 | tf_op jit(solution)/shard_map/ppermute | solution.py:93
  63.9 5.6 %collective-permute-start.12 = (bf16[64,3712]{1,0:T(8,128)(2,1)S(1)}, bf16[64,3712]{1,0:T(8,128)(2,1)S(1)}, u32[]{:S(2)}, u32[]{:S(2)}) collective-permute-start(bf16[64,3712]{1,0:T(8,128)(2,1)S(1)} %collective-permute-done.10.refs_4_), channel_id=1, source_target_pairs={{0,1},{1,0},{2,3},{3,2},{4,5},{5,4},{6,7},{7,6},{8,9},{9,8},{10,11... | collective-permute-start | bytes 1425416 | tf_op jit(solution)/shard_map/ppermute | solution.py:93
  64.4 30.3 %collective-permute-start.19 = (bf16[3,192,1024]{2,1,0:T(8,128)(2,1)}, bf16[3,192,1024]{2,1,0:T(8,128)(2,1)S(1)}, u32[]{:S(2)}, u32[]{:S(2)}) collective-permute-start(bf16[3,192,1024]{2,1,0:T(8,128)(2,1)} %get-tuple-element.192), channel_id=1, source_target_pairs={{0,16},{16,0},{1,17},{17,1},{2,18},{18,2},{3,19},{19,3},{4,20},{20... | collective-permute-start | bytes 3538952 | tf_op jit(solution)/shard_map/ppermute | solution.py:32
  66.6 21.1 %copy-start.13 = (bf16[64,3712]{1,0:T(8,128)(2,1)}, bf16[64,3712]{1,0:T(8,128)(2,1)S(1)}, u32[]{:S(2)}) copy-start(bf16[64,3712]{1,0:T(8,128)(2,1)S(1)} %collective-permute-done.15.refs_3_) | copy-start | bytes 1425412
  66.6 21.1 %collective-permute-start.16 = (bf16[64,3712]{1,0:T(8,128)(2,1)S(1)}, bf16[64,3712]{1,0:T(8,128)(2,1)S(1)}, u32[]{:S(2)}, u32[]{:S(2)}) collective-permute-start(bf16[64,3712]{1,0:T(8,128)(2,1)S(1)} %collective-permute-done.15.refs_3_), channel_id=1, source_target_pairs={{0,2},{1,3},{2,0},{3,1},{4,6},{5,7},{6,4},{7,5},{8,10},{9,11},{10,... | collective-permute-start | bytes 1425416 | tf_op jit(solution)/shard_map/ppermute | solution.py:93
  85.9 2.2 %collective-permute-start.13 = (bf16[64,3712]{1,0:T(8,128)(2,1)}, bf16[64,3712]{1,0:T(8,128)(2,1)S(1)}, u32[]{:S(2)}, u32[]{:S(2)}) collective-permute-start(bf16[64,3712]{1,0:T(8,128)(2,1)} %get-tuple-element.205), channel_id=1, source_target_pairs={{0,1},{1,0},{2,3},{3,2},{4,5},{5,4},{6,7},{7,6},{8,9},{9,8},{10,11... | collective-permute-start | bytes 1425416 | tf_op jit(solution)/shard_map/ppermute | solution.py:93
  86.0 34.1 %collective-permute-start.18 = (bf16[3,192,1024]{2,1,0:T(8,128)(2,1)}, bf16[3,192,1024]{2,1,0:T(8,128)(2,1)S(1)}, u32[]{:S(2)}, u32[]{:S(2)}) collective-permute-start(bf16[3,192,1024]{2,1,0:T(8,128)(2,1)} %get-tuple-element.210), channel_id=1, source_target_pairs={{0,16},{16,0},{1,17},{17,1},{2,18},{18,2},{3,19},{19,3},{4,20},{20... | collective-permute-start | bytes 3538952 | tf_op jit(solution)/shard_map/ppermute | solution.py:32
  87.5 2.1 %collective-permute-start.14 = (bf16[64,3712]{1,0:T(8,128)(2,1)}, bf16[64,3712]{1,0:T(8,128)(2,1)S(1)}, u32[]{:S(2)}, u32[]{:S(2)}) collective-permute-start(bf16[64,3712]{1,0:T(8,128)(2,1)} %get-tuple-element.207), channel_id=1, source_target_pairs={{0,1},{1,0},{2,3},{3,2},{4,5},{5,4},{6,7},{7,6},{8,9},{9,8},{10,11... | collective-permute-start | bytes 1425416 | tf_op jit(solution)/shard_map/ppermute | solution.py:93
  87.7 7.1 %collective-permute-start.20 = (bf16[64,3712]{1,0:T(8,128)(2,1)S(1)}, bf16[64,3712]{1,0:T(8,128)(2,1)S(1)}, u32[]{:S(2)}, u32[]{:S(2)}) collective-permute-start(bf16[64,3712]{1,0:T(8,128)(2,1)S(1)} %collective-permute-done.15.refs_3_), channel_id=1, source_target_pairs={{0,1},{1,0},{2,3},{3,2},{4,5},{5,4},{6,7},{7,6},{8,9},{9,8},{10,11... | collective-permute-start | bytes 1425416 | tf_op jit(solution)/shard_map/ppermute | solution.py:93
  88.1 6.6 %collective-permute-start.21 = (bf16[64,3712]{1,0:T(8,128)(2,1)S(1)}, bf16[64,3712]{1,0:T(8,128)(2,1)S(1)}, u32[]{:S(2)}, u32[]{:S(2)}) collective-permute-start(bf16[64,3712]{1,0:T(8,128)(2,1)S(1)} %collective-permute-done.16.refs_4_), channel_id=1, source_target_pairs={{0,1},{1,0},{2,3},{3,2},{4,5},{5,4},{6,7},{7,6},{8,9},{9,8},{10,11... | collective-permute-start | bytes 1425416 | tf_op jit(solution)/shard_map/ppermute | solution.py:93
  96.1 15.6 %copy-start.39 = (bf16[64,3712]{1,0:T(8,128)(2,1)S(1)}, bf16[64,3712]{1,0:T(8,128)(2,1)}, u32[]{:S(2)}) copy-start(bf16[64,3712]{1,0:T(8,128)(2,1)} %get-tuple-element.219) | copy-start | bytes 1425412
  111.1 2.6 %collective-permute-start.22 = (bf16[64,3712]{1,0:T(8,128)(2,1)}, bf16[64,3712]{1,0:T(8,128)(2,1)S(1)}, u32[]{:S(2)}, u32[]{:S(2)}) collective-permute-start(bf16[64,3712]{1,0:T(8,128)(2,1)} %get-tuple-element.232), channel_id=1, source_target_pairs={{0,1},{1,0},{2,3},{3,2},{4,5},{5,4},{6,7},{7,6},{8,9},{9,8},{10,11... | collective-permute-start | bytes 1425416 | tf_op jit(solution)/shard_map/ppermute | solution.py:93
  111.2 2.7 %collective-permute-start.23 = (bf16[64,3712]{1,0:T(8,128)(2,1)}, bf16[64,3712]{1,0:T(8,128)(2,1)S(1)}, u32[]{:S(2)}, u32[]{:S(2)}) collective-permute-start(bf16[64,3712]{1,0:T(8,128)(2,1)} %get-tuple-element.234), channel_id=1, source_target_pairs={{0,1},{1,0},{2,3},{3,2},{4,5},{5,4},{6,7},{7,6},{8,9},{9,8},{10,11... | collective-permute-start | bytes 1425416 | tf_op jit(solution)/shard_map/ppermute | solution.py:93
  111.7 20.7 %collective-permute-start.17 = (bf16[64,3712]{1,0:T(8,128)(2,1)S(1)}, bf16[64,3712]{1,0:T(8,128)(2,1)S(1)}, u32[]{:S(2)}, u32[]{:S(2)}) collective-permute-start(bf16[64,3712]{1,0:T(8,128)(2,1)S(1)} %copy-done.39), channel_id=1, source_target_pairs={{0,2},{1,3},{2,0},{3,1},{4,6},{5,7},{6,4},{7,5},{8,10},{9,11},{10,... | collective-permute-start | bytes 1425416 | tf_op jit(solution)/shard_map/ppermute | solution.py:93
  112.3 32.2 %collective-permute-start.25 = (bf16[3,192,1024]{2,1,0:T(8,128)(2,1)}, bf16[3,192,1024]{2,1,0:T(8,128)(2,1)S(1)}, u32[]{:S(2)}, u32[]{:S(2)}) collective-permute-start(bf16[3,192,1024]{2,1,0:T(8,128)(2,1)} %get-tuple-element.235), channel_id=1, source_target_pairs={{0,16},{16,0},{1,17},{17,1},{2,18},{18,2},{3,19},{19,3},{4,20},{20... | collective-permute-start | bytes 3538952 | tf_op jit(solution)/shard_map/ppermute | solution.py:32
  117.4 27.1 %collective-permute-start.24 = (bf16[64,3712]{1,0:T(8,128)(2,1)}, bf16[64,3712]{1,0:T(8,128)(2,1)S(1)}, u32[]{:S(2)}, u32[]{:S(2)}) collective-permute-start(bf16[64,3712]{1,0:T(8,128)(2,1)} %get-tuple-element.253), channel_id=1, source_target_pairs={{0,2},{1,3},{2,0},{3,1},{4,6},{5,7},{6,4},{7,5},{8,10},{9,11},{10,... | collective-permute-start | bytes 1425416 | tf_op jit(solution)/shard_map/ppermute | solution.py:93
  121.1 11.4 %copy-start.5 = (f32[64,3712]{1,0:T(8,128)S(1)}, f32[64,3712]{1,0:T(8,128)}, u32[]{:S(2)}) copy-start(f32[64,3712]{1,0:T(8,128)} %get-tuple-element.251) | copy-start | bytes 2850820
  131.8 12.6 %copy-start.6 = (f32[64,3712]{1,0:T(8,128)S(1)}, f32[64,3712]{1,0:T(8,128)}, u32[]{:S(2)}) copy-start(f32[64,3712]{1,0:T(8,128)} %get-tuple-element.262) | copy-start | bytes 2850820
  131.8 2.1 %collective-permute-start.26 = (bf16[64,3712]{1,0:T(8,128)(2,1)}, bf16[64,3712]{1,0:T(8,128)(2,1)S(1)}, u32[]{:S(2)}, u32[]{:S(2)}) collective-permute-start(bf16[64,3712]{1,0:T(8,128)(2,1)} %get-tuple-element.249), channel_id=1, source_target_pairs={{0,1},{1,0},{2,3},{3,2},{4,5},{5,4},{6,7},{7,6},{8,9},{9,8},{10,11... | collective-permute-start | bytes 1425416 | tf_op jit(solution)/shard_map/ppermute | solution.py:93
  131.9 2.7 %collective-permute-start.27 = (bf16[64,3712]{1,0:T(8,128)(2,1)}, bf16[64,3712]{1,0:T(8,128)(2,1)S(1)}, u32[]{:S(2)}, u32[]{:S(2)}) collective-permute-start(bf16[64,3712]{1,0:T(8,128)(2,1)} %get-tuple-element.250), channel_id=1, source_target_pairs={{0,1},{1,0},{2,3},{3,2},{4,5},{5,4},{6,7},{7,6},{8,9},{9,8},{10,11... | collective-permute-start | bytes 1425416 | tf_op jit(solution)/shard_map/ppermute | solution.py:93
  144.6 13.2 %collective-permute-start.28 = (bf16[64,3712]{1,0:T(8,128)(2,1)S(1)}, bf16[64,3712]{1,0:T(8,128)(2,1)S(1)}, u32[]{:S(2)}, u32[]{:S(2)}) collective-permute-start(bf16[64,3712]{1,0:T(8,128)(2,1)S(1)} %add_convert_fusion.2), channel_id=1, source_target_pairs={{0,12},{1,13},{2,14},{3,15},{4,0},{5,1},{6,2},{7,3},{8,4},{9,5},{1... | collective-permute-start | bytes 1425416 | tf_op jit(solution)/shard_map/ppermute | solution.py:93
  146.0 12.1 %collective-permute-start.30 = (bf16[64,3712]{1,0:T(8,128)(2,1)}, bf16[64,3712]{1,0:T(8,128)(2,1)S(1)}, u32[]{:S(2)}, u32[]{:S(2)}) collective-permute-start(bf16[64,3712]{1,0:T(8,128)(2,1)} %get-tuple-element.275), channel_id=1, source_target_pairs={{0,2},{1,3},{2,0},{3,1},{4,6},{5,7},{6,4},{7,5},{8,10},{9,11},{10,... | collective-permute-start | bytes 1425416 | tf_op jit(solution)/shard_map/ppermute | solution.py:93
  157.7 5.4 %collective-permute-start.33 = (bf16[128,3712]{1,0:T(8,128)(2,1)}, bf16[128,3712]{1,0:T(8,128)(2,1)S(1)}, u32[]{:S(2)}, u32[]{:S(2)}) collective-permute-start(bf16[128,3712]{1,0:T(8,128)(2,1)} %get-tuple-element.271), channel_id=1, source_target_pairs={{0,1},{1,0},{2,3},{3,2},{4,5},{5,4},{6,7},{7,6},{8,9},{9,8},{10,11... | collective-permute-start | bytes 2850824 | tf_op jit(solution)/shard_map/ppermute | solution.py:93
  158.0 29.5 %collective-permute-start.29 = (bf16[32,3712]{1,0:T(8,128)(2,1)S(1)}, bf16[32,3712]{1,0:T(8,128)(2,1)S(1)}, u32[]{:S(2)}, u32[]{:S(2)}) collective-permute-start(bf16[32,3712]{1,0:T(8,128)(2,1)S(1)} %select_convert_fusion), channel_id=1, source_target_pairs={{0,16},{16,0},{1,17},{17,1},{2,18},{18,2},{3,19},{19,3},{4,20},{20... | collective-permute-start | bytes 712712 | tf_op jit(solution)/shard_map/ppermute | solution.py:32
  159.7 27.8 %collective-permute-start.32 = (bf16[32,3712]{1,0:T(8,128)(2,1)S(1)}, bf16[32,3712]{1,0:T(8,128)(2,1)S(1)}, u32[]{:S(2)}, u32[]{:S(2)}) collective-permute-start(bf16[32,3712]{1,0:T(8,128)(2,1)S(1)} %get-tuple-element.336), channel_id=1, source_target_pairs={{0,24},{1,25},{2,26},{3,27},{4,28},{5,29},{6,30},{7,31},{8,16},{9,... | collective-permute-start | bytes 712712 | tf_op jit(solution)/shard_map/ppermute | solution.py:105
  160.7 33.1 %collective-permute-start.31 = (bf16[32,3712]{1,0:T(8,128)(2,1)S(1)}, bf16[32,3712]{1,0:T(8,128)(2,1)S(1)}, u32[]{:S(2)}, u32[]{:S(2)}) collective-permute-start(bf16[32,3712]{1,0:T(8,128)(2,1)S(1)} %get-tuple-element.337), channel_id=1, source_target_pairs={{0,8},{1,9},{2,10},{3,11},{4,12},{5,13},{6,14},{7,15},{8,0},{9,1},... | collective-permute-start | bytes 712712 | tf_op jit(solution)/shard_map/ppermute | solution.py:105
  163.4 12.3 %collective-permute-start.34 = (bf16[64,3712]{1,0:T(8,128)(2,1)S(1)}, bf16[64,3712]{1,0:T(8,128)(2,1)S(1)}, u32[]{:S(2)}, u32[]{:S(2)}) collective-permute-start(bf16[64,3712]{1,0:T(8,128)(2,1)S(1)} %slice.126), channel_id=1, source_target_pairs={{0,2},{1,3},{2,0},{3,1},{4,6},{5,7},{6,4},{7,5},{8,10},{9,11},{10,... | collective-permute-start | bytes 1425416 | tf_op jit(solution)/shard_map/ppermute | solution.py:93
  170.1 8.0 %copy-start.9 = (bf16[192,1792]{1,0:T(8,128)(2,1)S(1)}, bf16[192,1792]{1,0:T(8,128)(2,1)}, u32[]{:S(2)}) copy-start(bf16[192,1792]{1,0:T(8,128)(2,1)} %get-tuple-element.307) | copy-start | bytes 2064388
  170.1 8.0 %copy-start.10 = (bf16[192,1792]{1,0:T(8,128)(2,1)S(1)}, bf16[192,1792]{1,0:T(8,128)(2,1)}, u32[]{:S(2)}) copy-start(bf16[192,1792]{1,0:T(8,128)(2,1)} %get-tuple-element.308) | copy-start | bytes 2064388
  170.1 8.1 %copy-start.11 = (bf16[192,1792]{1,0:T(8,128)(2,1)S(1)}, bf16[192,1792]{1,0:T(8,128)(2,1)}, u32[]{:S(2)}) copy-start(bf16[192,1792]{1,0:T(8,128)(2,1)} %get-tuple-element.309) | copy-start | bytes 2064388
  175.8 17.9 %collective-permute-start.36 = (bf16[32,3712]{1,0:T(8,128)(2,1)S(1)}, bf16[32,3712]{1,0:T(8,128)(2,1)S(1)}, u32[]{:S(2)}, u32[]{:S(2)}) collective-permute-start(bf16[32,3712]{1,0:T(8,128)(2,1)S(1)} %get-tuple-element.334), channel_id=1, source_target_pairs={{0,20},{1,21},{2,22},{3,23},{4,24},{5,25},{6,26},{7,27},{8,28},{9,... | collective-permute-start | bytes 712712 | tf_op jit(solution)/shard_map/ppermute | solution.py:105
  177.1 16.6 %collective-permute-start.35 = (bf16[32,3712]{1,0:T(8,128)(2,1)S(1)}, bf16[32,3712]{1,0:T(8,128)(2,1)S(1)}, u32[]{:S(2)}, u32[]{:S(2)}) collective-permute-start(bf16[32,3712]{1,0:T(8,128)(2,1)S(1)} %get-tuple-element.335), channel_id=1, source_target_pairs={{0,4},{1,5},{2,6},{3,7},{4,8},{5,9},{6,10},{7,11},{8,12},{9,13},{1... | collective-permute-start | bytes 712712 | tf_op jit(solution)/shard_map/ppermute | solution.py:105
  (41 other events, 92.1 us)
